TPU v7x, 256 devices: a whole 4x4x8 slice. The times are simulated.
256 devices in a mesh: pair: 8 (over x, core), tile: 32 (over z, y).
Axes of the slice: x: 4, y: 4, z: 8, core: 2. Of those that a mesh axis runs over, the one named last changes fastest.
Arguments:
- amplitudes: bfloat16 [4096, 32, 256], P('pair', 'tile'), may hold values from -6 to 6
- size_cd: int32 [32], P('tile'), may hold values from 64 to 256, as said below
- integrals: bfloat16 [1024, 256, 256], P('tile'), may hold values from -0.125 to 0.125
- block_rows: int32 [1024], P('tile'), may hold values from 0 to 63, as said below
- block_cols: int32 [1024], P('tile'), may hold values from 0 to 31
- size_ab: int32 [64], P('tile'), may hold values from 64 to 256, as said below
- mirror: int32 [4096], replicated, may hold values from 0 to 4095, as said below
Outputs:
- symmetrized: bfloat16 [4096, 64, 256], P('pair', 'tile')
Inputs may be any that keep to these rules, and one draw needn't show every extreme that they name: `block_rows`: each block's row tile and column tile carry the same irreducible representation. Of the 32 blocks of one device of tile (aligned runs), at most 2 name row tiles d * 2 to (d + 1) * 2 - 1 of any one owner d, and exactly 2 for some owner. mirror[mirror[k]] = k and mirror[k] != k. `size_cd`: tile 0 is full. `size_ab`: tile 0 is full.
All inputs are finite; a program needn't handle non-finite values.
Results may differ from a plain program's by a relative error of at most 0.0059.
Values may be sent and summed in bfloat16 or wider, within the bound.
No kernel may reach another device: no remote copies, remote signals or barrier semaphores. Data moves between devices by JAX's collectives and lax.ppermute only.
A program may use at most 128 MiB of HBM per device.

v0:
```python
import math

import jax
import jax.numpy as jnp
from jax import lax
from jax.sharding import PartitionSpec as P


def local(amplitudes, size_cd, integrals, block_rows, block_cols, size_ab, mirror):
    pair_count, column_tiles, width_slots = amplitudes.shape
    tile_devices = lax.axis_size("tile")
    block_count = integrals.shape[0]
    tile_count = size_ab.shape[0]
    capacity = max(2, 2 * block_count // tile_devices)
    position = lax.broadcasted_iota(jnp.int32, (1, column_tiles, width_slots), 2)
    masked = jnp.where(position < size_cd[None, :, None], amplitudes, jnp.zeros_like(amplitudes))
    gathered = lax.all_gather(masked, "tile", axis=1, tiled=True)
    owner = block_rows // tile_count
    local_row = block_rows % tile_count
    one_hot = (owner[:, None] == jnp.arange(tile_devices, dtype=jnp.int32)[None, :]).astype(
        jnp.int32
    )
    before = jnp.cumsum(one_hot, axis=0) - one_hot
    rank_owner = jnp.sum(before * one_hot, axis=1)
    target = owner * capacity + rank_owner
    owned_tiles = jnp.arange(tile_count, dtype=jnp.int32)
    send_weight = jnp.zeros((tile_devices * capacity, width_slots, width_slots), jnp.bfloat16)
    send_weight = (
        send_weight.at[target]
        .set(integrals)
        .reshape(tile_devices, capacity, width_slots, width_slots)
    )
    tags = jnp.stack([local_row, block_cols], axis=1).astype(jnp.bfloat16)
    labels = jnp.zeros((tile_devices * capacity, 2), jnp.bfloat16).at[target].set(tags)
    labels = labels.reshape(tile_devices, capacity, 2)
    weights = lax.all_to_all(send_weight, "tile", split_axis=0, concat_axis=0, tiled=True)
    tag_piece = lax.all_to_all(labels, "tile", split_axis=0, concat_axis=0, tiled=True)
    senders = tag_piece.shape[0]
    items = tag_piece.shape[1]
    group = math.gcd(senders, 8)
    rounds = senders // group
    columns = tag_piece[:, :, 1].astype(jnp.int32).reshape(rounds, group, items)
    row_tags = tag_piece[:, :, 0].astype(jnp.int32)
    selector = (row_tags[:, :, None] == owned_tiles[None, None, :]).astype(jnp.bfloat16)
    selector = selector.reshape(rounds, group, items, tile_count)
    grouped = weights.reshape(rounds, group, items, width_slots, width_slots)

    def accumulate(total, parts):
        weight_group, column_group, select_group = parts
        chosen = jnp.take(gathered, column_group.reshape(-1), axis=1)
        chosen = chosen.reshape(pair_count, group, items, width_slots)
        terms = jnp.einsum(
            "pnks,nkts->nkpt", chosen, weight_group, preferred_element_type=jnp.float32
        )
        terms = terms.astype(jnp.bfloat16)
        added = jnp.einsum(
            "nkpt,nka->kpat", terms, select_group, preferred_element_type=jnp.float32
        )
        return (total + added, None)

    start_total = jnp.zeros((items, pair_count, tile_count, width_slots), jnp.float32)
    total, unused = lax.scan(accumulate, start_total, (grouped, columns, selector))
    result = jnp.sum(total, axis=0)
    live_mask = (
        lax.broadcasted_iota(jnp.int32, (1, tile_count, width_slots), 2) < size_ab[None, :, None]
    )
    ladder = jnp.where(live_mask, result, jnp.zeros_like(result)).astype(jnp.bfloat16)
    everyone = lax.all_gather(ladder, "pair", axis=0, tiled=True)
    first_pair = lax.axis_index("pair") * pair_count
    partner_ids = lax.dynamic_slice_in_dim(mirror, first_pair, pair_count)
    partner = jnp.take(everyone, partner_ids, axis=0)
    return (ladder.astype(jnp.float32) + partner.astype(jnp.float32)).astype(jnp.bfloat16)


def solution(mesh):
    in_specs = (
        P("pair", "tile", None),
        P("tile"),
        P("tile", None, None),
        P("tile"),
        P("tile"),
        P("tile"),
        P(),
    )
    out_specs = P("pair", "tile", None)
    return jax.shard_map(local, mesh=mesh, in_specs=in_specs, out_specs=out_specs, check_vma=False)
```

profile of v0, /device:TPU:1, one launch (start us, length us, event | category | flops | bytes accessed | tf_op | source)
XLA Modules:
  0.0 414.4 jit_solution(13700868940168465872)
XLA Ops:
  6.5 0.7 fusion.23
  7.3 0.2 select_reduce_fusion
  7.5 0.7 convert_bitcast_fusion
  8.2 0.1 copy.36
  8.3 0.7 scatter_custom_fusion
  9.0 0.9 copy.38
  9.9 12.0 %all-to-all-start = ((bf16[32,2,2]{1,2,0:T(2,128)(2,1)}), bf16[32,2,2]{1,2,0:T(2,128)(2,1)S(1)}, u32[]{:S(2)}, u32[]{:S(2)}) async-start(bf16[32,2,2]{1,2,0:T(2,128)(2,1)} %copy.38), calls=%async_computation | async-start | bytes 32768 | tf_op jit(solution)/shard_map/all_to_all | solution.py:37
  22.6 1.7 broadcast_select_fusion.1
  24.3 4.2 %broadcast_in_dim.69 = bf16[64,256,256]{2,1,0:T(8,128)(2,1)} broadcast(bf16[]{:T(256)} %constant.82.clone.1), dimensions={} | broadcast | bytes 8388610 | tf_op jit(solution)/shard_map/broadcast_in_dim | solution.py:27
  28.5 11.3 %scatter_fusion = bf16[64,256,256]{2,1,0:T(8,128)(2,1)} fusion(bf16[64,256,256]{2,1,0:T(8,128)(2,1)} %broadcast_in_dim.69, s32[32]{0:T(128)S(1)} %compare_select_fusion.3, bf16[32,256,256]{2,1,0:T(8,128)(2,1)} %param.11), kind=kCustom, calls=%fused_computation.3 | custom fusion | bytes 12583040 | tf_op jit(solution)/shard_map/scatter | solution.py:30
  39.8 9.5 %all-to-all-start.1 = ((bf16[32,2,256,256]{3,2,1,0:T(8,128)(2,1)}), bf16[32,2,256,256]{3,2,1,0:T(8,128)(2,1)}, u32[]{:S(2)}, u32[]{:S(2)}) async-start(bf16[32,2,256,256]{3,2,1,0:T(8,128)(2,1)} %bitcast.43), calls=%async_computation.1 | async-start | bytes 16777216 | tf_op jit(solution)/shard_map/all_to_all | solution.py:36
  49.4 0.7 all-gather.3.cloned.1.call-update
  50.1 0.2 all-gather.5.cloned.1.call-start
  50.4 0.1 copy.48
  50.5 0.1 copy.46
  50.6 0.1 copy.47
  50.7 0.1 reshape.98
  50.8 227.9 %all-to-all-done.1 = bf16[32,2,256,256]{3,2,1,0:T(8,128)(2,1)} async-done(((bf16[32,2,256,256]{3,2,1,0:T(8,128)(2,1)}), bf16[32,2,256,256]{3,2,1,0:T(8,128)(2,1)}, u32[]{:S(2)}, u32[]{:S(2)}) %all-to-all-start.1) | async-done | bytes 8388640 | tf_op jit(solution)/shard_map/all_to_all | solution.py:36
  278.7 80.1 %while.11 = (s32[]{:T(128)}, f32[2,512,2,256]{3,2,1,0:T(2,128)S(1)}, bf16[4,8,2,2]{1,3,2,0:T(2,128)(2,1)S(1)}, s32[4,8,2]{2,1,0:T(8,128)S(1)}, bf16[512,32,256]{...) while((s32[]{:T(128)}, f32[2,512,2,256]{3,2,1,0:T(2,128)S(1)}, ...), condition=%wide.region_5.6_spmd.clone, body=%wide.region_4.5_spmd.clone.sunk | while | flops 1087374464 | bytes 27269476 | solution.py:62
  278.7 0.1 reshape.148
  278.8 6.1 %gather_fusion = bf16[16,512,256]{2,1,0:T(8,128)(2,1)} fusion(bf16[512,32,256]{2,0,1:T(8,128)(2,1)} %get-tuple-element.158, s32[1024]{0:T(1024)S(1)} %pad_clamp_fusion.3), kind=kCustom, calls=%fused_computation.clone.clone.1 | custom fusion | bytes 8388672 | tf_op jit(solution)/shard_map/while/body/eval_jaxpr/jit(_take)/gather | solution.py:50
  285.0 0.1 copy.57
  285.1 0.1 copy.58
  285.2 6.1 %fusion.36 = bf16[8,2,512,256]{3,2,1,0:T(8,128)(2,1)} fusion(bf16[512,8,2,256]{3,0,2,1:T(8,128)(2,1)} %bitcast.42, pred[8,2]{1,0:T(8,128)(4,1)S(1)} %copy.58, bf16[4,8,2,256,256]{4,3,2,1,0:T(8,128)(2,1)} %get-tuple-element.159, s32[]{:T(128)} %get-tuple-element.146), kind=kOutput, calls=%fused_computation.9.clone.1 | convolution fusion | flops 1077936128 | bytes 10486288 | tf_op jit(solution)/shard_map/while/body/eval_jaxpr/pnks,nkts->nkpt/dot_general | solution.py:52
  291.3 7.4 %bitcast_add_fusion.2 = f32[2,512,2,256]{3,2,1,0:T(2,128)S(1)} fusion(f32[2,512,2,256]{3,2,1,0:T(2,128)S(1)} %get-tuple-element.147, pred[]{:T(512)S(6)} %compare.6, bf16[8,2,512,256]{3,2,1,0:T(8,128)(2,1)} %fusion.36, bf16[4,8,2,2]{1,3,2,0:T(2,128)(2,1)S(1)} %get-tuple-element.156, s32[]{:T(128)} %get-tuple-element.146), kind=kOutput, calls=%fused_computation.10.clone.1 | convolution fusion | flops 9437184 | bytes 8389637 | tf_op jit(solution)/shard_map/while/body/eval_jaxpr/nkpt,nka->kpat/dot_general | solution.py:56
  298.8 0.1 reshape.148
  298.9 6.1 %gather_fusion = bf16[16,512,256]{2,1,0:T(8,128)(2,1)} fusion(bf16[512,32,256]{2,0,1:T(8,128)(2,1)} %get-tuple-element.158, s32[1024]{0:T(1024)S(1)} %pad_clamp_fusion.3), kind=kCustom, calls=%fused_computation.clone.clone.1 | custom fusion | bytes 8388672 | tf_op jit(solution)/shard_map/while/body/eval_jaxpr/jit(_take)/gather | solution.py:50
  305.0 0.1 copy.57
  305.1 0.1 copy.58
  305.2 6.1 %fusion.36 = bf16[8,2,512,256]{3,2,1,0:T(8,128)(2,1)} fusion(bf16[512,8,2,256]{3,0,2,1:T(8,128)(2,1)} %bitcast.42, pred[8,2]{1,0:T(8,128)(4,1)S(1)} %copy.58, bf16[4,8,2,256,256]{4,3,2,1,0:T(8,128)(2,1)} %get-tuple-element.159, s32[]{:T(128)} %get-tuple-element.146), kind=kOutput, calls=%fused_computation.9.clone.1 | convolution fusion | flops 1077936128 | bytes 10486288 | tf_op jit(solution)/shard_map/while/body/eval_jaxpr/pnks,nkts->nkpt/dot_general | solution.py:52
  311.3 7.4 %bitcast_add_fusion.2 = f32[2,512,2,256]{3,2,1,0:T(2,128)S(1)} fusion(f32[2,512,2,256]{3,2,1,0:T(2,128)S(1)} %get-tuple-element.147, pred[]{:T(512)S(6)} %compare.6, bf16[8,2,512,256]{3,2,1,0:T(8,128)(2,1)} %fusion.36, bf16[4,8,2,2]{1,3,2,0:T(2,128)(2,1)S(1)} %get-tuple-element.156, s32[]{:T(128)} %get-tuple-element.146), kind=kOutput, calls=%fused_computation.10.clone.1 | convolution fusion | flops 9437184 | bytes 8389637 | tf_op jit(solution)/shard_map/while/body/eval_jaxpr/nkpt,nka->kpat/dot_general | solution.py:56
  318.9 6.1 %gather_fusion = bf16[16,512,256]{2,1,0:T(8,128)(2,1)} fusion(bf16[512,32,256]{2,0,1:T(8,128)(2,1)} %get-tuple-element.158, s32[1024]{0:T(1024)S(1)} %pad_clamp_fusion.3), kind=kCustom, calls=%fused_computation.clone.clone.1 | custom fusion | bytes 8388672 | tf_op jit(solution)/shard_map/while/body/eval_jaxpr/jit(_take)/gather | solution.py:50
  325.0 0.1 copy.57
  325.1 0.1 copy.58
  325.2 6.1 %fusion.36 = bf16[8,2,512,256]{3,2,1,0:T(8,128)(2,1)} fusion(bf16[512,8,2,256]{3,0,2,1:T(8,128)(2,1)} %bitcast.42, pred[8,2]{1,0:T(8,128)(4,1)S(1)} %copy.58, bf16[4,8,2,256,256]{4,3,2,1,0:T(8,128)(2,1)} %get-tuple-element.159, s32[]{:T(128)} %get-tuple-element.146), kind=kOutput, calls=%fused_computation.9.clone.1 | convolution fusion | flops 1077936128 | bytes 10486288 | tf_op jit(solution)/shard_map/while/body/eval_jaxpr/pnks,nkts->nkpt/dot_general | solution.py:52
  331.4 7.4 %bitcast_add_fusion.2 = f32[2,512,2,256]{3,2,1,0:T(2,128)S(1)} fusion(f32[2,512,2,256]{3,2,1,0:T(2,128)S(1)} %get-tuple-element.147, pred[]{:T(512)S(6)} %compare.6, bf16[8,2,512,256]{3,2,1,0:T(8,128)(2,1)} %fusion.36, bf16[4,8,2,2]{1,3,2,0:T(2,128)(2,1)S(1)} %get-tuple-element.156, s32[]{:T(128)} %get-tuple-element.146), kind=kOutput, calls=%fused_computation.10.clone.1 | convolution fusion | flops 9437184 | bytes 8389637 | tf_op jit(solution)/shard_map/while/body/eval_jaxpr/nkpt,nka->kpat/dot_general | solution.py:56
  338.8 0.1 reshape.148
  338.9 6.1 %gather_fusion = bf16[16,512,256]{2,1,0:T(8,128)(2,1)} fusion(bf16[512,32,256]{2,0,1:T(8,128)(2,1)} %get-tuple-element.158, s32[1024]{0:T(1024)S(1)} %pad_clamp_fusion.3), kind=kCustom, calls=%fused_computation.clone.clone.1 | custom fusion | bytes 8388672 | tf_op jit(solution)/shard_map/while/body/eval_jaxpr/jit(_take)/gather | solution.py:50
  345.1 0.1 copy.57
  345.2 0.1 copy.58
  345.3 6.1 %fusion.36 = bf16[8,2,512,256]{3,2,1,0:T(8,128)(2,1)} fusion(bf16[512,8,2,256]{3,0,2,1:T(8,128)(2,1)} %bitcast.42, pred[8,2]{1,0:T(8,128)(4,1)S(1)} %copy.58, bf16[4,8,2,256,256]{4,3,2,1,0:T(8,128)(2,1)} %get-tuple-element.159, s32[]{:T(128)} %get-tuple-element.146), kind=kOutput, calls=%fused_computation.9.clone.1 | convolution fusion | flops 1077936128 | bytes 10486288 | tf_op jit(solution)/shard_map/while/body/eval_jaxpr/pnks,nkts->nkpt/dot_general | solution.py:52
  351.4 7.4 %bitcast_add_fusion.2 = f32[2,512,2,256]{3,2,1,0:T(2,128)S(1)} fusion(f32[2,512,2,256]{3,2,1,0:T(2,128)S(1)} %get-tuple-element.147, pred[]{:T(512)S(6)} %compare.6, bf16[8,2,512,256]{3,2,1,0:T(8,128)(2,1)} %fusion.36, bf16[4,8,2,2]{1,3,2,0:T(2,128)(2,1)S(1)} %get-tuple-element.156, s32[]{:T(128)} %get-tuple-element.146), kind=kOutput, calls=%fused_computation.10.clone.1 | convolution fusion | flops 9437184 | bytes 8389637 | tf_op jit(solution)/shard_map/while/body/eval_jaxpr/nkpt,nka->kpat/dot_general | solution.py:56
  358.9 2.0 reduce_sum.19
  360.9 1.3 select_convert_fusion
  362.1 0.8 compare_and_fusion.1
  362.9 37.9 %all-gather.5.cloned.1.call-done = bf16[4096,2,256]{2,1,0:T(2,128)(2,1)} async-done(((bf16[512,2,256]{2,1,0:T(2,128)(2,1)}), bf16[4096,2,256]{2,1,0:T(2,128)(2,1)}) %all-gather.5.cloned.1.call-update) | async-done | bytes 4194320 | tf_op jit(solution)/shard_map/all_gather | solution.py:68
  400.9 4.2 %gather_fusion.1 = bf16[512,2,256]{2,1,0:T(2,128)(2,1)S(1)} fusion(bf16[4096,2,256]{2,1,0:T(2,128)(2,1)} %all-gather.5.cloned.1.call-done, s32[1024]{0:T(1024)S(1)} %pad_clamp_fusion.1), kind=kCustom, calls=%fused_computation.1 | custom fusion | bytes 1050624 | tf_op jit(solution)/shard_map/jit(_take)/gather | solution.py:71
  405.0 2.6 add_convert_fusion
  (36 shorter events, 0.6 us)
Async XLA Ops:
  9.9 29.9 %all-to-all-start = ((bf16[32,2,2]{1,2,0:T(2,128)(2,1)}), bf16[32,2,2]{1,2,0:T(2,128)(2,1)S(1)}, u32[]{:S(2)}, u32[]{:S(2)}) async-start(bf16[32,2,2]{1,2,0:T(2,128)(2,1)} %copy.38), calls=%async_computation | async-start | bytes 32768 | tf_op jit(solution)/shard_map/all_to_all | solution.py:37
  39.8 10.5 %copy-start = (s32[2]{0:T(128)S(1)}, s32[2]{0:T(128)}, u32[]{:S(2)}) copy-start(s32[2]{0:T(128)} %param.14) | copy-start | bytes 28
  39.8 238.9 %all-to-all-start.1 = ((bf16[32,2,256,256]{3,2,1,0:T(8,128)(2,1)}), bf16[32,2,256,256]{3,2,1,0:T(8,128)(2,1)}, u32[]{:S(2)}, u32[]{:S(2)}) async-start(bf16[32,2,256,256]{3,2,1,0:T(8,128)(2,1)} %bitcast.43), calls=%async_computation.1 | async-start | bytes 16777216 | tf_op jit(solution)/shard_map/all_to_all | solution.py:36
  49.3 229.4 %all-gather.3.cloned.1.call-start = ((), (), s32[]{:S(2)}) async-start(), calls=%async_computation.2 | async-start | bytes 8650752 | tf_op jit(solution)/shard_map/all_gather | solution.py:17
  50.1 350.8 %all-gather.5.cloned.1.call-start = ((), (), s32[]{:S(2)}) async-start(), calls=%async_computation.3 | async-start | bytes 4718592 | tf_op jit(solution)/shard_map/all_gather | solution.py:68
Sparse Core Ops, SparseCore 0:
  52.8 218.8 all-gather.2
  362.3 38.5 all-gather.4
where the time goes:
time: 415 us; the launch traced here: 414 us
  waiting for transfers between devices  267 us (64%)
  matrix products  54.4 us (13%)
  local copies, waits for them, and re-layouts  47.3 us (11%)
  starting transfers between devices  21.8 us (5%)
  between operations  14.2 us (3%)
  other arithmetic  10.1 us (2%)
    all_to_all x1, waiting for transfers between devices, local(): lax.all_to_all(send_weight, 'tile', split_axis=0, concat_axis=0, tiled=True)  228 us
    all_gather x1, waiting for transfers between devices, local(): everyone = lax.all_gather(ladder, 'pair', axis=0, tiled=True)  37.9 us
    dot_general x4, matrix products, accumulate(): jnp.einsum('nkpt,nka->kpat', terms, select_group, preferred_element_type=...  29.8 us
    dot_general x4, matrix products, accumulate(): jnp.einsum('pnks,nkts->nkpt', chosen, weight_group, preferred_element_typ...  24.6 us
    gather x4, local copies, waits for them, and re-layouts, accumulate(): chosen = jnp.take(gathered, column_group.reshape(-1), axis=1)  24.5 us
    all_to_all x1, starting transfers between devices, local(): lax.all_to_all(labels, 'tile', split_axis=0, concat_axis=0, tiled=True)  12 us
    scatter x1, local copies, waits for them, and re-layouts, local(): send_weight = send_weight.at[target].set(integrals).reshape(tile_devices,...  11.3 us
    all_to_all x1, starting transfers between devices, local(): lax.all_to_all(send_weight, 'tile', split_axis=0, concat_axis=0, tiled=True)  9.54 us
  transfers between devices with their start and end apart: 4, of which 2 were waited for; matrix products, arithmetic and copies ran while one was open for 4% of the time, Pallas kernels for 0%

commit v1 on v0

v1 whole, which is shorter than its diff:
```python
import functools

import jax
import jax.numpy as jnp
from jax import lax
from jax.experimental import pallas as pl
from jax.experimental.pallas import tpu as pltpu
from jax.sharding import PartitionSpec as P

NZ, NY = 8, 4
LABEL_ROWS = 8


def ring_pairs(axis, shift):
    pairs = []
    for z in range(NZ):
        for y in range(NY):
            to = ((z + shift) % NZ, y) if axis == "z" else (z, (y + shift) % NY)
            pairs.append((z * NY + y, to[0] * NY + to[1]))
    return pairs


def ring_gather(axis, piece):
    size = NZ if axis == "z" else NY
    ahead, back = ring_pairs(axis, 1), ring_pairs(axis, -1)
    parts = {0: [piece]}
    left = right = piece
    for step in range(1, size // 2):
        left = lax.ppermute(left, "tile", ahead)
        right = lax.ppermute(right, "tile", back)
        parts[step], parts[size - step] = [left], [right]
    half = piece.shape[0] // 2
    parts[size // 2] = [
        lax.ppermute(left[:half], "tile", ahead),
        lax.ppermute(right[half:], "tile", back),
    ]
    return [p for s in range(size) for p in parts[s]]


def route_kernel(rows_ref, cols_ref, share_ref, w_ref, o_ref, count):
    owners, height, width = o_ref.shape
    blocks, share, _ = w_ref.shape
    o_ref[...] = jnp.zeros_like(o_ref)
    for d in range(owners):
        count[d] = 0
    line = lax.broadcasted_iota(jnp.int32, (LABEL_ROWS, width), 0)
    for b in range(blocks):
        row = rows_ref[b]
        owner = row // 2
        rank = count[owner]
        count[owner] = rank + 1
        o_ref[owner, pl.ds(pl.multiple_of(rank * share, share), share), :] = w_ref[b]
        tags = o_ref[owner, 2 * share :, :].astype(jnp.float32)
        tags = jnp.where(line == 2 * rank, (row % 2 + 1).astype(jnp.float32), tags)
        tags = jnp.where(line == 2 * rank + 1, cols_ref[b].astype(jnp.float32), tags)
        o_ref[owner, 2 * share :, :] = tags.astype(jnp.bfloat16)


def route(block_rows, block_cols, share_id, integrals, owners, shares):
    blocks, height, width = integrals.shape
    share = height // shares
    return pl.pallas_call(
        route_kernel,
        grid_spec=pltpu.PrefetchScalarGridSpec(
            num_scalar_prefetch=3,
            grid=(1,),
            in_specs=[pl.BlockSpec((blocks, share, width), lambda i, r, c, s: (0, s[0], 0))],
            out_specs=pl.BlockSpec((owners, 2 * share + LABEL_ROWS, width), lambda i, r, c, s: (0, 0, 0)),
            scratch_shapes=[pltpu.SMEM((owners,), jnp.int32)],
        ),
        out_shape=jax.ShapeDtypeStruct((owners, 2 * share + LABEL_ROWS, width), jnp.bfloat16),
        compiler_params=pltpu.CompilerParams(vmem_limit_bytes=16 << 20),
    )(block_rows, block_cols, share_id, integrals)


def mirror_kernel(first_ref, live_ref, mirror_ref, all_ref, a_ref, b_ref, *, step):
    total_pairs, width = all_ref.shape
    count = a_ref.shape[0]
    live = lax.broadcasted_iota(jnp.int32, (1, width), 1) < live_ref[0]
    for part, out in enumerate((a_ref, b_ref)):
        me = lax.broadcasted_iota(jnp.int32, (count, step), 0) + (first_ref[0] + part * count)
        total = jnp.zeros((count, width), jnp.float32)
        for at in range(0, total_pairs, step):
            here = lax.broadcasted_iota(jnp.int32, (count, step), 1) + at
            pick = (mirror_ref[:, at : at + step] == me) | (here == me)
            pick = jnp.where(pick, 1.0, 0.0).astype(jnp.bfloat16)
            total = total + jnp.dot(pick, all_ref[at : at + step, :], preferred_element_type=jnp.float32)
        out[...] = jnp.where(live, total, 0.0).astype(jnp.bfloat16)


def mirror_sum(first, live, mirror, everyone, count):
    total_pairs, width = everyone.shape
    half = count // 2
    smem = pl.BlockSpec(memory_space=pltpu.SMEM)
    vmem = pl.BlockSpec(memory_space=pltpu.VMEM)
    return pl.pallas_call(
        functools.partial(mirror_kernel, step=512),
        in_specs=[smem, smem, vmem, vmem],
        out_specs=[vmem, vmem],
        out_shape=[jax.ShapeDtypeStruct((half, width), jnp.bfloat16)] * 2,
        compiler_params=pltpu.CompilerParams(vmem_limit_bytes=24 << 20),
    )(first, live, mirror.reshape(1, total_pairs), everyone)


def ladder_kernel(tags_ref, place_a, place_b, live_ref, *refs, n_a, n_b, group):
    pieces_a, pieces_b = refs[:n_a], refs[n_a : n_a + n_b]
    w_ref, o_ref, amps_a, amps_b, total, sems = refs[n_a + n_b :]
    share = w_ref.shape[2] // 2
    width = w_ref.shape[3]
    half = total.shape[1] // 2
    step = pl.program_id(0)

    def copies():
        made = []
        for pieces, amps in ((pieces_a, amps_a), (pieces_b, amps_b)):
            at = 0
            for piece in pieces:
                rows = piece.shape[0]
                made.append(
                    pltpu.make_async_copy(piece, amps.at[pl.ds(at, rows), :], sems.at[len(made)])
                )
                at += rows
        return made

    @pl.when(step == 0)
    def _():
        made = copies()
        for copy in made:
            copy.start()
        total[...] = jnp.zeros_like(total)
        for copy in made:
            copy.wait()

    for i in range(group):
        for j in range(2):
            slot = (step * group + i) * 2 + j
            tag = tags_ref[slot]

            @pl.when(tag > 0)
            def _(i=i, j=j, slot=slot, tag=tag):
                weight = w_ref[:, i, j * share : (j + 1) * share, :].reshape(-1, width)
                row = tag - 1
                at_a = pl.multiple_of(place_a[slot] * half, half)
                at_b = pl.multiple_of(place_b[slot] * half, half)
                for at, amps, base in ((at_a, amps_a, 0), (at_b, amps_b, half)):
                    term = lax.dot_general(
                        amps[pl.ds(at, half), :],
                        weight,
                        (((1,), (1,)), ((), ())),
                        preferred_element_type=jnp.float32,
                    )
                    total[row, base : base + half, :] += term

    @pl.when(step == pl.num_programs(0) - 1)
    def _():
        position = lax.broadcasted_iota(jnp.int32, (1, width), 1)
        for r in range(2):
            kept = jnp.where(position < live_ref[r], total[r], 0.0)
            o_ref[:, r * width : (r + 1) * width] = kept.astype(jnp.bfloat16)


def ladder(tags, place_a, place_b, live, pieces_a, pieces_b, weights, count):
    shares, senders, height, width = weights.shape
    group = 4
    n_a, n_b = len(pieces_a), len(pieces_b)
    rows_a = sum(p.shape[0] for p in pieces_a)
    rows_b = sum(p.shape[0] for p in pieces_b)
    return pl.pallas_call(
        functools.partial(ladder_kernel, n_a=n_a, n_b=n_b, group=group),
        grid_spec=pltpu.PrefetchScalarGridSpec(
            num_scalar_prefetch=4,
            grid=(senders // group,),
            in_specs=[pl.BlockSpec(memory_space=pl.ANY)] * (n_a + n_b)
            + [pl.BlockSpec((shares, group, height, width), lambda i, *_: (0, i, 0, 0))],
            out_specs=pl.BlockSpec((count, 2 * width), lambda i, *_: (0, 0)),
            scratch_shapes=[
                pltpu.VMEM((rows_a, width), jnp.bfloat16),
                pltpu.VMEM((rows_b, width), jnp.bfloat16),
                pltpu.VMEM((2, count, width), jnp.float32),
                pltpu.SemaphoreType.DMA((n_a + n_b,)),
            ],
        ),
        out_shape=jax.ShapeDtypeStruct((count, 2 * width), jnp.bfloat16),
        compiler_params=pltpu.CompilerParams(vmem_limit_bytes=32 << 20),
    )(tags, place_a, place_b, live, *pieces_a, *pieces_b, weights)


def local(amplitudes, size_cd, integrals, block_rows, block_cols, size_ab, mirror):
    count, _, width = amplitudes.shape
    owners = lax.axis_size("tile")
    shares = lax.axis_size("pair")
    pair_id = lax.axis_index("pair").astype(jnp.int32)
    tile_id = lax.axis_index("tile").astype(jnp.int32)
    share = width // shares

    everyone = lax.all_gather(amplitudes.reshape(count, width), "pair", axis=0, tiled=True)

    send = route(block_rows, block_cols, pair_id.reshape(1), integrals, owners, shares)
    got = lax.all_to_all(send, "tile", split_axis=0, concat_axis=0, tiled=True)
    weights = lax.all_gather(got[:, : 2 * share, :], "pair", axis=0)
    labels = got[:, 2 * share : 2 * share + 4, 0].astype(jnp.int32)
    tags = labels[:, 0::2].reshape(-1)
    cols = labels[:, 1::2].reshape(-1)
    behind_z = (tile_id // NY - cols // NY) % NZ
    behind_y = (tile_id % NY - cols % NY) % NY

    half_a, half_b = mirror_sum((pair_id * count).reshape(1), size_cd, mirror, everyone, count)
    bundle_a = jnp.concatenate(ring_gather("y", half_a), axis=0)
    bundle_b = jnp.concatenate(ring_gather("z", half_b), axis=0)
    pieces_a = ring_gather("z", bundle_a)
    pieces_b = ring_gather("y", bundle_b)
    result = ladder(
        tags,
        behind_z * NY + behind_y,
        behind_y * NZ + behind_z,
        size_ab,
        pieces_a,
        pieces_b,
        weights,
        count,
    )
    return result.reshape(count, 2, width)


def solution(mesh):
    in_specs = (
        P("pair", "tile", None),
        P("tile"),
        P("tile", None, None),
        P("tile"),
        P("tile"),
        P("tile"),
        P(),
    )
    out_specs = P("pair", "tile", None)
    return jax.shard_map(local, mesh=mesh, in_specs=in_specs, out_specs=out_specs, check_vma=False)
```

time: 415 us -> 170 us (0.41)
  the two profiles are of different devices: /device:TPU:1 before, /device:TPU:2 now
where the time goes in v1:
time: 170 us; the launch traced here: 169 us
  blocking collectives  44.2 us (26%)
  waiting for transfers between devices  36.8 us (22%)
  starting transfers between devices  35.4 us (21%)
  local copies, waits for them, and re-layouts  23.2 us (14%)
  between operations  14.4 us (8%)
  Pallas kernels  14.3 us (8%)
    all_to_all x1, blocking collectives, local(): got = lax.all_to_all(send, 'tile', split_axis=0, concat_axis=0, tiled=True)  44.2 us
    ppermute x8, starting transfers between devices, ring_gather(): right = lax.ppermute(right, 'tile', back)  19.5 us
    unnamed x44, local copies, waits for them, and re-layouts  15.6 us
    ppermute x8, waiting for transfers between devices, ring_gather(): right = lax.ppermute(right, 'tile', back)  13.1 us
    ppermute x4, starting transfers between devices, ring_gather(): lax.ppermute(right[half:], 'tile', back)  12.8 us
    pallas_call x1, Pallas kernels, ladder(): pl.pallas_call(functools.partial(ladder_kernel, n_a=n_a, n_b=n_b, group=g...  11.6 us
    ppermute x8, waiting for transfers between devices, ring_gather(): left = lax.ppermute(left, 'tile', ahead)  11.4 us
    ppermute x4, waiting for transfers between devices, ring_gather(): lax.ppermute(left[:half], 'tile', ahead)  9.31 us
  transfers between devices with their start and end apart: 26, of which 10 were waited for; matrix products, arithmetic and copies ran while one was open for 5% of the time, Pallas kernels for 2%

profile of v1, /device:TPU:2, one launch (start us, length us, event | category | flops | bytes accessed | tf_op | source)
XLA Modules:
  0.0 169.2 jit_solution(6952153381509407383)
XLA Ops:
  6.5 0.7 all-gather.5.cloned.1.call-update
  7.3 2.2 %copy-done.1 = bf16[32,256,256]{2,1,0:T(8,128)(2,1)S(1)} copy-done((bf16[32,256,256]{2,1,0:T(8,128)(2,1)S(1)}, bf16[32,256,256]{2,1,0:T(8,128)(2,1)}, u32[]{:S(2)}) %copy-start.1) | copy-done | bytes 4194328
  9.5 0.7 copy-done.13
  10.2 0.7 copy-done.14
  10.8 0.9 shard_map.73
  11.7 44.2 %all_to_all.5 = bf16[32,72,256]{2,1,0:T(8,128)(2,1)S(1)} all-to-all(bf16[32,72,256]{2,1,0:T(8,128)(2,1)S(1)} %shard_map.73), channel_id=1, replica_groups=mesh['pair'=8,'tile'=32] {'tile'}, dimensions={0} | all-to-all | bytes 2359296 | tf_op jit(solution)/shard_map/all_to_all | solution.py:199
  56.0 1.0 copy-done.15
  57.0 1.2 slice.57
  58.9 1.6 copy-done.2
  60.5 1.8 %shard_map.74 = (bf16[256,256]{1,0:T(8,128)(2,1)S(1)}, bf16[256,256]{1,0:T(8,128)(2,1)S(1)}) custom-call(s32[1]{0:T(128)} %bitcast.2.first_ref, s32[1]{0:T(128)S(6)} %copy.32.live_ref, s32[1,4096]{1,0:T(1,128)S(1)} %bitcast.8, bf16[4096,256]{1,0:T(8,128)(2,1)S(1)} %bitcast.7), custom_call_target="tpu_custom_call" | custom-call | tf_op jit(solution)/shard_map/pallas_call | solution.py:96
  62.2 0.9 collective-permute-start.12
  63.1 2.4 %collective-permute-start.16 = (bf16[256,256]{1,0:T(8,128)(2,1)S(1)}, bf16[256,256]{1,0:T(8,128)(2,1)S(1)}, u32[]{:S(2)}, u32[]{:S(2)}) collective-permute-start(bf16[256,256]{1,0:T(8,128)(2,1)S(1)} %get-tuple-element.8), channel_id=1, source_target_pairs={{0,28},{1,29},{2,30},{3,31},{4,0},{5,1},{6,2},{7,3},{8,4},{9,5},{1... | collective-permute-start | bytes 393224 | tf_op jit(solution)/shard_map/ppermute | solution.py:30
  65.6 3.2 %collective-permute-start.2 = (bf16[256,256]{1,0:T(8,128)(2,1)S(1)}, bf16[256,256]{1,0:T(8,128)(2,1)S(1)}, u32[]{:S(2)}, u32[]{:S(2)}) collective-permute-start(bf16[256,256]{1,0:T(8,128)(2,1)S(1)} %get-tuple-element.7), channel_id=1, source_target_pairs={{0,3},{1,0},{2,1},{3,2},{4,7},{5,4},{6,5},{7,6},{8,11},{9,8},{10,9... | collective-permute-start | bytes 393224 | tf_op jit(solution)/shard_map/ppermute | solution.py:30
  68.8 2.9 %collective-permute-done = bf16[256,256]{1,0:T(8,128)(2,1)S(1)} collective-permute-done((bf16[256,256]{1,0:T(8,128)(2,1)S(1)}, bf16[256,256]{1,0:T(8,128)(2,1)S(1)}, u32[]{:S(2)}, u32[]{:S(2)}) %collective-permute-start) | collective-permute-done | bytes 131104 | tf_op jit(solution)/shard_map/ppermute | solution.py:29
  71.8 3.3 %collective-permute-start.3 = (bf16[128,256]{1,0:T(8,128)(2,1)S(1)}, bf16[128,256]{1,0:T(8,128)(2,1)S(1)}, u32[]{:S(2)}, u32[]{:S(2)}) collective-permute-start(bf16[128,256]{1,0:T(8,128)(2,1)S(1)} %slice.50), channel_id=1, source_target_pairs={{0,3},{1,0},{2,1},{3,2},{4,7},{5,4},{6,5},{7,6},{8,11},{9,8},{10,9... | collective-permute-start | bytes 196616 | tf_op jit(solution)/shard_map/ppermute | solution.py:35
  75.1 3.2 %collective-permute-start.17 = (bf16[256,256]{1,0:T(8,128)(2,1)S(1)}, bf16[256,256]{1,0:T(8,128)(2,1)S(1)}, u32[]{:S(2)}, u32[]{:S(2)}) collective-permute-start(bf16[256,256]{1,0:T(8,128)(2,1)S(1)} %collective-permute-done.16), channel_id=1, source_target_pairs={{0,28},{1,29},{2,30},{3,31},{4,0},{5,1},{6,2},{7,3},{8,4},{9,5},{1... | collective-permute-start | bytes 393224 | tf_op jit(solution)/shard_map/ppermute | solution.py:30
  78.4 4.0 %collective-permute-done.13 = bf16[256,256]{1,0:T(8,128)(2,1)S(1)} collective-permute-done((bf16[256,256]{1,0:T(8,128)(2,1)S(1)}, bf16[256,256]{1,0:T(8,128)(2,1)S(1)}, u32[]{:S(2)}, u32[]{:S(2)}) %collective-permute-start.13) | collective-permute-done | bytes 131104 | tf_op jit(solution)/shard_map/ppermute | solution.py:29
  82.4 3.5 %collective-permute-start.18 = (bf16[256,256]{1,0:T(8,128)(2,1)S(1)}, bf16[256,256]{1,0:T(8,128)(2,1)S(1)}, u32[]{:S(2)}, u32[]{:S(2)}) collective-permute-start(bf16[256,256]{1,0:T(8,128)(2,1)S(1)} %collective-permute-done.17), channel_id=1, source_target_pairs={{0,28},{1,29},{2,30},{3,31},{4,0},{5,1},{6,2},{7,3},{8,4},{9,5},{1... | collective-permute-start | bytes 393224 | tf_op jit(solution)/shard_map/ppermute | solution.py:30
  86.0 2.0 %collective-permute-start.4 = (bf16[1024,256]{1,0:T(8,128)(2,1)S(1)}, bf16[1024,256]{1,0:T(8,128)(2,1)S(1)}, u32[]{:S(2)}, u32[]{:S(2)}) collective-permute-start(bf16[1024,256]{1,0:T(8,128)(2,1)S(1)} %constant_dynamic-update-slice_fusion.refs_0_), channel_id=1, source_target_pairs={{0,4},{1,5},{2,6},{3,7},{4,8},{5,9},{6,10},{7,11},{8,12},{9,13},{1... | collective-permute-start | bytes 1572872 | tf_op jit(solution)/shard_map/ppermute | solution.py:29
  88.0 2.0 %collective-permute-done.14 = bf16[256,256]{1,0:T(8,128)(2,1)S(1)} collective-permute-done((bf16[256,256]{1,0:T(8,128)(2,1)S(1)}, bf16[256,256]{1,0:T(8,128)(2,1)S(1)}, u32[]{:S(2)}, u32[]{:S(2)}) %collective-permute-start.14) | collective-permute-done | bytes 131104 | tf_op jit(solution)/shard_map/ppermute | solution.py:29
  90.1 3.3 %collective-permute-start.19 = (bf16[128,256]{1,0:T(8,128)(2,1)S(1)}, bf16[128,256]{1,0:T(8,128)(2,1)S(1)}, u32[]{:S(2)}, u32[]{:S(2)}) collective-permute-start(bf16[128,256]{1,0:T(8,128)(2,1)S(1)} %slice.54), channel_id=1, source_target_pairs={{0,28},{1,29},{2,30},{3,31},{4,0},{5,1},{6,2},{7,3},{8,4},{9,5},{1... | collective-permute-start | bytes 196616 | tf_op jit(solution)/shard_map/ppermute | solution.py:35
  93.4 3.9 %collective-permute-done.15 = bf16[128,256]{1,0:T(8,128)(2,1)S(1)} collective-permute-done((bf16[128,256]{1,0:T(8,128)(2,1)S(1)}, bf16[128,256]{1,0:T(8,128)(2,1)S(1)}, u32[]{:S(2)}, u32[]{:S(2)}) %collective-permute-start.15) | collective-permute-done | bytes 65568 | tf_op jit(solution)/shard_map/ppermute | solution.py:34
  97.5 3.2 %collective-permute-start.22 = (bf16[2048,256]{1,0:T(8,128)(2,1)S(1)}, bf16[2048,256]{1,0:T(8,128)(2,1)S(1)}, u32[]{:S(2)}, u32[]{:S(2)}) collective-permute-start(bf16[2048,256]{1,0:T(8,128)(2,1)S(1)} %constant_dynamic-update-slice_fusion.5.refs_9_), channel_id=1, source_target_pairs={{0,3},{1,0},{2,1},{3,2},{4,7},{5,4},{6,5},{7,6},{8,11},{9,8},{10,9... | collective-permute-start | bytes 3145736 | tf_op jit(solution)/shard_map/ppermute | solution.py:30
  100.7 2.1 %collective-permute-start.9 = (bf16[1024,256]{1,0:T(8,128)(2,1)S(1)}, bf16[1024,256]{1,0:T(8,128)(2,1)}, u32[]{:S(2)}, u32[]{:S(2)}) collective-permute-start(bf16[1024,256]{1,0:T(8,128)(2,1)S(1)} %collective-permute-done.8.refs_8_), channel_id=1, source_target_pairs={{0,28},{1,29},{2,30},{3,31},{4,0},{5,1},{6,2},{7,3},{8,4},{9,5},{1... | collective-permute-start | bytes 1572872 | tf_op jit(solution)/shard_map/ppermute | solution.py:30
  102.8 0.8 copy-done.7
  103.7 0.8 copy-done.9
  104.5 11.0 %collective-permute-done.9.refs_7_ = bf16[1024,256]{1,0:T(8,128)(2,1)} collective-permute-done((bf16[1024,256]{1,0:T(8,128)(2,1)S(1)}, bf16[1024,256]{1,0:T(8,128)(2,1)}, u32[]{:S(2)}, u32[]{:S(2)}) %collective-permute-start.9) | collective-permute-done | bytes 524320 | tf_op jit(solution)/shard_map/ppermute | solution.py:30
  115.5 1.8 %collective-permute-start.10 = (bf16[1024,256]{1,0:T(8,128)(2,1)}, bf16[1024,256]{1,0:T(8,128)(2,1)}, u32[]{:S(2)}, u32[]{:S(2)}) collective-permute-start(bf16[1024,256]{1,0:T(8,128)(2,1)} %collective-permute-done.9.refs_7_), channel_id=1, source_target_pairs={{0,28},{1,29},{2,30},{3,31},{4,0},{5,1},{6,2},{7,3},{8,4},{9,5},{1... | collective-permute-start | bytes 1572872 | tf_op jit(solution)/shard_map/ppermute | solution.py:30
  117.3 1.1 collective-permute-done.5.refs_2_
  118.4 1.3 collective-permute-done.20.refs_10_
  119.7 0.8 slice.55
  120.5 0.8 slice.56
  121.4 3.2 %collective-permute-start.23 = (bf16[1024,256]{1,0:T(8,128)(2,1)}, bf16[1024,256]{1,0:T(8,128)(2,1)}, u32[]{:S(2)}, u32[]{:S(2)}) collective-permute-start(bf16[1024,256]{1,0:T(8,128)(2,1)} %slice.56), channel_id=1, source_target_pairs={{0,3},{1,0},{2,1},{3,2},{4,7},{5,4},{6,5},{7,6},{8,11},{9,8},{10,9... | collective-permute-start | bytes 1572872 | tf_op jit(solution)/shard_map/ppermute | solution.py:35
  124.6 0.9 slice_convert_fusion
  125.7 0.1 reshape.25
  125.8 2.0 %collective-permute-done.10.refs_6_ = bf16[1024,256]{1,0:T(8,128)(2,1)} collective-permute-done((bf16[1024,256]{1,0:T(8,128)(2,1)}, bf16[1024,256]{1,0:T(8,128)(2,1)}, u32[]{:S(2)}, u32[]{:S(2)}) %collective-permute-start.10) | collective-permute-done | bytes 524320 | tf_op jit(solution)/shard_map/ppermute | solution.py:30
  127.8 1.7 slice.52
  129.5 3.0 %collective-permute-start.11 = (bf16[512,256]{1,0:T(8,128)(2,1)}, bf16[512,256]{1,0:T(8,128)(2,1)S(1)}, u32[]{:S(2)}, u32[]{:S(2)}) collective-permute-start(bf16[512,256]{1,0:T(8,128)(2,1)} %slice.52), channel_id=1, source_target_pairs={{0,28},{1,29},{2,30},{3,31},{4,0},{5,1},{6,2},{7,3},{8,4},{9,5},{1... | collective-permute-start | bytes 786440 | tf_op jit(solution)/shard_map/ppermute | solution.py:35
  132.4 1.7 slice.51
  134.4 2.3 %collective-permute-done.11.refs_5_ = bf16[512,256]{1,0:T(8,128)(2,1)S(1)} collective-permute-done((bf16[512,256]{1,0:T(8,128)(2,1)}, bf16[512,256]{1,0:T(8,128)(2,1)S(1)}, u32[]{:S(2)}, u32[]{:S(2)}) %collective-permute-start.11) | collective-permute-done | bytes 262176 | tf_op jit(solution)/shard_map/ppermute | solution.py:35
  136.6 5.4 %collective-permute-done.7.refs_4_ = bf16[512,256]{1,0:T(8,128)(2,1)} collective-permute-done((bf16[512,256]{1,0:T(8,128)(2,1)}, bf16[512,256]{1,0:T(8,128)(2,1)}, u32[]{:S(2)}, u32[]{:S(2)}) %collective-permute-start.7) | collective-permute-done | bytes 262176 | tf_op jit(solution)/shard_map/ppermute | solution.py:34
  142.1 3.4 %copy-done = bf16[256,64,256]{2,1,0:T(8,128)(2,1)S(1)} copy-done((bf16[256,64,256]{2,1,0:T(8,128)(2,1)S(1)}, bf16[256,64,256]{2,1,0:T(8,128)(2,1)}, u32[]{:S(2)}) %copy-start) | copy-done | bytes 8388632
  145.4 1.2 copy-done.4
  146.7 1.0 copy-done.6
  147.7 1.0 copy-done.8
  148.7 1.0 copy-done.10
  149.8 11.6 %shard_map.75 = bf16[512,512]{1,0:T(8,128)(2,1)S(1)} custom-call(s32[64]{0:T(128)S(1)} %reshape.24.tags_ref, s32[64]{0:T(128)S(1)} %multiply_add_fusion.1.place_a, s32[64]{0:T(128)S(1)} %get-tuple-element.9.place_b, s32[2]{0:T(128)S(1)} %copy-done.12, bf16[1024,256]{1,0:T(8,128)(2,1)S(1)} %copy-done.6, bf16[1024,256]{1,0:T(8,128)(2,1)S(1)} %copy-done.10, ...), custom_call_target="tpu_custom_call" | custom-call | tf_op jit(solution)/shard_map/pallas_call | solution.py:168
  161.4 0.9 reshape.29
  (76 shorter events, 1.0 us)
Async XLA Ops:
  6.5 52.3 %all-gather.5.cloned.1.call-start = ((), (), s32[]{:S(2)}) async-start(), calls=%async_computation.1 | async-start | bytes 2359296 | tf_op jit(solution)/shard_map/all_gather | solution.py:196
  7.3 134.8 %all-gather.7.cloned.1.call-start = ((), (), s32[]{:S(2)}) async-start(), calls=%async_computation.2 | async-start | bytes 9437184 | tf_op jit(solution)/shard_map/all_gather | solution.py:200
  7.3 2.2 %copy-start.1 = (bf16[32,256,256]{2,1,0:T(8,128)(2,1)S(1)}, bf16[32,256,256]{2,1,0:T(8,128)(2,1)}, u32[]{:S(2)}) copy-start(bf16[32,256,256]{2,1,0:T(8,128)(2,1)} %w_ref.1) | copy-start | bytes 12582916
  9.5 0.7 copy-start.13
  10.2 0.7 copy-start.14
  56.0 1.0 copy-start.15
  57.0 1.9 %copy-start.11 = (s32[4096]{0:T(1024)S(1)}, s32[4096]{0:T(1024)}, u32[]{:S(2)}) copy-start(s32[4096]{0:T(1024)} %param.13) | copy-start | bytes 49156
  58.9 1.6 copy-start.2
  62.2 12.8 %collective-permute-start.12 = (bf16[256,256]{1,0:T(8,128)(2,1)S(1)}, bf16[256,256]{1,0:T(8,128)(2,1)S(1)}, u32[]{:S(2)}, u32[]{:S(2)}) collective-permute-start(bf16[256,256]{1,0:T(8,128)(2,1)S(1)} %get-tuple-element.8), channel_id=1, source_target_pairs={{0,4},{1,5},{2,6},{3,7},{4,8},{5,9},{6,10},{7,11},{8,12},{9,13},{1... | collective-permute-start | bytes 393224 | tf_op jit(solution)/shard_map/ppermute | solution.py:29
  63.1 12.0 %collective-permute-start.16 = (bf16[256,256]{1,0:T(8,128)(2,1)S(1)}, bf16[256,256]{1,0:T(8,128)(2,1)S(1)}, u32[]{:S(2)}, u32[]{:S(2)}) collective-permute-start(bf16[256,256]{1,0:T(8,128)(2,1)S(1)} %get-tuple-element.8), channel_id=1, source_target_pairs={{0,28},{1,29},{2,30},{3,31},{4,0},{5,1},{6,2},{7,3},{8,4},{9,5},{1... | collective-permute-start | bytes 393224 | tf_op jit(solution)/shard_map/ppermute | solution.py:30
  65.6 6.2 %collective-permute-start = (bf16[256,256]{1,0:T(8,128)(2,1)S(1)}, bf16[256,256]{1,0:T(8,128)(2,1)S(1)}, u32[]{:S(2)}, u32[]{:S(2)}) collective-permute-start(bf16[256,256]{1,0:T(8,128)(2,1)S(1)} %get-tuple-element.7), channel_id=1, source_target_pairs={{0,1},{1,2},{2,3},{3,0},{4,5},{5,6},{6,7},{7,4},{8,9},{9,10},{10,1... | collective-permute-start | bytes 393224 | tf_op jit(solution)/shard_map/ppermute | solution.py:29
  65.6 6.2 %collective-permute-start.2 = (bf16[256,256]{1,0:T(8,128)(2,1)S(1)}, bf16[256,256]{1,0:T(8,128)(2,1)S(1)}, u32[]{:S(2)}, u32[]{:S(2)}) collective-permute-start(bf16[256,256]{1,0:T(8,128)(2,1)S(1)} %get-tuple-element.7), channel_id=1, source_target_pairs={{0,3},{1,0},{2,1},{3,2},{4,7},{5,4},{6,5},{7,6},{8,11},{9,8},{10,9... | collective-permute-start | bytes 393224 | tf_op jit(solution)/shard_map/ppermute | solution.py:30
  71.7 6.6 %collective-permute-start.1 = (bf16[128,256]{1,0:T(8,128)(2,1)S(1)}, bf16[128,256]{1,0:T(8,128)(2,1)S(1)}, u32[]{:S(2)}, u32[]{:S(2)}) collective-permute-start(bf16[128,256]{1,0:T(8,128)(2,1)S(1)} %slice.49), channel_id=1, source_target_pairs={{0,1},{1,2},{2,3},{3,0},{4,5},{5,6},{6,7},{7,4},{8,9},{9,10},{10,1... | collective-permute-start | bytes 196616 | tf_op jit(solution)/shard_map/ppermute | solution.py:34
  71.8 6.6 %collective-permute-start.3 = (bf16[128,256]{1,0:T(8,128)(2,1)S(1)}, bf16[128,256]{1,0:T(8,128)(2,1)S(1)}, u32[]{:S(2)}, u32[]{:S(2)}) collective-permute-start(bf16[128,256]{1,0:T(8,128)(2,1)S(1)} %slice.50), channel_id=1, source_target_pairs={{0,3},{1,0},{2,1},{3,2},{4,7},{5,4},{6,5},{7,6},{8,11},{9,8},{10,9... | collective-permute-start | bytes 196616 | tf_op jit(solution)/shard_map/ppermute | solution.py:35
  75.1 7.3 %collective-permute-start.13 = (bf16[256,256]{1,0:T(8,128)(2,1)S(1)}, bf16[256,256]{1,0:T(8,128)(2,1)S(1)}, u32[]{:S(2)}, u32[]{:S(2)}) collective-permute-start(bf16[256,256]{1,0:T(8,128)(2,1)S(1)} %collective-permute-done.12), channel_id=1, source_target_pairs={{0,4},{1,5},{2,6},{3,7},{4,8},{5,9},{6,10},{7,11},{8,12},{9,13},{1... | collective-permute-start | bytes 393224 | tf_op jit(solution)/shard_map/ppermute | solution.py:29
  75.1 7.3 %collective-permute-start.17 = (bf16[256,256]{1,0:T(8,128)(2,1)S(1)}, bf16[256,256]{1,0:T(8,128)(2,1)S(1)}, u32[]{:S(2)}, u32[]{:S(2)}) collective-permute-start(bf16[256,256]{1,0:T(8,128)(2,1)S(1)} %collective-permute-done.16), channel_id=1, source_target_pairs={{0,28},{1,29},{2,30},{3,31},{4,0},{5,1},{6,2},{7,3},{8,4},{9,5},{1... | collective-permute-start | bytes 393224 | tf_op jit(solution)/shard_map/ppermute | solution.py:30
  82.4 7.6 %collective-permute-start.14 = (bf16[256,256]{1,0:T(8,128)(2,1)S(1)}, bf16[256,256]{1,0:T(8,128)(2,1)S(1)}, u32[]{:S(2)}, u32[]{:S(2)}) collective-permute-start(bf16[256,256]{1,0:T(8,128)(2,1)S(1)} %collective-permute-done.13), channel_id=1, source_target_pairs={{0,4},{1,5},{2,6},{3,7},{4,8},{5,9},{6,10},{7,11},{8,12},{9,13},{1... | collective-permute-start | bytes 393224 | tf_op jit(solution)/shard_map/ppermute | solution.py:29
  82.4 7.7 %collective-permute-start.18 = (bf16[256,256]{1,0:T(8,128)(2,1)S(1)}, bf16[256,256]{1,0:T(8,128)(2,1)S(1)}, u32[]{:S(2)}, u32[]{:S(2)}) collective-permute-start(bf16[256,256]{1,0:T(8,128)(2,1)S(1)} %collective-permute-done.17), channel_id=1, source_target_pairs={{0,28},{1,29},{2,30},{3,31},{4,0},{5,1},{6,2},{7,3},{8,4},{9,5},{1... | collective-permute-start | bytes 393224 | tf_op jit(solution)/shard_map/ppermute | solution.py:30
  85.9 11.6 %copy-start.5 = (bf16[1024,256]{1,0:T(8,128)(2,1)}, bf16[1024,256]{1,0:T(8,128)(2,1)S(1)}, u32[]{:S(2)}) copy-start(bf16[1024,256]{1,0:T(8,128)(2,1)S(1)} %constant_dynamic-update-slice_fusion.refs_0_) | copy-start | bytes 1572868
  85.9 14.9 %collective-permute-start.8 = (bf16[1024,256]{1,0:T(8,128)(2,1)S(1)}, bf16[1024,256]{1,0:T(8,128)(2,1)S(1)}, u32[]{:S(2)}, u32[]{:S(2)}) collective-permute-start(bf16[1024,256]{1,0:T(8,128)(2,1)S(1)} %constant_dynamic-update-slice_fusion.refs_0_), channel_id=1, source_target_pairs={{0,28},{1,29},{2,30},{3,31},{4,0},{5,1},{6,2},{7,3},{8,4},{9,5},{1... | collective-permute-start | bytes 1572872 | tf_op jit(solution)/shard_map/ppermute | solution.py:30
  86.0 17.7 %collective-permute-start.4 = (bf16[1024,256]{1,0:T(8,128)(2,1)S(1)}, bf16[1024,256]{1,0:T(8,128)(2,1)S(1)}, u32[]{:S(2)}, u32[]{:S(2)}) collective-permute-start(bf16[1024,256]{1,0:T(8,128)(2,1)S(1)} %constant_dynamic-update-slice_fusion.refs_0_), channel_id=1, source_target_pairs={{0,4},{1,5},{2,6},{3,7},{4,8},{5,9},{6,10},{7,11},{8,12},{9,13},{1... | collective-permute-start | bytes 1572872 | tf_op jit(solution)/shard_map/ppermute | solution.py:29
  90.0 7.3 %collective-permute-start.15 = (bf16[128,256]{1,0:T(8,128)(2,1)S(1)}, bf16[128,256]{1,0:T(8,128)(2,1)S(1)}, u32[]{:S(2)}, u32[]{:S(2)}) collective-permute-start(bf16[128,256]{1,0:T(8,128)(2,1)S(1)} %slice.53), channel_id=1, source_target_pairs={{0,4},{1,5},{2,6},{3,7},{4,8},{5,9},{6,10},{7,11},{8,12},{9,13},{1... | collective-permute-start | bytes 196616 | tf_op jit(solution)/shard_map/ppermute | solution.py:34
  90.1 7.2 %collective-permute-start.19 = (bf16[128,256]{1,0:T(8,128)(2,1)S(1)}, bf16[128,256]{1,0:T(8,128)(2,1)S(1)}, u32[]{:S(2)}, u32[]{:S(2)}) collective-permute-start(bf16[128,256]{1,0:T(8,128)(2,1)S(1)} %slice.54), channel_id=1, source_target_pairs={{0,28},{1,29},{2,30},{3,31},{4,0},{5,1},{6,2},{7,3},{8,4},{9,5},{1... | collective-permute-start | bytes 196616 | tf_op jit(solution)/shard_map/ppermute | solution.py:35
  97.3 44.7 %copy-start.12 = (s32[2]{0:T(128)S(1)}, s32[2]{0:T(128)}, u32[]{:S(2)}) copy-start(s32[2]{0:T(128)} %live_ref.2) | copy-start | bytes 28
  97.4 44.6 %copy-start.3 = (bf16[2048,256]{1,0:T(8,128)(2,1)}, bf16[2048,256]{1,0:T(8,128)(2,1)S(1)}, u32[]{:S(2)}) copy-start(bf16[2048,256]{1,0:T(8,128)(2,1)S(1)} %constant_dynamic-update-slice_fusion.5.refs_9_) | copy-start | bytes 3145732
  97.4 22.3 %collective-permute-start.20 = (bf16[2048,256]{1,0:T(8,128)(2,1)S(1)}, bf16[2048,256]{1,0:T(8,128)(2,1)S(1)}, u32[]{:S(2)}, u32[]{:S(2)}) collective-permute-start(bf16[2048,256]{1,0:T(8,128)(2,1)S(1)} %constant_dynamic-update-slice_fusion.5.refs_9_), channel_id=1, source_target_pairs={{0,1},{1,2},{2,3},{3,0},{4,5},{5,6},{6,7},{7,4},{8,9},{9,10},{10,1... | collective-permute-start | bytes 3145736 | tf_op jit(solution)/shard_map/ppermute | solution.py:29
  97.5 23.0 %collective-permute-start.22 = (bf16[2048,256]{1,0:T(8,128)(2,1)S(1)}, bf16[2048,256]{1,0:T(8,128)(2,1)S(1)}, u32[]{:S(2)}, u32[]{:S(2)}) collective-permute-start(bf16[2048,256]{1,0:T(8,128)(2,1)S(1)} %constant_dynamic-update-slice_fusion.5.refs_9_), channel_id=1, source_target_pairs={{0,3},{1,0},{2,1},{3,2},{4,7},{5,4},{6,5},{7,6},{8,11},{9,8},{10,9... | collective-permute-start | bytes 3145736 | tf_op jit(solution)/shard_map/ppermute | solution.py:30
  100.7 14.7 %collective-permute-start.9 = (bf16[1024,256]{1,0:T(8,128)(2,1)S(1)}, bf16[1024,256]{1,0:T(8,128)(2,1)}, u32[]{:S(2)}, u32[]{:S(2)}) collective-permute-start(bf16[1024,256]{1,0:T(8,128)(2,1)S(1)} %collective-permute-done.8.refs_8_), channel_id=1, source_target_pairs={{0,28},{1,29},{2,30},{3,31},{4,0},{5,1},{6,2},{7,3},{8,4},{9,5},{1... | collective-permute-start | bytes 1572872 | tf_op jit(solution)/shard_map/ppermute | solution.py:30
  102.8 0.8 copy-start.7
  103.6 14.7 %collective-permute-start.5 = (bf16[1024,256]{1,0:T(8,128)(2,1)S(1)}, bf16[1024,256]{1,0:T(8,128)(2,1)}, u32[]{:S(2)}, u32[]{:S(2)}) collective-permute-start(bf16[1024,256]{1,0:T(8,128)(2,1)S(1)} %collective-permute-done.4.refs_1_), channel_id=1, source_target_pairs={{0,4},{1,5},{2,6},{3,7},{4,8},{5,9},{6,10},{7,11},{8,12},{9,13},{1... | collective-permute-start | bytes 1572872 | tf_op jit(solution)/shard_map/ppermute | solution.py:29
  103.6 0.8 copy-start.9
  115.5 12.3 %collective-permute-start.10 = (bf16[1024,256]{1,0:T(8,128)(2,1)}, bf16[1024,256]{1,0:T(8,128)(2,1)}, u32[]{:S(2)}, u32[]{:S(2)}) collective-permute-start(bf16[1024,256]{1,0:T(8,128)(2,1)} %collective-permute-done.9.refs_7_), channel_id=1, source_target_pairs={{0,28},{1,29},{2,30},{3,31},{4,0},{5,1},{6,2},{7,3},{8,4},{9,5},{1... | collective-permute-start | bytes 1572872 | tf_op jit(solution)/shard_map/ppermute | solution.py:30
  118.4 14.1 %collective-permute-start.6 = (bf16[1024,256]{1,0:T(8,128)(2,1)}, bf16[1024,256]{1,0:T(8,128)(2,1)}, u32[]{:S(2)}, u32[]{:S(2)}) collective-permute-start(bf16[1024,256]{1,0:T(8,128)(2,1)} %collective-permute-done.5.refs_2_), channel_id=1, source_target_pairs={{0,4},{1,5},{2,6},{3,7},{4,8},{5,9},{6,10},{7,11},{8,12},{9,13},{1... | collective-permute-start | bytes 1572872 | tf_op jit(solution)/shard_map/ppermute | solution.py:29
  120.5 21.5 %collective-permute-start.21 = (bf16[1024,256]{1,0:T(8,128)(2,1)}, bf16[1024,256]{1,0:T(8,128)(2,1)}, u32[]{:S(2)}, u32[]{:S(2)}) collective-permute-start(bf16[1024,256]{1,0:T(8,128)(2,1)} %slice.55), channel_id=1, source_target_pairs={{0,1},{1,2},{2,3},{3,0},{4,5},{5,6},{6,7},{7,4},{8,9},{9,10},{10,1... | collective-permute-start | bytes 1572872 | tf_op jit(solution)/shard_map/ppermute | solution.py:34
  121.4 20.6 %collective-permute-start.23 = (bf16[1024,256]{1,0:T(8,128)(2,1)}, bf16[1024,256]{1,0:T(8,128)(2,1)}, u32[]{:S(2)}, u32[]{:S(2)}) collective-permute-start(bf16[1024,256]{1,0:T(8,128)(2,1)} %slice.56), channel_id=1, source_target_pairs={{0,3},{1,0},{2,1},{3,2},{4,7},{5,4},{6,5},{7,6},{8,11},{9,8},{10,9... | collective-permute-start | bytes 1572872 | tf_op jit(solution)/shard_map/ppermute | solution.py:35
  129.5 7.2 %collective-permute-start.11 = (bf16[512,256]{1,0:T(8,128)(2,1)}, bf16[512,256]{1,0:T(8,128)(2,1)S(1)}, u32[]{:S(2)}, u32[]{:S(2)}) collective-permute-start(bf16[512,256]{1,0:T(8,128)(2,1)} %slice.52), channel_id=1, source_target_pairs={{0,28},{1,29},{2,30},{3,31},{4,0},{5,1},{6,2},{7,3},{8,4},{9,5},{1... | collective-permute-start | bytes 786440 | tf_op jit(solution)/shard_map/ppermute | solution.py:35
  134.1 7.9 %collective-permute-start.7 = (bf16[512,256]{1,0:T(8,128)(2,1)}, bf16[512,256]{1,0:T(8,128)(2,1)}, u32[]{:S(2)}, u32[]{:S(2)}) collective-permute-start(bf16[512,256]{1,0:T(8,128)(2,1)} %slice.51), channel_id=1, source_target_pairs={{0,4},{1,5},{2,6},{3,7},{4,8},{5,9},{6,10},{7,11},{8,12},{9,13},{1... | collective-permute-start | bytes 786440 | tf_op jit(solution)/shard_map/ppermute | solution.py:34
  142.0 3.4 %copy-start = (bf16[256,64,256]{2,1,0:T(8,128)(2,1)S(1)}, bf16[256,64,256]{2,1,0:T(8,128)(2,1)}, u32[]{:S(2)}) copy-start(bf16[256,64,256]{2,1,0:T(8,128)(2,1)} %all-gather.7.cloned.1.call-done) | copy-start | bytes 25165828
  145.4 1.2 copy-start.4
  146.7 1.0 copy-start.6
  147.7 1.0 copy-start.8
  148.7 1.0 copy-start.10
Sparse Core Ops, SparseCore 0:
  9.2 29.3 all-gather.4
  58.3 46.4 all-gather.6

commit v2 on v1

v2 whole, which is shorter than its diff:
```python
import functools

import jax
import jax.numpy as jnp
from jax import lax
from jax.experimental import pallas as pl
from jax.experimental.pallas import tpu as pltpu
from jax.sharding import PartitionSpec as P

NX, NY, NZ = 4, 4, 8
ROWS_A = 256
LABEL_ROWS = 8


def ring_steps(axis, shift):
    if axis == "x":
        return [(2 * x + c, 2 * ((x + shift) % NX) + c) for x in range(NX) for c in range(2)]
    steps = []
    for z in range(NZ):
        for y in range(NY):
            to = ((z + shift) % NZ, y) if axis == "z" else (z, (y + shift) % NY)
            steps.append((z * NY + y, to[0] * NY + to[1]))
    return steps


def ring_gather(axis, piece):
    size = {"x": NX, "y": NY, "z": NZ}[axis]
    name = "pair" if axis == "x" else "tile"
    ahead, back = ring_steps(axis, 1), ring_steps(axis, -1)
    parts = {0: [piece]}
    left = right = piece
    for step in range(1, size // 2):
        left = lax.ppermute(left, name, ahead)
        right = lax.ppermute(right, name, back)
        parts[step], parts[size - step] = [left], [right]
    half = piece.shape[0] // 2
    parts[size // 2] = [
        lax.ppermute(left[:half], name, ahead),
        lax.ppermute(right[half:], name, back),
    ]
    return [parts[s] for s in range(size)]


def flat(parts):
    return [p for part in parts for p in part]


def other_core(piece):
    return lax.ppermute(piece, "pair", [(p, p ^ 1) for p in range(2 * NX)])


def route_kernel(rows_ref, cols_ref, share_ref, w_ref, o_ref, count):
    owners, height, width = o_ref.shape
    blocks, share, _ = w_ref.shape
    o_ref[...] = jnp.zeros_like(o_ref)
    for d in range(owners):
        count[d] = 0
    line = lax.broadcasted_iota(jnp.int32, (LABEL_ROWS, width), 0)
    for b in range(blocks):
        row = rows_ref[b]
        owner = row // 2
        rank = count[owner]
        count[owner] = rank + 1
        o_ref[owner, pl.ds(pl.multiple_of(rank * share, share), share), :] = w_ref[b]
        tags = o_ref[owner, 2 * share :, :].astype(jnp.float32)
        tags = jnp.where(line == 2 * rank, (row % 2 + 1).astype(jnp.float32), tags)
        tags = jnp.where(line == 2 * rank + 1, cols_ref[b].astype(jnp.float32), tags)
        o_ref[owner, 2 * share :, :] = tags.astype(jnp.bfloat16)


def route(block_rows, block_cols, share_id, integrals, owners, shares):
    blocks, height, width = integrals.shape
    share = height // shares
    return pl.pallas_call(
        route_kernel,
        grid_spec=pltpu.PrefetchScalarGridSpec(
            num_scalar_prefetch=3,
            grid=(1,),
            in_specs=[pl.BlockSpec((blocks, share, width), lambda i, r, c, s: (0, s[0], 0))],
            out_specs=pl.BlockSpec((owners, 2 * share + LABEL_ROWS, width), lambda i, r, c, s: (0, 0, 0)),
            scratch_shapes=[pltpu.SMEM((owners,), jnp.int32)],
        ),
        out_shape=jax.ShapeDtypeStruct((owners, 2 * share + LABEL_ROWS, width), jnp.bfloat16),
        compiler_params=pltpu.CompilerParams(vmem_limit_bytes=60 << 20),
    )(block_rows, block_cols, share_id, integrals)


def mirror_kernel(pair_ref, live_ref, mirror_ref, mine_ref, other_ref, a_ref, b_ref):
    rows, width = mine_ref.shape
    count = rows // NX
    live = lax.broadcasted_iota(jnp.int32, (1, width), 1) < live_ref[0]
    me = pair_ref[0]
    start = 0
    for out in (a_ref, b_ref):
        tall = out.shape[0]
        own = lax.broadcasted_iota(jnp.int32, (tall, count), 0) + (me * count + start)
        total = jnp.zeros((tall, width), jnp.float32)
        for core, ref in enumerate((mine_ref, other_ref)):
            for behind in range(NX):
                x = lax.rem(me // 2 + NX - behind, NX)
                source = 2 * x + lax.rem(me + core, 2)
                first = pl.multiple_of(source * count, count)
                here = lax.broadcasted_iota(jnp.int32, (tall, count), 1) + first
                pick = (mirror_ref[:, pl.ds(first, count)] == own) | (here == own)
                pick = jnp.where(pick, 1.0, 0.0).astype(jnp.bfloat16)
                total = total + jnp.dot(
                    pick,
                    ref[behind * count : (behind + 1) * count, :],
                    preferred_element_type=jnp.float32,
                )
        out[...] = jnp.where(live, total, 0.0).astype(jnp.bfloat16)
        start += tall


def mirror_sum(pair_id, live, mirror, mine, other, count):
    width = mine.shape[1]
    smem = pl.BlockSpec(memory_space=pltpu.SMEM)
    vmem = pl.BlockSpec(memory_space=pltpu.VMEM)
    return pl.pallas_call(
        mirror_kernel,
        in_specs=[smem, smem, vmem, vmem, vmem],
        out_specs=[vmem, vmem],
        out_shape=[
            jax.ShapeDtypeStruct((rows, width), jnp.bfloat16) for rows in (ROWS_A, count - ROWS_A)
        ],
        compiler_params=pltpu.CompilerParams(vmem_limit_bytes=24 << 20),
    )(pair_id, live, mirror.reshape(1, -1), mine, other)


def ladder_kernel(tags_ref, place_a, place_b, live_ref, pair_ref, *refs, n_a, n_b, n_w):
    pieces_a, pieces_b = refs[:n_a], refs[n_a : n_a + n_b]
    pieces_w = refs[n_a + n_b : n_a + n_b + n_w]
    o_ref, amps_a, amps_b, weights, total, sems = refs[n_a + n_b + n_w :]
    width = weights.shape[3]
    share = width // weights.shape[0]
    rows_a = amps_a.shape[0] // (NY * NZ)
    rows_b = amps_b.shape[0] // (NY * NZ)
    me = pair_ref[0]
    made = []

    def copy(source, target):
        made.append(pltpu.make_async_copy(source, target, sems.at[len(made)]))
        made[-1].start()

    for pieces, amps in ((pieces_a, amps_a), (pieces_b, amps_b)):
        at = 0
        for piece in pieces:
            copy(piece, amps.at[pl.ds(at, piece.shape[0]), :])
            at += piece.shape[0]
    at = 0
    for piece in pieces_w:
        behind, core = at // weights.shape[1] % NX, at // weights.shape[1] // NX
        source = 2 * lax.rem(me // 2 + NX - behind, NX) + lax.rem(me + core, 2)
        copy(piece, weights.at[source, pl.ds(at % weights.shape[1], piece.shape[0])])
        at += piece.shape[0]
    total[...] = jnp.zeros_like(total)
    for one in made:
        one.wait()

    @pl.loop(0, tags_ref.shape[0] // 2)
    def _(sender):
        for j in range(2):
            slot = sender * 2 + j
            tag = tags_ref[slot]

            @pl.when(tag > 0)
            def _(j=j, slot=slot, tag=tag):
                weight = weights[:, sender, j * share : (j + 1) * share, :].reshape(-1, width)
                row = tag - 1
                base = 0
                for place, amps, rows in ((place_a, amps_a, rows_a), (place_b, amps_b, rows_b)):
                    at = pl.multiple_of(place[slot] * rows, 16)
                    total[row, base : base + rows, :] += lax.dot_general(
                        amps[pl.ds(at, rows), :],
                        weight,
                        (((1,), (1,)), ((), ())),
                        preferred_element_type=jnp.float32,
                    )
                    base += rows

    position = lax.broadcasted_iota(jnp.int32, (1, width), 1)
    for r in range(2):
        kept = jnp.where(position < live_ref[r], total[r], 0.0)
        o_ref[:, r * width : (r + 1) * width] = kept.astype(jnp.bfloat16)


def ladder(tags, place_a, place_b, live, pair_id, pieces_a, pieces_b, pieces_w, count):
    senders, height, width = pieces_w[0].shape
    n_a, n_b, n_w = len(pieces_a), len(pieces_b), len(pieces_w)
    rows_a = sum(p.shape[0] for p in pieces_a)
    rows_b = sum(p.shape[0] for p in pieces_b)
    return pl.pallas_call(
        functools.partial(ladder_kernel, n_a=n_a, n_b=n_b, n_w=n_w),
        in_specs=[pl.BlockSpec(memory_space=pltpu.SMEM)] * 5
        + [pl.BlockSpec(memory_space=pl.ANY)] * (n_a + n_b + n_w),
        out_specs=pl.BlockSpec(memory_space=pltpu.VMEM),
        scratch_shapes=[
            pltpu.VMEM((rows_a, width), jnp.bfloat16),
            pltpu.VMEM((rows_b, width), jnp.bfloat16),
            pltpu.VMEM((2 * NX, senders, height, width), jnp.bfloat16),
            pltpu.VMEM((2, count, width), jnp.float32),
            pltpu.SemaphoreType.DMA((n_a + n_b + n_w,)),
        ],
        out_shape=jax.ShapeDtypeStruct((count, 2 * width), jnp.bfloat16),
        compiler_params=pltpu.CompilerParams(vmem_limit_bytes=60 << 20),
    )(tags, place_a, place_b, live, pair_id, *pieces_a, *pieces_b, *pieces_w)


def local(amplitudes, size_cd, integrals, block_rows, block_cols, size_ab, mirror):
    count, _, width = amplitudes.shape
    owners = lax.axis_size("tile")
    shares = lax.axis_size("pair")
    pair_id = lax.axis_index("pair").astype(jnp.int32)
    tile_id = lax.axis_index("tile").astype(jnp.int32)
    share = width // shares

    send = route(block_rows, block_cols, pair_id.reshape(1), integrals, owners, shares)
    got = lax.all_to_all(send, "tile", split_axis=0, concat_axis=0, tiled=True)

    mine = jnp.concatenate(flat(ring_gather("x", amplitudes.reshape(count, width))), axis=0)
    half_a, half_b = mirror_sum(pair_id.reshape(1), size_cd, mirror, mine, other_core(mine), count)
    bundle_a = jnp.concatenate(flat(ring_gather("y", half_a)), axis=0)
    bundle_b = jnp.concatenate(flat(ring_gather("z", half_b)), axis=0)
    pieces_a = flat(ring_gather("z", bundle_a))
    pieces_b = flat(ring_gather("y", bundle_b))

    shares_x = flat(ring_gather("x", got))
    pieces_w = shares_x + [other_core(p) for p in shares_x]
    labels = got[:, 2 * share : 2 * share + 4, 0].astype(jnp.int32)
    tags = labels[:, 0::2].reshape(-1)
    cols = labels[:, 1::2].reshape(-1)
    behind_z = (tile_id // NY - cols // NY) % NZ
    behind_y = (tile_id % NY - cols % NY) % NY
    result = ladder(
        tags,
        behind_z * NY + behind_y,
        behind_y * NZ + behind_z,
        size_ab,
        pair_id.reshape(1),
        pieces_a,
        pieces_b,
        pieces_w,
        count,
    )
    return result.reshape(count, 2, width)


def solution(mesh):
    in_specs = (
        P("pair", "tile", None),
        P("tile"),
        P("tile", None, None),
        P("tile"),
        P("tile"),
        P("tile"),
        P(),
    )
    out_specs = P("pair", "tile", None)
    return jax.shard_map(local, mesh=mesh, in_specs=in_specs, out_specs=out_specs, check_vma=False)
```

time: 170 us -> 193 us (1.14)
  the two profiles are of different devices: /device:TPU:2 before, /device:TPU:104 now
where the time goes in v2:
time: 193 us; the launch traced here: 194 us
  waiting for transfers between devices  79.7 us (41%)
  starting transfers between devices  60.1 us (31%)
  Pallas kernels  29.9 us (15%)
  local copies, waits for them, and re-layouts  21.4 us (11%)
    ppermute x10, waiting for transfers between devices, ring_gather(): right = lax.ppermute(right, name, back)  48 us
    pallas_call x1, Pallas kernels, ladder(): pl.pallas_call(functools.partial(ladder_kernel, n_a=n_a, n_b=n_b, n_w=n_w...  24.9 us
    ppermute x10, starting transfers between devices, ring_gather(): left = lax.ppermute(left, name, ahead)  22.9 us
    ppermute x6, waiting for transfers between devices, ring_gather(): lax.ppermute(left[:half], name, ahead)  12.3 us
    all_to_all x1, starting transfers between devices, local(): got = lax.all_to_all(send, 'tile', split_axis=0, concat_axis=0, tiled=True)  10.5 us
    ppermute x6, waiting for transfers between devices, ring_gather(): lax.ppermute(right[half:], name, back)  9.84 us
    ppermute x10, waiting for transfers between devices, ring_gather(): left = lax.ppermute(left, name, ahead)  9.66 us
    unnamed x46, local copies, waits for them, and re-layouts  9.41 us
  transfers between devices with their start and end apart: 39, of which 13 were waited for; matrix products, arithmetic and copies ran while one was open for 10% of the time, Pallas kernels for 3%

profile of v2, /device:TPU:104, one launch (start us, length us, event | category | flops | bytes accessed | tf_op | source)
XLA Modules:
  0.0 194.0 jit_solution(10113261170054368461)
XLA Ops:
  0.0 1.5 collective-permute-start
  1.5 1.7 collective-permute-start.2
  3.2 6.2 %collective-permute-done = bf16[512,256]{1,0:T(8,128)(2,1)S(1)} collective-permute-done((bf16[512,256]{1,0:T(8,128)(2,1)}, bf16[512,256]{1,0:T(8,128)(2,1)S(1)}, u32[]{:S(2)}, u32[]{:S(2)}) %collective-permute-start) | collective-permute-done | bytes 262176 | tf_op jit(solution)/shard_map/ppermute | solution.py:33
  9.8 1.0 constant_dynamic-update-slice_fusion.4
  10.8 3.0 %collective-permute-start.3 = (bf16[256,256]{1,0:T(8,128)(2,1)S(1)}, bf16[256,256]{1,0:T(8,128)(2,1)S(1)}, u32[]{:S(2)}, u32[]{:S(2)}) collective-permute-start(bf16[256,256]{1,0:T(8,128)(2,1)S(1)} %slice.62), channel_id=1, source_target_pairs={{0,192},{32,224},{64,0},{96,32},{128,64},{160,96},{192,128},{224,1... | collective-permute-start | bytes 393224 | tf_op jit(solution)/shard_map/ppermute | solution.py:39
  13.9 1.8 collective-permute-done.1
  16.5 3.2 %shard_map.73 = bf16[32,72,256]{2,1,0:T(8,128)(2,1)} custom-call(s32[32]{0:T(128)} %rows_ref.1, s32[32]{0:T(128)} %cols_ref.1, s32[1]{0:T(128)} %bitcast.share_ref.pair_ref, bf16[32,256,256]{2,1,0:T(8,128)(2,1)} %w_ref.1), custom_call_target="tpu_custom_call" | custom-call | tf_op jit(solution)/shard_map/pallas_call | solution.py:74
  19.7 10.5 %all-to-all-start = ((bf16[32,72,256]{2,1,0:T(8,128)(2,1)}), bf16[32,72,256]{2,1,0:T(8,128)(2,1)S(1)}, u32[]{:S(2)}, u32[]{:S(2)}) async-start(bf16[32,72,256]{2,1,0:T(8,128)(2,1)} %shard_map.73), calls=%async_computation | async-start | bytes 2359296 | tf_op jit(solution)/shard_map/all_to_all | solution.py:218
  30.9 1.8 shard_map.74
  33.3 1.5 collective-permute-start.5
  34.8 5.3 %collective-permute-done.7 = bf16[256,256]{1,0:T(8,128)(2,1)S(1)} collective-permute-done((bf16[256,256]{1,0:T(8,128)(2,1)S(1)}, bf16[256,256]{1,0:T(8,128)(2,1)S(1)}, u32[]{:S(2)}, u32[]{:S(2)}) %collective-permute-start.7) | collective-permute-done | bytes 131104 | tf_op jit(solution)/shard_map/ppermute | solution.py:34
  40.1 1.5 collective-permute-start.8
  41.6 1.7 collective-permute-start.6
  43.3 4.0 %collective-permute-done.6 = bf16[128,256]{1,0:T(8,128)(2,1)S(1)} collective-permute-done((bf16[128,256]{1,0:T(8,128)(2,1)S(1)}, bf16[128,256]{1,0:T(8,128)(2,1)S(1)}, u32[]{:S(2)}, u32[]{:S(2)}) %collective-permute-start.6) | collective-permute-done | bytes 65568 | tf_op jit(solution)/shard_map/ppermute | solution.py:38
  47.3 1.9 collective-permute-start.13
  49.2 2.4 %collective-permute-start.9 = (bf16[1024,256]{1,0:T(8,128)(2,1)S(1)}, bf16[1024,256]{1,0:T(8,128)(2,1)S(1)}, u32[]{:S(2)}, u32[]{:S(2)}) collective-permute-start(bf16[1024,256]{1,0:T(8,128)(2,1)S(1)} %constant_dynamic-update-slice_fusion.5.refs_0_), channel_id=1, source_target_pairs={{0,4},{1,5},{2,6},{3,7},{4,8},{5,9},{6,10},{7,11},{8,12},{9,13},{1... | collective-permute-start | bytes 1572872 | tf_op jit(solution)/shard_map/ppermute | solution.py:33
  51.6 3.2 %collective-permute-start.17 = (bf16[256,256]{1,0:T(8,128)(2,1)S(1)}, bf16[256,256]{1,0:T(8,128)(2,1)S(1)}, u32[]{:S(2)}, u32[]{:S(2)}) collective-permute-start(bf16[256,256]{1,0:T(8,128)(2,1)S(1)} %get-tuple-element.8), channel_id=1, source_target_pairs={{0,4},{1,5},{2,6},{3,7},{4,8},{5,9},{6,10},{7,11},{8,12},{9,13},{1... | collective-permute-start | bytes 393224 | tf_op jit(solution)/shard_map/ppermute | solution.py:33
  54.8 16.1 %collective-permute-done.13.refs_8_ = bf16[1024,256]{1,0:T(8,128)(2,1)S(1)} collective-permute-done((bf16[1024,256]{1,0:T(8,128)(2,1)S(1)}, bf16[1024,256]{1,0:T(8,128)(2,1)S(1)}, u32[]{:S(2)}, u32[]{:S(2)}) %collective-permute-start.13) | collective-permute-done | bytes 524320 | tf_op jit(solution)/shard_map/ppermute | solution.py:34
  70.9 3.2 %collective-permute-start.10 = (bf16[1024,256]{1,0:T(8,128)(2,1)S(1)}, bf16[1024,256]{1,0:T(8,128)(2,1)}, u32[]{:S(2)}, u32[]{:S(2)}) collective-permute-start(bf16[1024,256]{1,0:T(8,128)(2,1)S(1)} %collective-permute-done.9.refs_1_), channel_id=1, source_target_pairs={{0,4},{1,5},{2,6},{3,7},{4,8},{5,9},{6,10},{7,11},{8,12},{9,13},{1... | collective-permute-start | bytes 1572872 | tf_op jit(solution)/shard_map/ppermute | solution.py:33
  74.1 3.2 %collective-permute-start.18 = (bf16[256,256]{1,0:T(8,128)(2,1)S(1)}, bf16[256,256]{1,0:T(8,128)(2,1)S(1)}, u32[]{:S(2)}, u32[]{:S(2)}) collective-permute-start(bf16[256,256]{1,0:T(8,128)(2,1)S(1)} %collective-permute-done.17), channel_id=1, source_target_pairs={{0,4},{1,5},{2,6},{3,7},{4,8},{5,9},{6,10},{7,11},{8,12},{9,13},{1... | collective-permute-start | bytes 393224 | tf_op jit(solution)/shard_map/ppermute | solution.py:33
  78.0 9.6 %collective-permute-done.22 = bf16[256,256]{1,0:T(8,128)(2,1)S(1)} collective-permute-done((bf16[256,256]{1,0:T(8,128)(2,1)S(1)}, bf16[256,256]{1,0:T(8,128)(2,1)S(1)}, u32[]{:S(2)}, u32[]{:S(2)}) %collective-permute-start.22) | collective-permute-done | bytes 131104 | tf_op jit(solution)/shard_map/ppermute | solution.py:34
  87.6 3.2 %collective-permute-start.19 = (bf16[256,256]{1,0:T(8,128)(2,1)S(1)}, bf16[256,256]{1,0:T(8,128)(2,1)S(1)}, u32[]{:S(2)}, u32[]{:S(2)}) collective-permute-start(bf16[256,256]{1,0:T(8,128)(2,1)S(1)} %collective-permute-done.18), channel_id=1, source_target_pairs={{0,4},{1,5},{2,6},{3,7},{4,8},{5,9},{6,10},{7,11},{8,12},{9,13},{1... | collective-permute-start | bytes 393224 | tf_op jit(solution)/shard_map/ppermute | solution.py:33
  92.2 1.6 collective-permute-done.23
  93.9 3.3 %collective-permute-start.20 = (bf16[128,256]{1,0:T(8,128)(2,1)S(1)}, bf16[128,256]{1,0:T(8,128)(2,1)S(1)}, u32[]{:S(2)}, u32[]{:S(2)}) collective-permute-start(bf16[128,256]{1,0:T(8,128)(2,1)S(1)} %slice.67), channel_id=1, source_target_pairs={{0,4},{1,5},{2,6},{3,7},{4,8},{5,9},{6,10},{7,11},{8,12},{9,13},{1... | collective-permute-start | bytes 196616 | tf_op jit(solution)/shard_map/ppermute | solution.py:38
  97.9 3.2 %collective-permute-start.11 = (bf16[1024,256]{1,0:T(8,128)(2,1)}, bf16[1024,256]{1,0:T(8,128)(2,1)}, u32[]{:S(2)}, u32[]{:S(2)}) collective-permute-start(bf16[1024,256]{1,0:T(8,128)(2,1)} %collective-permute-done.10.refs_2_), channel_id=1, source_target_pairs={{0,4},{1,5},{2,6},{3,7},{4,8},{5,9},{6,10},{7,11},{8,12},{9,13},{1... | collective-permute-start | bytes 1572872 | tf_op jit(solution)/shard_map/ppermute | solution.py:33
  102.5 3.7 %collective-permute-start.31 = (bf16[32,72,256]{2,1,0:T(8,128)(2,1)S(1)}, bf16[32,72,256]{2,1,0:T(8,128)(2,1)S(1)}, u32[]{:S(2)}, u32[]{:S(2)}) collective-permute-start(bf16[32,72,256]{2,1,0:T(8,128)(2,1)S(1)} %all-to-all-done.refs_14_), channel_id=1, source_target_pairs={{0,192},{32,224},{64,0},{96,32},{128,64},{160,96},{192,128},{224,1... | collective-permute-start | bytes 3538952 | tf_op jit(solution)/shard_map/ppermute | solution.py:34
  106.1 1.6 constant_dynamic-update-slice_fusion.12
  107.7 1.6 constant_dynamic-update-slice_fusion.11
  109.3 1.6 constant_dynamic-update-slice_fusion.10.refs_9_
  111.4 1.5 collective-permute-start.25
  112.9 1.0 slice.66
  113.8 1.0 slice.65
  114.8 12.5 %collective-permute-done.31.refs_18_ = bf16[32,72,256]{2,1,0:T(8,128)(2,1)S(1)} collective-permute-done((bf16[32,72,256]{2,1,0:T(8,128)(2,1)S(1)}, bf16[32,72,256]{2,1,0:T(8,128)(2,1)S(1)}, u32[]{:S(2)}, u32[]{:S(2)}) %collective-permute-start.31) | collective-permute-done | bytes 1179680 | tf_op jit(solution)/shard_map/ppermute | solution.py:34
  127.3 3.4 %collective-permute-done.29.refs_15_ = bf16[32,72,256]{2,1,0:T(8,128)(2,1)S(1)} collective-permute-done((bf16[32,72,256]{2,1,0:T(8,128)(2,1)S(1)}, bf16[32,72,256]{2,1,0:T(8,128)(2,1)S(1)}, u32[]{:S(2)}, u32[]{:S(2)}) %collective-permute-start.29) | collective-permute-done | bytes 1179680 | tf_op jit(solution)/shard_map/ppermute | solution.py:33
  130.7 1.2 collective-permute-start.12
  132.0 0.9 slice.72
  132.8 0.9 slice.71
  133.8 2.9 %collective-permute-done.27.refs_13_ = bf16[2048,256]{1,0:T(8,128)(2,1)S(1)} collective-permute-done((bf16[2048,256]{1,0:T(8,128)(2,1)}, bf16[2048,256]{1,0:T(8,128)(2,1)S(1)}, u32[]{:S(2)}, u32[]{:S(2)}) %collective-permute-start.27) | collective-permute-done | bytes 1048608 | tf_op jit(solution)/shard_map/ppermute | solution.py:34
  136.6 3.2 %collective-permute-start.32 = (bf16[16,72,256]{2,1,0:T(8,128)(2,1)}, bf16[16,72,256]{2,1,0:T(8,128)(2,1)}, u32[]{:S(2)}, u32[]{:S(2)}) collective-permute-start(bf16[16,72,256]{2,1,0:T(8,128)(2,1)} %slice.72), channel_id=1, source_target_pairs={{0,192},{32,224},{64,0},{96,32},{128,64},{160,96},{192,128},{224,1... | collective-permute-start | bytes 1769480 | tf_op jit(solution)/shard_map/ppermute | solution.py:39
  139.9 0.9 slice.70
  140.8 1.1 collective-permute-start.28
  143.3 1.9 slice.69
  145.2 9.2 %collective-permute-done.28.refs_12_ = bf16[1024,256]{1,0:T(8,128)(2,1)} collective-permute-done((bf16[1024,256]{1,0:T(8,128)(2,1)}, bf16[1024,256]{1,0:T(8,128)(2,1)}, u32[]{:S(2)}, u32[]{:S(2)}) %collective-permute-start.28) | collective-permute-done | bytes 524320 | tf_op jit(solution)/shard_map/ppermute | solution.py:39
  154.4 2.0 %collective-permute-start.26 = (bf16[1024,256]{1,0:T(8,128)(2,1)}, bf16[1024,256]{1,0:T(8,128)(2,1)}, u32[]{:S(2)}, u32[]{:S(2)}) collective-permute-start(bf16[1024,256]{1,0:T(8,128)(2,1)} %slice.69), channel_id=1, source_target_pairs={{0,1},{1,2},{2,3},{3,0},{4,5},{5,6},{6,7},{7,4},{8,9},{9,10},{10,1... | collective-permute-start | bytes 1572872 | tf_op jit(solution)/shard_map/ppermute | solution.py:38
  157.5 0.9 copy.14
  160.6 6.4 %collective-permute-done.26.refs_11_ = bf16[1024,256]{1,0:T(8,128)(2,1)} collective-permute-done((bf16[1024,256]{1,0:T(8,128)(2,1)}, bf16[1024,256]{1,0:T(8,128)(2,1)}, u32[]{:S(2)}, u32[]{:S(2)}) %collective-permute-start.26) | collective-permute-done | bytes 524320 | tf_op jit(solution)/shard_map/ppermute | solution.py:38
  167.1 24.9 %shard_map.75 = bf16[512,512]{1,0:T(8,128)(2,1)} custom-call(s32[64]{0:T(128)} %reshape.23.tags_ref, s32[64]{0:T(128)} %multiply_add_fusion.1.place_a, s32[64]{0:T(128)} %get-tuple-element.9.place_b, s32[2]{0:T(128)} %live_ref.2, s32[1]{0:T(128)} %bitcast.share_ref.pair_ref, bf16[1024,256]{1,0:T(8,128)(2,1)} %copy-done.7, bf16[1024,256]{1,0:T(8,128)(2,1)} %copy-done.9, ...), custom_call_target="tpu_custom_call" | custom-call | tf_op jit(solution)/shard_map/pallas_call | solution.py:192
  192.0 2.0 %reshape.27 = bf16[512,2,256]{2,1,0:T(2,128)(2,1)} reshape(bf16[512,512]{1,0:T(8,128)(2,1)} %shard_map.75) | data formatting | bytes 1048576 | tf_op jit(solution)/shard_map/reshape | solution.py:245
  (105 shorter events, 11.2 us)
Async XLA Ops:
  0.0 9.5 %collective-permute-start = (bf16[512,256]{1,0:T(8,128)(2,1)}, bf16[512,256]{1,0:T(8,128)(2,1)S(1)}, u32[]{:S(2)}, u32[]{:S(2)}) collective-permute-start(bf16[512,256]{1,0:T(8,128)(2,1)} %bitcast.6), channel_id=1, source_target_pairs={{0,64},{32,96},{64,128},{96,160},{128,192},{160,224},{192,0},{224,... | collective-permute-start | bytes 786440 | tf_op jit(solution)/shard_map/ppermute | solution.py:33
  1.5 9.3 %collective-permute-start.2 = (bf16[512,256]{1,0:T(8,128)(2,1)}, bf16[512,256]{1,0:T(8,128)(2,1)S(1)}, u32[]{:S(2)}, u32[]{:S(2)}) collective-permute-start(bf16[512,256]{1,0:T(8,128)(2,1)} %bitcast.7), channel_id=1, source_target_pairs={{0,192},{32,224},{64,0},{96,32},{128,64},{160,96},{192,128},{224,1... | collective-permute-start | bytes 786440 | tf_op jit(solution)/shard_map/ppermute | solution.py:34
  9.5 6.3 %collective-permute-start.1 = (bf16[256,256]{1,0:T(8,128)(2,1)S(1)}, bf16[256,256]{1,0:T(8,128)(2,1)S(1)}, u32[]{:S(2)}, u32[]{:S(2)}) collective-permute-start(bf16[256,256]{1,0:T(8,128)(2,1)S(1)} %slice.61), channel_id=1, source_target_pairs={{0,64},{32,96},{64,128},{96,160},{128,192},{160,224},{192,0},{224,... | collective-permute-start | bytes 393224 | tf_op jit(solution)/shard_map/ppermute | solution.py:38
  10.8 5.6 %collective-permute-start.3 = (bf16[256,256]{1,0:T(8,128)(2,1)S(1)}, bf16[256,256]{1,0:T(8,128)(2,1)S(1)}, u32[]{:S(2)}, u32[]{:S(2)}) collective-permute-start(bf16[256,256]{1,0:T(8,128)(2,1)S(1)} %slice.62), channel_id=1, source_target_pairs={{0,192},{32,224},{64,0},{96,32},{128,64},{160,96},{192,128},{224,1... | collective-permute-start | bytes 393224 | tf_op jit(solution)/shard_map/ppermute | solution.py:39
  16.4 14.4 %collective-permute-start.4 = (bf16[2048,256]{1,0:T(8,128)(2,1)S(1)}, bf16[2048,256]{1,0:T(8,128)(2,1)S(1)}, u32[]{:S(2)}, u32[]{:S(2)}) collective-permute-start(bf16[2048,256]{1,0:T(8,128)(2,1)S(1)} %constant_dynamic-update-slice_fusion.mine_ref), channel_id=1, source_target_pairs={{0,32},{32,0},{64,96},{96,64},{128,160},{160,128},{192,224},{224,1... | collective-permute-start | bytes 3145736 | tf_op jit(solution)/shard_map/ppermute | solution.py:49
  19.7 11.1 %copy-start = (s32[4096]{0:T(1024)S(1)}, s32[4096]{0:T(1024)}, u32[]{:S(2)}) copy-start(s32[4096]{0:T(1024)} %param.13) | copy-start | bytes 49156
  19.7 82.7 %all-to-all-start = ((bf16[32,72,256]{2,1,0:T(8,128)(2,1)}), bf16[32,72,256]{2,1,0:T(8,128)(2,1)S(1)}, u32[]{:S(2)}, u32[]{:S(2)}) async-start(bf16[32,72,256]{2,1,0:T(8,128)(2,1)} %shard_map.73), calls=%async_computation | async-start | bytes 2359296 | tf_op jit(solution)/shard_map/all_to_all | solution.py:218
  32.7 7.4 %collective-permute-start.7 = (bf16[256,256]{1,0:T(8,128)(2,1)S(1)}, bf16[256,256]{1,0:T(8,128)(2,1)S(1)}, u32[]{:S(2)}, u32[]{:S(2)}) collective-permute-start(bf16[256,256]{1,0:T(8,128)(2,1)S(1)} %get-tuple-element.7), channel_id=1, source_target_pairs={{0,3},{1,0},{2,1},{3,2},{4,7},{5,4},{6,5},{7,6},{8,11},{9,8},{10,9... | collective-permute-start | bytes 393224 | tf_op jit(solution)/shard_map/ppermute | solution.py:34
  33.3 8.3 %collective-permute-start.5 = (bf16[256,256]{1,0:T(8,128)(2,1)S(1)}, bf16[256,256]{1,0:T(8,128)(2,1)S(1)}, u32[]{:S(2)}, u32[]{:S(2)}) collective-permute-start(bf16[256,256]{1,0:T(8,128)(2,1)S(1)} %get-tuple-element.7), channel_id=1, source_target_pairs={{0,1},{1,2},{2,3},{3,0},{4,5},{5,6},{6,7},{7,4},{8,9},{9,10},{10,1... | collective-permute-start | bytes 393224 | tf_op jit(solution)/shard_map/ppermute | solution.py:33
  40.1 7.2 %collective-permute-start.8 = (bf16[128,256]{1,0:T(8,128)(2,1)S(1)}, bf16[128,256]{1,0:T(8,128)(2,1)S(1)}, u32[]{:S(2)}, u32[]{:S(2)}) collective-permute-start(bf16[128,256]{1,0:T(8,128)(2,1)S(1)} %slice.64), channel_id=1, source_target_pairs={{0,3},{1,0},{2,1},{3,2},{4,7},{5,4},{6,5},{7,6},{8,11},{9,8},{10,9... | collective-permute-start | bytes 196616 | tf_op jit(solution)/shard_map/ppermute | solution.py:39
  41.6 5.7 %collective-permute-start.6 = (bf16[128,256]{1,0:T(8,128)(2,1)S(1)}, bf16[128,256]{1,0:T(8,128)(2,1)S(1)}, u32[]{:S(2)}, u32[]{:S(2)}) collective-permute-start(bf16[128,256]{1,0:T(8,128)(2,1)S(1)} %slice.63), channel_id=1, source_target_pairs={{0,1},{1,2},{2,3},{3,0},{4,5},{5,6},{6,7},{7,4},{8,9},{9,10},{10,1... | collective-permute-start | bytes 196616 | tf_op jit(solution)/shard_map/ppermute | solution.py:38
  47.3 54.5 %copy-start.7 = (bf16[1024,256]{1,0:T(8,128)(2,1)}, bf16[1024,256]{1,0:T(8,128)(2,1)S(1)}, u32[]{:S(2)}) copy-start(bf16[1024,256]{1,0:T(8,128)(2,1)S(1)} %constant_dynamic-update-slice_fusion.5.refs_0_) | copy-start | bytes 1572868
  47.3 23.6 %collective-permute-start.13 = (bf16[1024,256]{1,0:T(8,128)(2,1)S(1)}, bf16[1024,256]{1,0:T(8,128)(2,1)S(1)}, u32[]{:S(2)}, u32[]{:S(2)}) collective-permute-start(bf16[1024,256]{1,0:T(8,128)(2,1)S(1)} %constant_dynamic-update-slice_fusion.5.refs_0_), channel_id=1, source_target_pairs={{0,28},{1,29},{2,30},{3,31},{4,0},{5,1},{6,2},{7,3},{8,4},{9,5},{1... | collective-permute-start | bytes 1572872 | tf_op jit(solution)/shard_map/ppermute | solution.py:34
  49.2 21.7 %collective-permute-start.9 = (bf16[1024,256]{1,0:T(8,128)(2,1)S(1)}, bf16[1024,256]{1,0:T(8,128)(2,1)S(1)}, u32[]{:S(2)}, u32[]{:S(2)}) collective-permute-start(bf16[1024,256]{1,0:T(8,128)(2,1)S(1)} %constant_dynamic-update-slice_fusion.5.refs_0_), channel_id=1, source_target_pairs={{0,4},{1,5},{2,6},{3,7},{4,8},{5,9},{6,10},{7,11},{8,12},{9,13},{1... | collective-permute-start | bytes 1572872 | tf_op jit(solution)/shard_map/ppermute | solution.py:33
  51.6 22.6 %collective-permute-start.21 = (bf16[256,256]{1,0:T(8,128)(2,1)S(1)}, bf16[256,256]{1,0:T(8,128)(2,1)S(1)}, u32[]{:S(2)}, u32[]{:S(2)}) collective-permute-start(bf16[256,256]{1,0:T(8,128)(2,1)S(1)} %get-tuple-element.8), channel_id=1, source_target_pairs={{0,28},{1,29},{2,30},{3,31},{4,0},{5,1},{6,2},{7,3},{8,4},{9,5},{1... | collective-permute-start | bytes 393224 | tf_op jit(solution)/shard_map/ppermute | solution.py:34
  51.6 22.6 %collective-permute-start.17 = (bf16[256,256]{1,0:T(8,128)(2,1)S(1)}, bf16[256,256]{1,0:T(8,128)(2,1)S(1)}, u32[]{:S(2)}, u32[]{:S(2)}) collective-permute-start(bf16[256,256]{1,0:T(8,128)(2,1)S(1)} %get-tuple-element.8), channel_id=1, source_target_pairs={{0,4},{1,5},{2,6},{3,7},{4,8},{5,9},{6,10},{7,11},{8,12},{9,13},{1... | collective-permute-start | bytes 393224 | tf_op jit(solution)/shard_map/ppermute | solution.py:33
  70.9 30.9 %copy-start.8 = (bf16[1024,256]{1,0:T(8,128)(2,1)}, bf16[1024,256]{1,0:T(8,128)(2,1)S(1)}, u32[]{:S(2)}) copy-start(bf16[1024,256]{1,0:T(8,128)(2,1)S(1)} %collective-permute-done.13.refs_8_) | copy-start | bytes 1572868
  70.9 27.0 %collective-permute-start.14 = (bf16[1024,256]{1,0:T(8,128)(2,1)S(1)}, bf16[1024,256]{1,0:T(8,128)(2,1)}, u32[]{:S(2)}, u32[]{:S(2)}) collective-permute-start(bf16[1024,256]{1,0:T(8,128)(2,1)S(1)} %collective-permute-done.13.refs_8_), channel_id=1, source_target_pairs={{0,28},{1,29},{2,30},{3,31},{4,0},{5,1},{6,2},{7,3},{8,4},{9,5},{1... | collective-permute-start | bytes 1572872 | tf_op jit(solution)/shard_map/ppermute | solution.py:34
  70.9 30.9 %copy-start.9 = (bf16[1024,256]{1,0:T(8,128)(2,1)}, bf16[1024,256]{1,0:T(8,128)(2,1)S(1)}, u32[]{:S(2)}) copy-start(bf16[1024,256]{1,0:T(8,128)(2,1)S(1)} %collective-permute-done.9.refs_1_) | copy-start | bytes 1572868
  70.9 27.0 %collective-permute-start.10 = (bf16[1024,256]{1,0:T(8,128)(2,1)S(1)}, bf16[1024,256]{1,0:T(8,128)(2,1)}, u32[]{:S(2)}, u32[]{:S(2)}) collective-permute-start(bf16[1024,256]{1,0:T(8,128)(2,1)S(1)} %collective-permute-done.9.refs_1_), channel_id=1, source_target_pairs={{0,4},{1,5},{2,6},{3,7},{4,8},{5,9},{6,10},{7,11},{8,12},{9,13},{1... | collective-permute-start | bytes 1572872 | tf_op jit(solution)/shard_map/ppermute | solution.py:33
  74.1 13.5 %collective-permute-start.22 = (bf16[256,256]{1,0:T(8,128)(2,1)S(1)}, bf16[256,256]{1,0:T(8,128)(2,1)S(1)}, u32[]{:S(2)}, u32[]{:S(2)}) collective-permute-start(bf16[256,256]{1,0:T(8,128)(2,1)S(1)} %collective-permute-done.21), channel_id=1, source_target_pairs={{0,28},{1,29},{2,30},{3,31},{4,0},{5,1},{6,2},{7,3},{8,4},{9,5},{1... | collective-permute-start | bytes 393224 | tf_op jit(solution)/shard_map/ppermute | solution.py:34
  74.1 13.5 %collective-permute-start.18 = (bf16[256,256]{1,0:T(8,128)(2,1)S(1)}, bf16[256,256]{1,0:T(8,128)(2,1)S(1)}, u32[]{:S(2)}, u32[]{:S(2)}) collective-permute-start(bf16[256,256]{1,0:T(8,128)(2,1)S(1)} %collective-permute-done.17), channel_id=1, source_target_pairs={{0,4},{1,5},{2,6},{3,7},{4,8},{5,9},{6,10},{7,11},{8,12},{9,13},{1... | collective-permute-start | bytes 393224 | tf_op jit(solution)/shard_map/ppermute | solution.py:33
  87.6 14.2 %copy-start.14 = (bf16[256,256]{1,0:T(8,128)(2,1)}, bf16[256,256]{1,0:T(8,128)(2,1)S(1)}, u32[]{:S(2)}) copy-start(bf16[256,256]{1,0:T(8,128)(2,1)S(1)} %collective-permute-done.22) | copy-start | bytes 393220
  87.6 6.2 %collective-permute-start.23 = (bf16[256,256]{1,0:T(8,128)(2,1)S(1)}, bf16[256,256]{1,0:T(8,128)(2,1)S(1)}, u32[]{:S(2)}, u32[]{:S(2)}) collective-permute-start(bf16[256,256]{1,0:T(8,128)(2,1)S(1)} %collective-permute-done.22), channel_id=1, source_target_pairs={{0,28},{1,29},{2,30},{3,31},{4,0},{5,1},{6,2},{7,3},{8,4},{9,5},{1... | collective-permute-start | bytes 393224 | tf_op jit(solution)/shard_map/ppermute | solution.py:34
  87.6 6.3 %collective-permute-start.19 = (bf16[256,256]{1,0:T(8,128)(2,1)S(1)}, bf16[256,256]{1,0:T(8,128)(2,1)S(1)}, u32[]{:S(2)}, u32[]{:S(2)}) collective-permute-start(bf16[256,256]{1,0:T(8,128)(2,1)S(1)} %collective-permute-done.18), channel_id=1, source_target_pairs={{0,4},{1,5},{2,6},{3,7},{4,8},{5,9},{6,10},{7,11},{8,12},{9,13},{1... | collective-permute-start | bytes 393224 | tf_op jit(solution)/shard_map/ppermute | solution.py:33
  93.8 8.0 %copy-start.10 = (bf16[256,256]{1,0:T(8,128)(2,1)}, bf16[256,256]{1,0:T(8,128)(2,1)S(1)}, u32[]{:S(2)}) copy-start(bf16[256,256]{1,0:T(8,128)(2,1)S(1)} %collective-permute-done.23) | copy-start | bytes 393220
  93.8 8.0 %collective-permute-start.24 = (bf16[128,256]{1,0:T(8,128)(2,1)S(1)}, bf16[128,256]{1,0:T(8,128)(2,1)S(1)}, u32[]{:S(2)}, u32[]{:S(2)}) collective-permute-start(bf16[128,256]{1,0:T(8,128)(2,1)S(1)} %slice.68), channel_id=1, source_target_pairs={{0,28},{1,29},{2,30},{3,31},{4,0},{5,1},{6,2},{7,3},{8,4},{9,5},{1... | collective-permute-start | bytes 196616 | tf_op jit(solution)/shard_map/ppermute | solution.py:39
  93.9 7.2 %collective-permute-start.20 = (bf16[128,256]{1,0:T(8,128)(2,1)S(1)}, bf16[128,256]{1,0:T(8,128)(2,1)S(1)}, u32[]{:S(2)}, u32[]{:S(2)}) collective-permute-start(bf16[128,256]{1,0:T(8,128)(2,1)S(1)} %slice.67), channel_id=1, source_target_pairs={{0,4},{1,5},{2,6},{3,7},{4,8},{5,9},{6,10},{7,11},{8,12},{9,13},{1... | collective-permute-start | bytes 196616 | tf_op jit(solution)/shard_map/ppermute | solution.py:38
  97.9 12.9 %collective-permute-start.15 = (bf16[1024,256]{1,0:T(8,128)(2,1)}, bf16[1024,256]{1,0:T(8,128)(2,1)}, u32[]{:S(2)}, u32[]{:S(2)}) collective-permute-start(bf16[1024,256]{1,0:T(8,128)(2,1)} %collective-permute-done.14.refs_7_), channel_id=1, source_target_pairs={{0,28},{1,29},{2,30},{3,31},{4,0},{5,1},{6,2},{7,3},{8,4},{9,5},{1... | collective-permute-start | bytes 1572872 | tf_op jit(solution)/shard_map/ppermute | solution.py:34
  97.9 13.5 %collective-permute-start.11 = (bf16[1024,256]{1,0:T(8,128)(2,1)}, bf16[1024,256]{1,0:T(8,128)(2,1)}, u32[]{:S(2)}, u32[]{:S(2)}) collective-permute-start(bf16[1024,256]{1,0:T(8,128)(2,1)} %collective-permute-done.10.refs_2_), channel_id=1, source_target_pairs={{0,4},{1,5},{2,6},{3,7},{4,8},{5,9},{6,10},{7,11},{8,12},{9,13},{1... | collective-permute-start | bytes 1572872 | tf_op jit(solution)/shard_map/ppermute | solution.py:33
  102.5 54.4 %copy-start.1 = (bf16[32,72,256]{2,1,0:T(8,128)(2,1)}, bf16[32,72,256]{2,1,0:T(8,128)(2,1)S(1)}, u32[]{:S(2)}) copy-start(bf16[32,72,256]{2,1,0:T(8,128)(2,1)S(1)} %all-to-all-done.refs_14_) | copy-start | bytes 3538948
  102.5 24.8 %collective-permute-start.31 = (bf16[32,72,256]{2,1,0:T(8,128)(2,1)S(1)}, bf16[32,72,256]{2,1,0:T(8,128)(2,1)S(1)}, u32[]{:S(2)}, u32[]{:S(2)}) collective-permute-start(bf16[32,72,256]{2,1,0:T(8,128)(2,1)S(1)} %all-to-all-done.refs_14_), channel_id=1, source_target_pairs={{0,192},{32,224},{64,0},{96,32},{128,64},{160,96},{192,128},{224,1... | collective-permute-start | bytes 3538952 | tf_op jit(solution)/shard_map/ppermute | solution.py:34
  106.1 24.6 %collective-permute-start.29 = (bf16[32,72,256]{2,1,0:T(8,128)(2,1)S(1)}, bf16[32,72,256]{2,1,0:T(8,128)(2,1)S(1)}, u32[]{:S(2)}, u32[]{:S(2)}) collective-permute-start(bf16[32,72,256]{2,1,0:T(8,128)(2,1)S(1)} %all-to-all-done.refs_14_), channel_id=1, source_target_pairs={{0,64},{32,96},{64,128},{96,160},{128,192},{160,224},{192,0},{224,... | collective-permute-start | bytes 3538952 | tf_op jit(solution)/shard_map/ppermute | solution.py:33
  109.3 31.5 %collective-permute-start.33 = (bf16[32,72,256]{2,1,0:T(8,128)(2,1)S(1)}, bf16[32,72,256]{2,1,0:T(8,128)(2,1)S(1)}, u32[]{:S(2)}, u32[]{:S(2)}) collective-permute-start(bf16[32,72,256]{2,1,0:T(8,128)(2,1)S(1)} %all-to-all-done.refs_14_), channel_id=1, source_target_pairs={{0,32},{32,0},{64,96},{96,64},{128,160},{160,128},{192,224},{224,1... | collective-permute-start | bytes 3538952 | tf_op jit(solution)/shard_map/ppermute | solution.py:49
  110.8 25.8 %collective-permute-start.27 = (bf16[2048,256]{1,0:T(8,128)(2,1)}, bf16[2048,256]{1,0:T(8,128)(2,1)S(1)}, u32[]{:S(2)}, u32[]{:S(2)}) collective-permute-start(bf16[2048,256]{1,0:T(8,128)(2,1)} %constant_dynamic-update-slice_fusion.10.refs_9_), channel_id=1, source_target_pairs={{0,3},{1,0},{2,1},{3,2},{4,7},{5,4},{6,5},{7,6},{8,11},{9,8},{10,9... | collective-permute-start | bytes 3145736 | tf_op jit(solution)/shard_map/ppermute | solution.py:34
  111.4 28.5 %collective-permute-start.25 = (bf16[2048,256]{1,0:T(8,128)(2,1)}, bf16[2048,256]{1,0:T(8,128)(2,1)S(1)}, u32[]{:S(2)}, u32[]{:S(2)}) collective-permute-start(bf16[2048,256]{1,0:T(8,128)(2,1)} %constant_dynamic-update-slice_fusion.10.refs_9_), channel_id=1, source_target_pairs={{0,1},{1,2},{2,3},{3,0},{4,5},{5,6},{6,7},{7,4},{8,9},{9,10},{10,1... | collective-permute-start | bytes 3145736 | tf_op jit(solution)/shard_map/ppermute | solution.py:33
  127.3 14.6 %copy-start.2 = (bf16[32,72,256]{2,1,0:T(8,128)(2,1)}, bf16[32,72,256]{2,1,0:T(8,128)(2,1)S(1)}, u32[]{:S(2)}) copy-start(bf16[32,72,256]{2,1,0:T(8,128)(2,1)S(1)} %collective-permute-done.31.refs_18_) | copy-start | bytes 3538948
  127.3 14.6 %collective-permute-start.16 = (bf16[512,256]{1,0:T(8,128)(2,1)S(1)}, bf16[512,256]{1,0:T(8,128)(2,1)S(1)}, u32[]{:S(2)}, u32[]{:S(2)}) collective-permute-start(bf16[512,256]{1,0:T(8,128)(2,1)S(1)} %slice.66), channel_id=1, source_target_pairs={{0,28},{1,29},{2,30},{3,31},{4,0},{5,1},{6,2},{7,3},{8,4},{9,5},{1... | collective-permute-start | bytes 786440 | tf_op jit(solution)/shard_map/ppermute | solution.py:39
  130.7 11.3 %copy-start.3 = (bf16[32,72,256]{2,1,0:T(8,128)(2,1)}, bf16[32,72,256]{2,1,0:T(8,128)(2,1)S(1)}, u32[]{:S(2)}) copy-start(bf16[32,72,256]{2,1,0:T(8,128)(2,1)S(1)} %collective-permute-done.29.refs_15_) | copy-start | bytes 3538948
  130.7 11.3 %collective-permute-start.12 = (bf16[512,256]{1,0:T(8,128)(2,1)S(1)}, bf16[512,256]{1,0:T(8,128)(2,1)S(1)}, u32[]{:S(2)}, u32[]{:S(2)}) collective-permute-start(bf16[512,256]{1,0:T(8,128)(2,1)S(1)} %slice.65), channel_id=1, source_target_pairs={{0,4},{1,5},{2,6},{3,7},{4,8},{5,9},{6,10},{7,11},{8,12},{9,13},{1... | collective-permute-start | bytes 786440 | tf_op jit(solution)/shard_map/ppermute | solution.py:38
  136.6 19.7 %collective-permute-start.32 = (bf16[16,72,256]{2,1,0:T(8,128)(2,1)}, bf16[16,72,256]{2,1,0:T(8,128)(2,1)}, u32[]{:S(2)}, u32[]{:S(2)}) collective-permute-start(bf16[16,72,256]{2,1,0:T(8,128)(2,1)} %slice.72), channel_id=1, source_target_pairs={{0,192},{32,224},{64,0},{96,32},{128,64},{160,96},{192,128},{224,1... | collective-permute-start | bytes 1769480 | tf_op jit(solution)/shard_map/ppermute | solution.py:39
  139.9 16.5 %collective-permute-start.30 = (bf16[16,72,256]{2,1,0:T(8,128)(2,1)}, bf16[16,72,256]{2,1,0:T(8,128)(2,1)}, u32[]{:S(2)}, u32[]{:S(2)}) collective-permute-start(bf16[16,72,256]{2,1,0:T(8,128)(2,1)} %slice.71), channel_id=1, source_target_pairs={{0,64},{32,96},{64,128},{96,160},{128,192},{160,224},{192,0},{224,... | collective-permute-start | bytes 1769480 | tf_op jit(solution)/shard_map/ppermute | solution.py:38
  140.8 13.6 %collective-permute-start.28 = (bf16[1024,256]{1,0:T(8,128)(2,1)}, bf16[1024,256]{1,0:T(8,128)(2,1)}, u32[]{:S(2)}, u32[]{:S(2)}) collective-permute-start(bf16[1024,256]{1,0:T(8,128)(2,1)} %slice.70), channel_id=1, source_target_pairs={{0,3},{1,0},{2,1},{3,2},{4,7},{5,4},{6,5},{7,6},{8,11},{9,8},{10,9... | collective-permute-start | bytes 1572872 | tf_op jit(solution)/shard_map/ppermute | solution.py:39
  141.9 25.1 %collective-permute-start.37 = (bf16[32,72,256]{2,1,0:T(8,128)(2,1)S(1)}, bf16[32,72,256]{2,1,0:T(8,128)(2,1)}, u32[]{:S(2)}, u32[]{:S(2)}) collective-permute-start(bf16[32,72,256]{2,1,0:T(8,128)(2,1)S(1)} %collective-permute-done.31.refs_18_), channel_id=1, source_target_pairs={{0,32},{32,0},{64,96},{96,64},{128,160},{160,128},{192,224},{224,1... | collective-permute-start | bytes 3538952 | tf_op jit(solution)/shard_map/ppermute | solution.py:49
  143.3 23.8 %collective-permute-start.34 = (bf16[32,72,256]{2,1,0:T(8,128)(2,1)S(1)}, bf16[32,72,256]{2,1,0:T(8,128)(2,1)}, u32[]{:S(2)}, u32[]{:S(2)}) collective-permute-start(bf16[32,72,256]{2,1,0:T(8,128)(2,1)S(1)} %collective-permute-done.29.refs_15_), channel_id=1, source_target_pairs={{0,32},{32,0},{64,96},{96,64},{128,160},{160,128},{192,224},{224,1... | collective-permute-start | bytes 3538952 | tf_op jit(solution)/shard_map/ppermute | solution.py:49
  154.4 12.7 %collective-permute-start.26 = (bf16[1024,256]{1,0:T(8,128)(2,1)}, bf16[1024,256]{1,0:T(8,128)(2,1)}, u32[]{:S(2)}, u32[]{:S(2)}) collective-permute-start(bf16[1024,256]{1,0:T(8,128)(2,1)} %slice.69), channel_id=1, source_target_pairs={{0,1},{1,2},{2,3},{3,0},{4,5},{5,6},{6,7},{7,4},{8,9},{9,10},{10,1... | collective-permute-start | bytes 1572872 | tf_op jit(solution)/shard_map/ppermute | solution.py:38
  156.3 10.7 %collective-permute-start.36 = (bf16[16,72,256]{2,1,0:T(8,128)(2,1)}, bf16[16,72,256]{2,1,0:T(8,128)(2,1)}, u32[]{:S(2)}, u32[]{:S(2)}) collective-permute-start(bf16[16,72,256]{2,1,0:T(8,128)(2,1)} %collective-permute-done.32.refs_17_), channel_id=1, source_target_pairs={{0,32},{32,0},{64,96},{96,64},{128,160},{160,128},{192,224},{224,1... | collective-permute-start | bytes 1769480 | tf_op jit(solution)/shard_map/ppermute | solution.py:49
  156.4 10.7 %collective-permute-start.35 = (bf16[16,72,256]{2,1,0:T(8,128)(2,1)}, bf16[16,72,256]{2,1,0:T(8,128)(2,1)}, u32[]{:S(2)}, u32[]{:S(2)}) collective-permute-start(bf16[16,72,256]{2,1,0:T(8,128)(2,1)} %collective-permute-done.30.refs_16_), channel_id=1, source_target_pairs={{0,32},{32,0},{64,96},{96,64},{128,160},{160,128},{192,224},{224,1... | collective-permute-start | bytes 1769480 | tf_op jit(solution)/shard_map/ppermute | solution.py:49
  (6 other events, 14.1 us)

commit v3 on v2

v3 whole, which is shorter than its diff:
```python
import functools

import jax
import jax.numpy as jnp
from jax import lax
from jax.experimental import pallas as pl
from jax.experimental.pallas import tpu as pltpu
from jax.sharding import PartitionSpec as P

NX, NY, NZ = 4, 4, 8
ROWS_A = 256
LABEL_ROWS = 8


def ring_steps(axis, shift):
    if axis == "x":
        return [(2 * x + c, 2 * ((x + shift) % NX) + c) for x in range(NX) for c in range(2)]
    steps = []
    for z in range(NZ):
        for y in range(NY):
            to = ((z + shift) % NZ, y) if axis == "z" else (z, (y + shift) % NY)
            steps.append((z * NY + y, to[0] * NY + to[1]))
    return steps


def send(axis, shift, piece):
    return lax.ppermute(piece, "pair" if axis == "x" else "tile", ring_steps(axis, shift))


def after(piece, *others):
    return lax.optimization_barrier((piece, *others))[0]


def other_core(piece):
    return lax.ppermute(piece, "pair", [(p, p ^ 1) for p in range(2 * NX)])


def route_kernel(rows_ref, cols_ref, share_ref, w_ref, o_ref, count):
    owners, height, width = o_ref.shape
    blocks, share, _ = w_ref.shape
    o_ref[...] = jnp.zeros_like(o_ref)
    for d in range(owners):
        count[d] = 0
    line = lax.broadcasted_iota(jnp.int32, (LABEL_ROWS, width), 0)
    for b in range(blocks):
        row = rows_ref[b]
        owner = row // 2
        rank = count[owner]
        count[owner] = rank + 1
        o_ref[owner, pl.ds(pl.multiple_of(rank * share, share), share), :] = w_ref[b]
        tags = o_ref[owner, 2 * share :, :].astype(jnp.float32)
        tags = jnp.where(line == 2 * rank, (row % 2 + 1).astype(jnp.float32), tags)
        tags = jnp.where(line == 2 * rank + 1, cols_ref[b].astype(jnp.float32), tags)
        o_ref[owner, 2 * share :, :] = tags.astype(jnp.bfloat16)


def route(block_rows, block_cols, share_id, integrals, owners, shares):
    blocks, height, width = integrals.shape
    share = height // shares
    return pl.pallas_call(
        route_kernel,
        grid_spec=pltpu.PrefetchScalarGridSpec(
            num_scalar_prefetch=3,
            grid=(1,),
            in_specs=[pl.BlockSpec((blocks, share, width), lambda i, r, c, s: (0, s[0], 0))],
            out_specs=pl.BlockSpec((owners, 2 * share + LABEL_ROWS, width), lambda i, r, c, s: (0, 0, 0)),
            scratch_shapes=[pltpu.SMEM((owners,), jnp.int32)],
        ),
        out_shape=jax.ShapeDtypeStruct((owners, 2 * share + LABEL_ROWS, width), jnp.bfloat16),
        compiler_params=pltpu.CompilerParams(vmem_limit_bytes=60 << 20),
    )(block_rows, block_cols, share_id, integrals)


def mirror_kernel(pair_ref, live_ref, mirror_ref, *refs):
    pieces, a_ref, b_ref = refs[:-2], refs[-2], refs[-1]
    count, width = pieces[0].shape
    live = lax.broadcasted_iota(jnp.int32, (1, width), 1) < live_ref[0]
    me = pair_ref[0]
    start = 0
    for out in (a_ref, b_ref):
        tall = out.shape[0]
        own = lax.broadcasted_iota(jnp.int32, (tall, 1), 0) + (me * count + start)
        total = jnp.zeros((tall, width), jnp.float32)
        at = 0
        for ref in pieces:
            height = ref.shape[0]
            behind, core, skip = at // count % NX, at // count // NX, at % count
            source = 2 * lax.rem(me // 2 + NX - behind, NX) + lax.rem(me + core, 2)
            first = pl.multiple_of(source * count + skip, height)
            here = lax.broadcasted_iota(jnp.int32, (tall, height), 1) + first
            pick = (mirror_ref[:, pl.ds(first, height)] == own) | (here == own)
            pick = jnp.where(pick, 1.0, 0.0).astype(jnp.bfloat16)
            total = total + jnp.dot(pick, ref[...], preferred_element_type=jnp.float32)
            at += height
        out[...] = jnp.where(live, total, 0.0).astype(jnp.bfloat16)
        start += tall


def mirror_sum(pair_id, live, mirror, pieces):
    count, width = pieces[0].shape
    smem = pl.BlockSpec(memory_space=pltpu.SMEM)
    vmem = pl.BlockSpec(memory_space=pltpu.VMEM)
    return pl.pallas_call(
        mirror_kernel,
        in_specs=[smem, smem] + [vmem] * (1 + len(pieces)),
        out_specs=[vmem, vmem],
        out_shape=[
            jax.ShapeDtypeStruct((rows, width), jnp.bfloat16) for rows in (ROWS_A, count - ROWS_A)
        ],
        compiler_params=pltpu.CompilerParams(vmem_limit_bytes=24 << 20),
    )(pair_id, live, mirror.reshape(1, -1), *pieces)


def ladder_kernel(tags_ref, place_ref, live_ref, pair_ref, *refs, n_amps):
    pieces, pieces_w = refs[:n_amps], refs[n_amps:-5]
    o_ref, amps, weights, total, sems = refs[-5:]
    senders, width = weights.shape[1], weights.shape[3]
    share = width // weights.shape[0]
    rows = amps.shape[0] // (NY * NZ)
    me = pair_ref[0]
    made = []

    def copy(source, target):
        made.append(pltpu.make_async_copy(source, target, sems.at[len(made)]))
        made[-1].start()

    at = 0
    for piece in pieces:
        copy(piece, amps.at[pl.ds(at, piece.shape[0]), :])
        at += piece.shape[0]
    at = 0
    for piece in pieces_w:
        behind, core = at // senders % NX, at // senders // NX
        source = 2 * lax.rem(me // 2 + NX - behind, NX) + lax.rem(me + core, 2)
        copy(piece, weights.at[source, pl.ds(at % senders, piece.shape[0])])
        at += piece.shape[0]
    total[...] = jnp.zeros_like(total)
    for one in made:
        one.wait()

    @pl.loop(0, senders)
    def _(sender):
        for j in range(2):
            slot = sender * 2 + j
            tag = tags_ref[slot]

            @pl.when(tag > 0)
            def _(j=j, slot=slot, tag=tag):
                weight = weights[:, sender, j * share : (j + 1) * share, :].reshape(-1, width)
                at = pl.multiple_of(place_ref[slot] * rows, 16)
                total[tag - 1] += lax.dot_general(
                    amps[pl.ds(at, rows), :],
                    weight,
                    (((1,), (1,)), ((), ())),
                    preferred_element_type=jnp.float32,
                )

    position = lax.broadcasted_iota(jnp.int32, (1, width), 1)
    for r in range(2):
        kept = jnp.where(position < live_ref[r], total[r], 0.0)
        o_ref[:, r * width : (r + 1) * width] = kept.astype(jnp.bfloat16)


def ladder(tags, place, live, pair_id, pieces, pieces_w):
    senders, height, width = pieces_w[0].shape
    n_amps, n_w = len(pieces), len(pieces_w)
    all_rows = sum(p.shape[0] for p in pieces)
    rows = all_rows // (NY * NZ)
    return pl.pallas_call(
        functools.partial(ladder_kernel, n_amps=n_amps),
        in_specs=[pl.BlockSpec(memory_space=pltpu.SMEM)] * 4
        + [pl.BlockSpec(memory_space=pl.ANY)] * (n_amps + n_w),
        out_specs=pl.BlockSpec(memory_space=pltpu.VMEM),
        scratch_shapes=[
            pltpu.VMEM((all_rows, width), jnp.bfloat16),
            pltpu.VMEM((2 * NX, senders, height, width), jnp.bfloat16),
            pltpu.VMEM((2, rows, width), jnp.float32),
            pltpu.SemaphoreType.DMA((n_amps + n_w,)),
        ],
        out_shape=jax.ShapeDtypeStruct((rows, 2 * width), jnp.bfloat16),
        compiler_params=pltpu.CompilerParams(vmem_limit_bytes=60 << 20),
    )(tags, place, live, pair_id, *pieces, *pieces_w)


def local(amplitudes, size_cd, integrals, block_rows, block_cols, size_ab, mirror):
    count, _, width = amplitudes.shape
    owners = lax.axis_size("tile")
    shares = lax.axis_size("pair")
    pair_id = lax.axis_index("pair").astype(jnp.int32)
    tile_id = lax.axis_index("tile").astype(jnp.int32)
    share = width // shares

    raw = amplitudes.reshape(count, width)
    half = count // 2
    pieces = [
        raw,
        send("x", 1, raw),
        send("x", 2, raw[:half]),
        send("x", -2, raw[half:]),
        send("x", -1, raw),
    ]

    routed = route(block_rows, block_cols, pair_id.reshape(1), integrals, owners, shares)
    got = lax.all_to_all(routed, "tile", split_axis=0, concat_axis=0, tiled=True)

    pieces += [other_core(p) for p in pieces]
    a, b = mirror_sum(pair_id.reshape(1), size_cd, mirror, pieces)

    half = a.shape[0] // 2
    b1, b7 = send("z", 1, b), send("z", -1, b)
    ay = [a, send("y", 1, a), send("y", 2, a[:half]), send("y", -2, a[half:]), send("y", -1, a)]
    a0 = jnp.concatenate(ay, axis=0)
    b2, b6 = send("z", 1, b1), send("z", -1, b7)
    a0 = after(a0, b1, b7)
    a1, a7 = send("z", 1, a0), send("z", -1, a0)
    b3, b5 = send("z", 1, b2), send("z", -1, b6)
    half = b.shape[0] // 2
    b4 = [send("z", 1, b3[:half]), send("z", -1, b5[half:])]
    a1, a7 = after(a1, b3, b5), after(a7, b3, b5)
    a2, a6 = send("z", 1, a1), send("z", -1, a7)
    b0 = jnp.concatenate([b, b1, b2, b3, *b4, b5, b6, b7], axis=0)
    by1, by3 = send("y", 1, b0), send("y", -1, b0)
    a2, a6 = after(a2, *b4), after(a6, *b4)
    a3, a5 = send("z", 1, a2), send("z", -1, a6)
    half = a0.shape[0] // 2
    a4 = [send("z", 1, a3[:half]), send("z", -1, a5[half:])]
    half = b0.shape[0] // 2
    by2 = [send("y", 1, by1[:half]), send("y", -1, by3[half:])]
    pieces_a = [a0, a1, a2, a3, *a4, a5, a6, a7]
    pieces_b = [b0, by1, *by2, by3]

    w1, w3 = send("x", 1, got), send("x", -1, got)
    half = got.shape[0] // 2
    w2 = [send("x", 1, w1[:half]), send("x", -1, w3[half:])]
    pieces_w = [got, w1, *w2, w3]
    pieces_w += [other_core(p) for p in pieces_w]
    labels = got[:, 2 * share : 2 * share + 4, 0].astype(jnp.int32)
    tags = labels[:, 0::2].reshape(-1)
    cols = labels[:, 1::2].reshape(-1)
    behind_z = (tile_id // NY - cols // NY) % NZ
    behind_y = (tile_id % NY - cols % NY) % NY
    above = ladder(tags, behind_z * NY + behind_y, size_ab, pair_id.reshape(1), pieces_a, pieces_w)
    below = ladder(tags, behind_y * NZ + behind_z, size_ab, pair_id.reshape(1), pieces_b, pieces_w)
    return jnp.concatenate([above, below], axis=0).reshape(count, 2, width)


def solution(mesh):
    in_specs = (
        P("pair", "tile", None),
        P("tile"),
        P("tile", None, None),
        P("tile"),
        P("tile"),
        P("tile"),
        P(),
    )
    out_specs = P("pair", "tile", None)
    return jax.shard_map(local, mesh=mesh, in_specs=in_specs, out_specs=out_specs, check_vma=False)
```

time: 193 us -> 183 us (0.948)
  the two profiles are of different devices: /device:TPU:104 before, /device:TPU:24 now
where the time goes in v3:
time: 183 us; the launch traced here: 184 us
  starting transfers between devices  59.3 us (32%)
  waiting for transfers between devices  57.2 us (31%)
  Pallas kernels  47.2 us (26%)
  local copies, waits for them, and re-layouts  15.5 us (8%)
  other arithmetic  3.37 us (2%)
    ppermute x32, waiting for transfers between devices, send(): lax.ppermute(piece, 'pair' if axis == 'x' else 'tile', ring_steps(axis, s...  56.5 us
    ppermute x32, starting transfers between devices, send(): lax.ppermute(piece, 'pair' if axis == 'x' else 'tile', ring_steps(axis, s...  46.9 us
    pallas_call x2, Pallas kernels, ladder(): pl.pallas_call(functools.partial(ladder_kernel, n_amps=n_amps), in_specs=...  42.2 us
    all_to_all x1, starting transfers between devices, local(): lax.all_to_all(routed, 'tile', split_axis=0, concat_axis=0, tiled=True)  11.6 us
    unnamed x48, local copies, waits for them, and re-layouts  4.03 us
  transfers between devices with their start and end apart: 43, of which 15 were waited for; matrix products, arithmetic and copies ran while one was open for 9% of the time, Pallas kernels for 12%

profile of v3, /device:TPU:24, one launch (start us, length us, event | category | flops | bytes accessed | tf_op | source)
XLA Modules:
  0.0 183.7 jit_solution(17307012512234524888)
XLA Ops:
  0.0 3.2 %shard_map.73 = bf16[32,72,256]{2,1,0:T(8,128)(2,1)} custom-call(s32[32]{0:T(128)} %rows_ref.1, s32[32]{0:T(128)} %cols_ref.1, s32[1]{0:T(128)} %bitcast.share_ref.pair_ref, bf16[32,256,256]{2,1,0:T(8,128)(2,1)} %w_ref.1), custom_call_target="tpu_custom_call" | custom-call | tf_op jit(solution)/shard_map/pallas_call | solution.py:60
  3.2 11.6 %all-to-all-start = ((bf16[32,72,256]{2,1,0:T(8,128)(2,1)}), bf16[32,72,256]{2,1,0:T(8,128)(2,1)S(1)}, u32[]{:S(2)}, u32[]{:S(2)}) async-start(bf16[32,72,256]{2,1,0:T(8,128)(2,1)} %shard_map.73), calls=%async_computation | async-start | bytes 2359296 | tf_op jit(solution)/shard_map/all_to_all | solution.py:204
  14.8 1.6 collective-permute-start
  16.4 1.7 collective-permute-start.3
  18.1 1.9 %collective-permute-start.1 = (bf16[256,256]{1,0:T(8,128)(2,1)S(1)}, bf16[256,256]{1,0:T(8,128)(2,1)S(1)}, u32[]{:S(2)}, u32[]{:S(2)}) collective-permute-start(bf16[256,256]{1,0:T(8,128)(2,1)S(1)} %get-tuple-element.23), channel_id=1, source_target_pairs={{0,128},{32,160},{64,192},{96,224},{128,0},{160,32},{192,64},{224,... | collective-permute-start | bytes 393224 | tf_op jit(solution)/shard_map/ppermute | solution.py:27
  20.0 1.7 collective-permute-start.2
  21.7 2.5 %collective-permute-done.refs_1_ = bf16[512,256]{1,0:T(8,128)(2,1)S(1)} collective-permute-done((bf16[512,256]{1,0:T(8,128)(2,1)S(1)}, bf16[512,256]{1,0:T(8,128)(2,1)S(1)}, u32[]{:S(2)}, u32[]{:S(2)}) %collective-permute-start) | collective-permute-done | bytes 262176 | tf_op jit(solution)/shard_map/ppermute | solution.py:27
  24.2 4.2 %collective-permute-done.3.refs_4_ = bf16[512,256]{1,0:T(8,128)(2,1)S(1)} collective-permute-done((bf16[512,256]{1,0:T(8,128)(2,1)S(1)}, bf16[512,256]{1,0:T(8,128)(2,1)S(1)}, u32[]{:S(2)}, u32[]{:S(2)}) %collective-permute-start.3) | collective-permute-done | bytes 262176 | tf_op jit(solution)/shard_map/ppermute | solution.py:27
  29.0 1.2 collective-permute-done.2.refs_3_
  31.5 1.8 shard_map.74
  33.3 1.5 collective-permute-start.13
  34.9 1.8 collective-permute-start.14
  37.2 1.6 collective-permute-start.12
  38.7 1.5 collective-permute-start.10
  40.9 4.6 %collective-permute-done.13 = bf16[256,256]{1,0:T(8,128)(2,1)S(1)} collective-permute-done((bf16[256,256]{1,0:T(8,128)(2,1)S(1)}, bf16[256,256]{1,0:T(8,128)(2,1)S(1)}, u32[]{:S(2)}, u32[]{:S(2)}) %collective-permute-start.13) | collective-permute-done | bytes 131104 | tf_op jit(solution)/shard_map/ppermute | solution.py:27
  45.5 1.4 collective-permute-start.11
  46.9 3.2 %collective-permute-start.18 = (bf16[256,256]{1,0:T(8,128)(2,1)S(1)}, bf16[256,256]{1,0:T(8,128)(2,1)S(1)}, u32[]{:S(2)}, u32[]{:S(2)}) collective-permute-start(bf16[256,256]{1,0:T(8,128)(2,1)S(1)} %collective-permute-done.14), channel_id=1, source_target_pairs={{0,28},{1,29},{2,30},{3,31},{4,0},{5,1},{6,2},{7,3},{8,4},{9,5},{1... | collective-permute-start | bytes 393224 | tf_op jit(solution)/shard_map/ppermute | solution.py:27
  52.7 3.3 %collective-permute-start.25 = (bf16[1024,256]{1,0:T(8,128)(2,1)}, bf16[1024,256]{1,0:T(8,128)(2,1)}, u32[]{:S(2)}, u32[]{:S(2)}) collective-permute-start(bf16[1024,256]{1,0:T(8,128)(2,1)} %constant_dynamic-update-slice_fusion.refs_0_), channel_id=1, source_target_pairs={{0,28},{1,29},{2,30},{3,31},{4,0},{5,1},{6,2},{7,3},{8,4},{9,5},{1... | collective-permute-start | bytes 1572872 | tf_op jit(solution)/shard_map/ppermute | solution.py:27
  56.1 3.2 %collective-permute-start.19 = (bf16[256,256]{1,0:T(8,128)(2,1)S(1)}, bf16[256,256]{1,0:T(8,128)(2,1)S(1)}, u32[]{:S(2)}, u32[]{:S(2)}) collective-permute-start(bf16[256,256]{1,0:T(8,128)(2,1)S(1)} %collective-permute-done.18), channel_id=1, source_target_pairs={{0,28},{1,29},{2,30},{3,31},{4,0},{5,1},{6,2},{7,3},{8,4},{9,5},{1... | collective-permute-start | bytes 393224 | tf_op jit(solution)/shard_map/ppermute | solution.py:27
  59.3 9.4 %collective-permute-done.17 = bf16[256,256]{1,0:T(8,128)(2,1)S(1)} collective-permute-done((bf16[256,256]{1,0:T(8,128)(2,1)S(1)}, bf16[256,256]{1,0:T(8,128)(2,1)S(1)}, u32[]{:S(2)}, u32[]{:S(2)}) %collective-permute-start.17) | collective-permute-done | bytes 131104 | tf_op jit(solution)/shard_map/ppermute | solution.py:27
  68.8 3.3 %collective-permute-start.22 = (bf16[128,256]{1,0:T(8,128)(2,1)S(1)}, bf16[128,256]{1,0:T(8,128)(2,1)S(1)}, u32[]{:S(2)}, u32[]{:S(2)}) collective-permute-start(bf16[128,256]{1,0:T(8,128)(2,1)S(1)} %slice.70), channel_id=1, source_target_pairs={{0,28},{1,29},{2,30},{3,31},{4,0},{5,1},{6,2},{7,3},{8,4},{9,5},{1... | collective-permute-start | bytes 196616 | tf_op jit(solution)/shard_map/ppermute | solution.py:27
  72.1 2.1 %collective-permute-done.21 = bf16[128,256]{1,0:T(8,128)(2,1)S(1)} collective-permute-done((bf16[128,256]{1,0:T(8,128)(2,1)S(1)}, bf16[128,256]{1,0:T(8,128)(2,1)S(1)}, u32[]{:S(2)}, u32[]{:S(2)}) %collective-permute-start.21) | collective-permute-done | bytes 65568 | tf_op jit(solution)/shard_map/ppermute | solution.py:27
  74.4 1.6 collective-permute-start.29
  76.0 2.2 %collective-permute-start.38 = (bf16[2048,256]{1,0:T(8,128)(2,1)S(1)}, bf16[2048,256]{1,0:T(8,128)(2,1)S(1)}, u32[]{:S(2)}, u32[]{:S(2)}) collective-permute-start(bf16[2048,256]{1,0:T(8,128)(2,1)S(1)} %constant_dynamic-update-slice_fusion.5.refs_0_), channel_id=1, source_target_pairs={{0,1},{1,2},{2,3},{3,0},{4,5},{5,6},{6,7},{7,4},{8,9},{9,10},{10,1... | collective-permute-start | bytes 3145736 | tf_op jit(solution)/shard_map/ppermute | solution.py:27
  78.2 1.7 collective-permute-start.31
  80.0 5.7 %collective-permute-done.20.refs_2_ = bf16[1024,256]{1,0:T(8,128)(2,1)} collective-permute-done((bf16[1024,256]{1,0:T(8,128)(2,1)}, bf16[1024,256]{1,0:T(8,128)(2,1)}, u32[]{:S(2)}, u32[]{:S(2)}) %collective-permute-start.20) | collective-permute-done | bytes 524320 | tf_op jit(solution)/shard_map/ppermute | solution.py:27
  85.7 10.0 %collective-permute-done.26.refs_7_ = bf16[1024,256]{1,0:T(8,128)(2,1)S(1)} collective-permute-done((bf16[1024,256]{1,0:T(8,128)(2,1)}, bf16[1024,256]{1,0:T(8,128)(2,1)S(1)}, u32[]{:S(2)}, u32[]{:S(2)}) %collective-permute-start.26) | collective-permute-done | bytes 524320 | tf_op jit(solution)/shard_map/ppermute | solution.py:27
  95.7 1.2 collective-permute-done.38.refs_1_
  96.9 3.2 %collective-permute-start.27 = (bf16[1024,256]{1,0:T(8,128)(2,1)S(1)}, bf16[1024,256]{1,0:T(8,128)(2,1)S(1)}, u32[]{:S(2)}, u32[]{:S(2)}) collective-permute-start(bf16[1024,256]{1,0:T(8,128)(2,1)S(1)} %collective-permute-done.26.refs_7_), channel_id=1, source_target_pairs={{0,28},{1,29},{2,30},{3,31},{4,0},{5,1},{6,2},{7,3},{8,4},{9,5},{1... | collective-permute-start | bytes 1572872 | tf_op jit(solution)/shard_map/ppermute | solution.py:27
  100.2 1.4 collective-permute-done.40.refs_4_
  101.6 2.4 %collective-permute-start.39 = (bf16[1024,256]{1,0:T(8,128)(2,1)S(1)}, bf16[1024,256]{1,0:T(8,128)(2,1)S(1)}, u32[]{:S(2)}, u32[]{:S(2)}) collective-permute-start(bf16[1024,256]{1,0:T(8,128)(2,1)S(1)} %slice.75), channel_id=1, source_target_pairs={{0,1},{1,2},{2,3},{3,0},{4,5},{5,6},{6,7},{7,4},{8,9},{9,10},{10,1... | collective-permute-start | bytes 1572872 | tf_op jit(solution)/shard_map/ppermute | solution.py:27
  104.2 2.1 %collective-permute-done.23.refs_3_ = bf16[1024,256]{1,0:T(8,128)(2,1)S(1)} collective-permute-done((bf16[1024,256]{1,0:T(8,128)(2,1)}, bf16[1024,256]{1,0:T(8,128)(2,1)S(1)}, u32[]{:S(2)}, u32[]{:S(2)}) %collective-permute-start.23) | collective-permute-done | bytes 524320 | tf_op jit(solution)/shard_map/ppermute | solution.py:27
  106.3 1.6 collective-permute-start.30
  107.9 1.9 %slice.74 = bf16[16,72,256]{2,1,0:T(8,128)(2,1)} slice(bf16[32,72,256]{2,1,0:T(8,128)(2,1)} %collective-permute-done.31.refs_13_.refs_9_), slice={[16:32], [0:72], [0:256]} | slice | bytes 1179648 | tf_op jit(solution)/shard_map/slice | solution.py:234
  109.9 2.4 %collective-permute-start.32 = (bf16[16,72,256]{2,1,0:T(8,128)(2,1)}, bf16[16,72,256]{2,1,0:T(8,128)(2,1)S(1)}, u32[]{:S(2)}, u32[]{:S(2)}) collective-permute-start(bf16[16,72,256]{2,1,0:T(8,128)(2,1)} %slice.74), channel_id=1, source_target_pairs={{0,192},{32,224},{64,0},{96,32},{128,64},{160,96},{192,128},{224,1... | collective-permute-start | bytes 1769480 | tf_op jit(solution)/shard_map/ppermute | solution.py:27
  112.4 2.1 %collective-permute-done.41.refs_3_ = bf16[1024,256]{1,0:T(8,128)(2,1)S(1)} collective-permute-done((bf16[1024,256]{1,0:T(8,128)(2,1)S(1)}, bf16[1024,256]{1,0:T(8,128)(2,1)S(1)}, u32[]{:S(2)}, u32[]{:S(2)}) %collective-permute-start.41) | collective-permute-done | bytes 524320 | tf_op jit(solution)/shard_map/ppermute | solution.py:27
  114.5 9.6 %collective-permute-done.30.refs_11_.refs_7_ = bf16[16,72,256]{2,1,0:T(8,128)(2,1)S(1)} collective-permute-done((bf16[16,72,256]{2,1,0:T(8,128)(2,1)S(1)}, bf16[16,72,256]{2,1,0:T(8,128)(2,1)S(1)}, u32[]{:S(2)}, u32[]{:S(2)}) %collective-permute-start.30) | collective-permute-done | bytes 589856 | tf_op jit(solution)/shard_map/ppermute | solution.py:27
  124.3 1.8 slice.71
  126.0 1.7 slice.72
  128.7 0.9 copy.14
  130.8 0.7 copy.16
  132.3 3.2 %collective-permute-start.28 = (bf16[512,256]{1,0:T(8,128)(2,1)}, bf16[512,256]{1,0:T(8,128)(2,1)S(1)}, u32[]{:S(2)}, u32[]{:S(2)}) collective-permute-start(bf16[512,256]{1,0:T(8,128)(2,1)} %slice.72), channel_id=1, source_target_pairs={{0,28},{1,29},{2,30},{3,31},{4,0},{5,1},{6,2},{7,3},{8,4},{9,5},{1... | collective-permute-start | bytes 786440 | tf_op jit(solution)/shard_map/ppermute | solution.py:27
  135.5 1.3 multiply_add_fusion.1
  137.5 0.7 reshape.26.tags_ref
  138.7 21.1 %shard_map.76 = bf16[256,512]{1,0:T(8,128)(2,1)} custom-call(s32[64]{0:T(128)} %reshape.26.tags_ref, s32[64]{0:T(128)} %multiply_add_fusion.place_ref, s32[2]{0:T(128)} %live_ref.4, s32[1]{0:T(128)} %bitcast.share_ref.pair_ref, bf16[2048,256]{1,0:T(8,128)(2,1)} %copy-done.8, bf16[2048,256]{1,0:T(8,128)(2,1)} %copy-done.6, bf16[1024,256]{1,0:T(8,128)(2,1)} %copy-done.13, ...), custom_call_target="tpu_custom_call" | custom-call | tf_op jit(solution)/shard_map/pallas_call | solution.py:169
  160.6 21.2 %shard_map.75 = bf16[256,512]{1,0:T(8,128)(2,1)} custom-call(s32[64]{0:T(128)} %reshape.26.tags_ref, s32[64]{0:T(128)} %get-tuple-element.19.place_ref, s32[2]{0:T(128)} %live_ref.4, s32[1]{0:T(128)} %bitcast.share_ref.pair_ref, bf16[1024,256]{1,0:T(8,128)(2,1)} %constant_dynamic-update-slice_fusion.refs_0_, ...), custom_call_target="tpu_custom_call" | custom-call | tf_op jit(solution)/shard_map/pallas_call | solution.py:169
  181.8 1.0 pad_maximum_fusion
  182.8 0.9 reshape.30
  (114 shorter events, 10.6 us)
Async XLA Ops:
  3.2 28.4 %copy-start.1 = (s32[4096]{0:T(1024)S(1)}, s32[4096]{0:T(1024)}, u32[]{:S(2)}) copy-start(s32[4096]{0:T(1024)} %param.13) | copy-start | bytes 49156
  3.2 71.2 %all-to-all-start = ((bf16[32,72,256]{2,1,0:T(8,128)(2,1)}), bf16[32,72,256]{2,1,0:T(8,128)(2,1)S(1)}, u32[]{:S(2)}, u32[]{:S(2)}) async-start(bf16[32,72,256]{2,1,0:T(8,128)(2,1)} %shard_map.73), calls=%async_computation | async-start | bytes 2359296 | tf_op jit(solution)/shard_map/all_to_all | solution.py:204
  14.8 9.4 %collective-permute-start = (bf16[512,256]{1,0:T(8,128)(2,1)S(1)}, bf16[512,256]{1,0:T(8,128)(2,1)S(1)}, u32[]{:S(2)}, u32[]{:S(2)}) collective-permute-start(bf16[512,256]{1,0:T(8,128)(2,1)S(1)} %bitcast.8), channel_id=1, source_target_pairs={{0,64},{32,96},{64,128},{96,160},{128,192},{160,224},{192,0},{224,... | collective-permute-start | bytes 786440 | tf_op jit(solution)/shard_map/ppermute | solution.py:27
  16.4 12.1 %collective-permute-start.3 = (bf16[512,256]{1,0:T(8,128)(2,1)S(1)}, bf16[512,256]{1,0:T(8,128)(2,1)S(1)}, u32[]{:S(2)}, u32[]{:S(2)}) collective-permute-start(bf16[512,256]{1,0:T(8,128)(2,1)S(1)} %bitcast.9), channel_id=1, source_target_pairs={{0,192},{32,224},{64,0},{96,32},{128,64},{160,96},{192,128},{224,1... | collective-permute-start | bytes 786440 | tf_op jit(solution)/shard_map/ppermute | solution.py:27
  18.1 12.7 %collective-permute-start.4 = (bf16[512,256]{1,0:T(8,128)(2,1)S(1)}, bf16[512,256]{1,0:T(8,128)(2,1)S(1)}, u32[]{:S(2)}, u32[]{:S(2)}) collective-permute-start(bf16[512,256]{1,0:T(8,128)(2,1)S(1)} %bitcast.10), channel_id=1, source_target_pairs={{0,32},{32,0},{64,96},{96,64},{128,160},{160,128},{192,224},{224,1... | collective-permute-start | bytes 786440 | tf_op jit(solution)/shard_map/ppermute | solution.py:35
  18.1 10.6 %collective-permute-start.1 = (bf16[256,256]{1,0:T(8,128)(2,1)S(1)}, bf16[256,256]{1,0:T(8,128)(2,1)S(1)}, u32[]{:S(2)}, u32[]{:S(2)}) collective-permute-start(bf16[256,256]{1,0:T(8,128)(2,1)S(1)} %get-tuple-element.23), channel_id=1, source_target_pairs={{0,128},{32,160},{64,192},{96,224},{128,0},{160,32},{192,64},{224,... | collective-permute-start | bytes 393224 | tf_op jit(solution)/shard_map/ppermute | solution.py:27
  20.0 10.1 %collective-permute-start.2 = (bf16[256,256]{1,0:T(8,128)(2,1)S(1)}, bf16[256,256]{1,0:T(8,128)(2,1)S(1)}, u32[]{:S(2)}, u32[]{:S(2)}) collective-permute-start(bf16[256,256]{1,0:T(8,128)(2,1)S(1)} %get-tuple-element.22), channel_id=1, source_target_pairs={{0,128},{32,160},{64,192},{96,224},{128,0},{160,32},{192,64},{224,... | collective-permute-start | bytes 393224 | tf_op jit(solution)/shard_map/ppermute | solution.py:27
  24.2 7.3 %collective-permute-start.5 = (bf16[512,256]{1,0:T(8,128)(2,1)S(1)}, bf16[512,256]{1,0:T(8,128)(2,1)S(1)}, u32[]{:S(2)}, u32[]{:S(2)}) collective-permute-start(bf16[512,256]{1,0:T(8,128)(2,1)S(1)} %collective-permute-done.refs_1_), channel_id=1, source_target_pairs={{0,32},{32,0},{64,96},{96,64},{128,160},{160,128},{192,224},{224,1... | collective-permute-start | bytes 786440 | tf_op jit(solution)/shard_map/ppermute | solution.py:35
  28.5 3.0 %collective-permute-start.8 = (bf16[512,256]{1,0:T(8,128)(2,1)S(1)}, bf16[512,256]{1,0:T(8,128)(2,1)S(1)}, u32[]{:S(2)}, u32[]{:S(2)}) collective-permute-start(bf16[512,256]{1,0:T(8,128)(2,1)S(1)} %collective-permute-done.3.refs_4_), channel_id=1, source_target_pairs={{0,32},{32,0},{64,96},{96,64},{128,160},{160,128},{192,224},{224,1... | collective-permute-start | bytes 786440 | tf_op jit(solution)/shard_map/ppermute | solution.py:35
  28.8 2.1 %collective-permute-start.6 = (bf16[256,256]{1,0:T(8,128)(2,1)S(1)}, bf16[256,256]{1,0:T(8,128)(2,1)S(1)}, u32[]{:S(2)}, u32[]{:S(2)}) collective-permute-start(bf16[256,256]{1,0:T(8,128)(2,1)S(1)} %collective-permute-done.1.refs_2_), channel_id=1, source_target_pairs={{0,32},{32,0},{64,96},{96,64},{128,160},{160,128},{192,224},{224,1... | collective-permute-start | bytes 393224 | tf_op jit(solution)/shard_map/ppermute | solution.py:35
  30.2 1.3 collective-permute-start.7
  33.3 12.2 %collective-permute-start.13 = (bf16[256,256]{1,0:T(8,128)(2,1)S(1)}, bf16[256,256]{1,0:T(8,128)(2,1)S(1)}, u32[]{:S(2)}, u32[]{:S(2)}) collective-permute-start(bf16[256,256]{1,0:T(8,128)(2,1)S(1)} %get-tuple-element.13), channel_id=1, source_target_pairs={{0,4},{1,5},{2,6},{3,7},{4,8},{5,9},{6,10},{7,11},{8,12},{9,13},{1... | collective-permute-start | bytes 393224 | tf_op jit(solution)/shard_map/ppermute | solution.py:27
  34.9 12.1 %collective-permute-start.14 = (bf16[256,256]{1,0:T(8,128)(2,1)S(1)}, bf16[256,256]{1,0:T(8,128)(2,1)S(1)}, u32[]{:S(2)}, u32[]{:S(2)}) collective-permute-start(bf16[256,256]{1,0:T(8,128)(2,1)S(1)} %get-tuple-element.13), channel_id=1, source_target_pairs={{0,28},{1,29},{2,30},{3,31},{4,0},{5,1},{6,2},{7,3},{8,4},{9,5},{1... | collective-permute-start | bytes 393224 | tf_op jit(solution)/shard_map/ppermute | solution.py:27
  36.6 10.3 %collective-permute-start.9 = (bf16[256,256]{1,0:T(8,128)(2,1)S(1)}, bf16[256,256]{1,0:T(8,128)(2,1)S(1)}, u32[]{:S(2)}, u32[]{:S(2)}) collective-permute-start(bf16[256,256]{1,0:T(8,128)(2,1)S(1)} %get-tuple-element.12), channel_id=1, source_target_pairs={{0,1},{1,2},{2,3},{3,0},{4,5},{5,6},{6,7},{7,4},{8,9},{9,10},{10,1... | collective-permute-start | bytes 393224 | tf_op jit(solution)/shard_map/ppermute | solution.py:27
  37.2 14.9 %collective-permute-start.12 = (bf16[256,256]{1,0:T(8,128)(2,1)S(1)}, bf16[256,256]{1,0:T(8,128)(2,1)S(1)}, u32[]{:S(2)}, u32[]{:S(2)}) collective-permute-start(bf16[256,256]{1,0:T(8,128)(2,1)S(1)} %get-tuple-element.12), channel_id=1, source_target_pairs={{0,3},{1,0},{2,1},{3,2},{4,7},{5,4},{6,5},{7,6},{8,11},{9,8},{10,9... | collective-permute-start | bytes 393224 | tf_op jit(solution)/shard_map/ppermute | solution.py:27
  38.7 12.1 %collective-permute-start.10 = (bf16[128,256]{1,0:T(8,128)(2,1)S(1)}, bf16[128,256]{1,0:T(8,128)(2,1)S(1)}, u32[]{:S(2)}, u32[]{:S(2)}) collective-permute-start(bf16[128,256]{1,0:T(8,128)(2,1)S(1)} %get-tuple-element.25), channel_id=1, source_target_pairs={{0,2},{1,3},{2,0},{3,1},{4,6},{5,7},{6,4},{7,5},{8,10},{9,11},{10,... | collective-permute-start | bytes 196616 | tf_op jit(solution)/shard_map/ppermute | solution.py:27
  45.5 6.0 %collective-permute-start.11 = (bf16[128,256]{1,0:T(8,128)(2,1)S(1)}, bf16[128,256]{1,0:T(8,128)(2,1)S(1)}, u32[]{:S(2)}, u32[]{:S(2)}) collective-permute-start(bf16[128,256]{1,0:T(8,128)(2,1)S(1)} %get-tuple-element.24), channel_id=1, source_target_pairs={{0,2},{1,3},{2,0},{3,1},{4,6},{5,7},{6,4},{7,5},{8,10},{9,11},{10,... | collective-permute-start | bytes 196616 | tf_op jit(solution)/shard_map/ppermute | solution.py:27
  46.9 9.2 %collective-permute-start.16 = (bf16[256,256]{1,0:T(8,128)(2,1)S(1)}, bf16[256,256]{1,0:T(8,128)(2,1)S(1)}, u32[]{:S(2)}, u32[]{:S(2)}) collective-permute-start(bf16[256,256]{1,0:T(8,128)(2,1)S(1)} %collective-permute-done.13), channel_id=1, source_target_pairs={{0,4},{1,5},{2,6},{3,7},{4,8},{5,9},{6,10},{7,11},{8,12},{9,13},{1... | collective-permute-start | bytes 393224 | tf_op jit(solution)/shard_map/ppermute | solution.py:27
  46.9 9.2 %collective-permute-start.18 = (bf16[256,256]{1,0:T(8,128)(2,1)S(1)}, bf16[256,256]{1,0:T(8,128)(2,1)S(1)}, u32[]{:S(2)}, u32[]{:S(2)}) collective-permute-start(bf16[256,256]{1,0:T(8,128)(2,1)S(1)} %collective-permute-done.14), channel_id=1, source_target_pairs={{0,28},{1,29},{2,30},{3,31},{4,0},{5,1},{6,2},{7,3},{8,4},{9,5},{1... | collective-permute-start | bytes 393224 | tf_op jit(solution)/shard_map/ppermute | solution.py:27
  52.7 21.5 %collective-permute-start.15 = (bf16[1024,256]{1,0:T(8,128)(2,1)}, bf16[1024,256]{1,0:T(8,128)(2,1)}, u32[]{:S(2)}, u32[]{:S(2)}) collective-permute-start(bf16[1024,256]{1,0:T(8,128)(2,1)} %constant_dynamic-update-slice_fusion.refs_0_), channel_id=1, source_target_pairs={{0,4},{1,5},{2,6},{3,7},{4,8},{5,9},{6,10},{7,11},{8,12},{9,13},{1... | collective-permute-start | bytes 1572872 | tf_op jit(solution)/shard_map/ppermute | solution.py:27
  52.7 27.2 %collective-permute-start.25 = (bf16[1024,256]{1,0:T(8,128)(2,1)}, bf16[1024,256]{1,0:T(8,128)(2,1)}, u32[]{:S(2)}, u32[]{:S(2)}) collective-permute-start(bf16[1024,256]{1,0:T(8,128)(2,1)} %constant_dynamic-update-slice_fusion.refs_0_), channel_id=1, source_target_pairs={{0,28},{1,29},{2,30},{3,31},{4,0},{5,1},{6,2},{7,3},{8,4},{9,5},{1... | collective-permute-start | bytes 1572872 | tf_op jit(solution)/shard_map/ppermute | solution.py:27
  56.1 12.7 %collective-permute-start.17 = (bf16[256,256]{1,0:T(8,128)(2,1)S(1)}, bf16[256,256]{1,0:T(8,128)(2,1)S(1)}, u32[]{:S(2)}, u32[]{:S(2)}) collective-permute-start(bf16[256,256]{1,0:T(8,128)(2,1)S(1)} %collective-permute-done.16), channel_id=1, source_target_pairs={{0,4},{1,5},{2,6},{3,7},{4,8},{5,9},{6,10},{7,11},{8,12},{9,13},{1... | collective-permute-start | bytes 393224 | tf_op jit(solution)/shard_map/ppermute | solution.py:27
  56.1 12.7 %collective-permute-start.19 = (bf16[256,256]{1,0:T(8,128)(2,1)S(1)}, bf16[256,256]{1,0:T(8,128)(2,1)S(1)}, u32[]{:S(2)}, u32[]{:S(2)}) collective-permute-start(bf16[256,256]{1,0:T(8,128)(2,1)S(1)} %collective-permute-done.18), channel_id=1, source_target_pairs={{0,28},{1,29},{2,30},{3,31},{4,0},{5,1},{6,2},{7,3},{8,4},{9,5},{1... | collective-permute-start | bytes 393224 | tf_op jit(solution)/shard_map/ppermute | solution.py:27
  68.8 5.5 %collective-permute-start.21 = (bf16[128,256]{1,0:T(8,128)(2,1)S(1)}, bf16[128,256]{1,0:T(8,128)(2,1)S(1)}, u32[]{:S(2)}, u32[]{:S(2)}) collective-permute-start(bf16[128,256]{1,0:T(8,128)(2,1)S(1)} %slice.69), channel_id=1, source_target_pairs={{0,4},{1,5},{2,6},{3,7},{4,8},{5,9},{6,10},{7,11},{8,12},{9,13},{1... | collective-permute-start | bytes 196616 | tf_op jit(solution)/shard_map/ppermute | solution.py:27
  68.8 5.5 %collective-permute-start.22 = (bf16[128,256]{1,0:T(8,128)(2,1)S(1)}, bf16[128,256]{1,0:T(8,128)(2,1)S(1)}, u32[]{:S(2)}, u32[]{:S(2)}) collective-permute-start(bf16[128,256]{1,0:T(8,128)(2,1)S(1)} %slice.70), channel_id=1, source_target_pairs={{0,28},{1,29},{2,30},{3,31},{4,0},{5,1},{6,2},{7,3},{8,4},{9,5},{1... | collective-permute-start | bytes 196616 | tf_op jit(solution)/shard_map/ppermute | solution.py:27
  74.3 11.5 %collective-permute-start.20 = (bf16[1024,256]{1,0:T(8,128)(2,1)}, bf16[1024,256]{1,0:T(8,128)(2,1)}, u32[]{:S(2)}, u32[]{:S(2)}) collective-permute-start(bf16[1024,256]{1,0:T(8,128)(2,1)} %collective-permute-done.15.refs_1_), channel_id=1, source_target_pairs={{0,4},{1,5},{2,6},{3,7},{4,8},{5,9},{6,10},{7,11},{8,12},{9,13},{1... | collective-permute-start | bytes 1572872 | tf_op jit(solution)/shard_map/ppermute | solution.py:27
  74.4 53.7 %copy-start.2 = (bf16[32,72,256]{2,1,0:T(8,128)(2,1)}, bf16[32,72,256]{2,1,0:T(8,128)(2,1)S(1)}, u32[]{:S(2)}) copy-start(bf16[32,72,256]{2,1,0:T(8,128)(2,1)S(1)} %all-to-all-done.refs_9_.refs_5_) | copy-start | bytes 3538948
  74.4 29.6 %collective-permute-start.29 = (bf16[32,72,256]{2,1,0:T(8,128)(2,1)S(1)}, bf16[32,72,256]{2,1,0:T(8,128)(2,1)S(1)}, u32[]{:S(2)}, u32[]{:S(2)}) collective-permute-start(bf16[32,72,256]{2,1,0:T(8,128)(2,1)S(1)} %all-to-all-done.refs_9_.refs_5_), channel_id=1, source_target_pairs={{0,64},{32,96},{64,128},{96,160},{128,192},{160,224},{192,0},{224,... | collective-permute-start | bytes 3538952 | tf_op jit(solution)/shard_map/ppermute | solution.py:27
  76.0 30.3 %copy-start.8 = (bf16[2048,256]{1,0:T(8,128)(2,1)}, bf16[2048,256]{1,0:T(8,128)(2,1)S(1)}, u32[]{:S(2)}) copy-start(bf16[2048,256]{1,0:T(8,128)(2,1)S(1)} %constant_dynamic-update-slice_fusion.5.refs_0_) | copy-start | bytes 3145732
  76.0 20.9 %collective-permute-start.38 = (bf16[2048,256]{1,0:T(8,128)(2,1)S(1)}, bf16[2048,256]{1,0:T(8,128)(2,1)S(1)}, u32[]{:S(2)}, u32[]{:S(2)}) collective-permute-start(bf16[2048,256]{1,0:T(8,128)(2,1)S(1)} %constant_dynamic-update-slice_fusion.5.refs_0_), channel_id=1, source_target_pairs={{0,1},{1,2},{2,3},{3,0},{4,5},{5,6},{6,7},{7,4},{8,9},{9,10},{10,1... | collective-permute-start | bytes 3145736 | tf_op jit(solution)/shard_map/ppermute | solution.py:27
  78.2 28.1 %collective-permute-start.31 = (bf16[32,72,256]{2,1,0:T(8,128)(2,1)S(1)}, bf16[32,72,256]{2,1,0:T(8,128)(2,1)}, u32[]{:S(2)}, u32[]{:S(2)}) collective-permute-start(bf16[32,72,256]{2,1,0:T(8,128)(2,1)S(1)} %all-to-all-done.refs_9_.refs_5_), channel_id=1, source_target_pairs={{0,192},{32,224},{64,0},{96,32},{128,64},{160,96},{192,128},{224,1... | collective-permute-start | bytes 3538952 | tf_op jit(solution)/shard_map/ppermute | solution.py:27
  80.0 21.6 %collective-permute-start.40 = (bf16[2048,256]{1,0:T(8,128)(2,1)S(1)}, bf16[2048,256]{1,0:T(8,128)(2,1)S(1)}, u32[]{:S(2)}, u32[]{:S(2)}) collective-permute-start(bf16[2048,256]{1,0:T(8,128)(2,1)S(1)} %constant_dynamic-update-slice_fusion.5.refs_0_), channel_id=1, source_target_pairs={{0,3},{1,0},{2,1},{3,2},{4,7},{5,4},{6,5},{7,6},{8,11},{9,8},{10,9... | collective-permute-start | bytes 3145736 | tf_op jit(solution)/shard_map/ppermute | solution.py:27
  85.7 10.0 %collective-permute-start.26 = (bf16[1024,256]{1,0:T(8,128)(2,1)}, bf16[1024,256]{1,0:T(8,128)(2,1)S(1)}, u32[]{:S(2)}, u32[]{:S(2)}) collective-permute-start(bf16[1024,256]{1,0:T(8,128)(2,1)} %collective-permute-done.25.refs_8_), channel_id=1, source_target_pairs={{0,28},{1,29},{2,30},{3,31},{4,0},{5,1},{6,2},{7,3},{8,4},{9,5},{1... | collective-permute-start | bytes 1572872 | tf_op jit(solution)/shard_map/ppermute | solution.py:27
  95.7 28.4 %copy-start.12 = (bf16[1024,256]{1,0:T(8,128)(2,1)}, bf16[1024,256]{1,0:T(8,128)(2,1)S(1)}, u32[]{:S(2)}) copy-start(bf16[1024,256]{1,0:T(8,128)(2,1)S(1)} %collective-permute-done.26.refs_7_) | copy-start | bytes 1572868
  95.7 10.6 %collective-permute-start.23 = (bf16[1024,256]{1,0:T(8,128)(2,1)}, bf16[1024,256]{1,0:T(8,128)(2,1)S(1)}, u32[]{:S(2)}, u32[]{:S(2)}) collective-permute-start(bf16[1024,256]{1,0:T(8,128)(2,1)} %collective-permute-done.20.refs_2_), channel_id=1, source_target_pairs={{0,4},{1,5},{2,6},{3,7},{4,8},{5,9},{6,10},{7,11},{8,12},{9,13},{1... | collective-permute-start | bytes 1572872 | tf_op jit(solution)/shard_map/ppermute | solution.py:27
  96.9 12.9 %collective-permute-start.27 = (bf16[1024,256]{1,0:T(8,128)(2,1)S(1)}, bf16[1024,256]{1,0:T(8,128)(2,1)S(1)}, u32[]{:S(2)}, u32[]{:S(2)}) collective-permute-start(bf16[1024,256]{1,0:T(8,128)(2,1)S(1)} %collective-permute-done.26.refs_7_), channel_id=1, source_target_pairs={{0,28},{1,29},{2,30},{3,31},{4,0},{5,1},{6,2},{7,3},{8,4},{9,5},{1... | collective-permute-start | bytes 1572872 | tf_op jit(solution)/shard_map/ppermute | solution.py:27
  101.6 10.7 %collective-permute-start.39 = (bf16[1024,256]{1,0:T(8,128)(2,1)S(1)}, bf16[1024,256]{1,0:T(8,128)(2,1)S(1)}, u32[]{:S(2)}, u32[]{:S(2)}) collective-permute-start(bf16[1024,256]{1,0:T(8,128)(2,1)S(1)} %slice.75), channel_id=1, source_target_pairs={{0,1},{1,2},{2,3},{3,0},{4,5},{5,6},{6,7},{7,4},{8,9},{9,10},{10,1... | collective-permute-start | bytes 1572872 | tf_op jit(solution)/shard_map/ppermute | solution.py:27
  104.1 10.5 %collective-permute-start.41 = (bf16[1024,256]{1,0:T(8,128)(2,1)S(1)}, bf16[1024,256]{1,0:T(8,128)(2,1)S(1)}, u32[]{:S(2)}, u32[]{:S(2)}) collective-permute-start(bf16[1024,256]{1,0:T(8,128)(2,1)S(1)} %slice.76), channel_id=1, source_target_pairs={{0,3},{1,0},{2,1},{3,2},{4,7},{5,4},{6,5},{7,6},{8,11},{9,8},{10,9... | collective-permute-start | bytes 1572872 | tf_op jit(solution)/shard_map/ppermute | solution.py:27
  106.3 25.9 %collective-permute-start.33 = (bf16[32,72,256]{2,1,0:T(8,128)(2,1)S(1)}, bf16[32,72,256]{2,1,0:T(8,128)(2,1)}, u32[]{:S(2)}, u32[]{:S(2)}) collective-permute-start(bf16[32,72,256]{2,1,0:T(8,128)(2,1)S(1)} %all-to-all-done.refs_9_.refs_5_), channel_id=1, source_target_pairs={{0,32},{32,0},{64,96},{96,64},{128,160},{160,128},{192,224},{224,1... | collective-permute-start | bytes 3538952 | tf_op jit(solution)/shard_map/ppermute | solution.py:35
  106.3 17.8 %collective-permute-start.30 = (bf16[16,72,256]{2,1,0:T(8,128)(2,1)S(1)}, bf16[16,72,256]{2,1,0:T(8,128)(2,1)S(1)}, u32[]{:S(2)}, u32[]{:S(2)}) collective-permute-start(bf16[16,72,256]{2,1,0:T(8,128)(2,1)S(1)} %slice.73), channel_id=1, source_target_pairs={{0,64},{32,96},{64,128},{96,160},{128,192},{160,224},{192,0},{224,... | collective-permute-start | bytes 1769480 | tf_op jit(solution)/shard_map/ppermute | solution.py:27
  109.9 17.9 %collective-permute-start.32 = (bf16[16,72,256]{2,1,0:T(8,128)(2,1)}, bf16[16,72,256]{2,1,0:T(8,128)(2,1)S(1)}, u32[]{:S(2)}, u32[]{:S(2)}) collective-permute-start(bf16[16,72,256]{2,1,0:T(8,128)(2,1)} %slice.74), channel_id=1, source_target_pairs={{0,192},{32,224},{64,0},{96,32},{128,64},{160,96},{192,128},{224,1... | collective-permute-start | bytes 1769480 | tf_op jit(solution)/shard_map/ppermute | solution.py:27
  112.3 26.5 %collective-permute-start.34 = (bf16[32,72,256]{2,1,0:T(8,128)(2,1)S(1)}, bf16[32,72,256]{2,1,0:T(8,128)(2,1)}, u32[]{:S(2)}, u32[]{:S(2)}) collective-permute-start(bf16[32,72,256]{2,1,0:T(8,128)(2,1)S(1)} %collective-permute-done.29.refs_10_.refs_6_), channel_id=1, source_target_pairs={{0,32},{32,0},{64,96},{96,64},{128,160},{160,128},{192,224},{224,1... | collective-permute-start | bytes 3538952 | tf_op jit(solution)/shard_map/ppermute | solution.py:35
  114.5 24.2 %collective-permute-start.37 = (bf16[32,72,256]{2,1,0:T(8,128)(2,1)}, bf16[32,72,256]{2,1,0:T(8,128)(2,1)}, u32[]{:S(2)}, u32[]{:S(2)}) collective-permute-start(bf16[32,72,256]{2,1,0:T(8,128)(2,1)} %collective-permute-done.31.refs_13_.refs_9_), channel_id=1, source_target_pairs={{0,32},{32,0},{64,96},{96,64},{128,160},{160,128},{192,224},{224,1... | collective-permute-start | bytes 3538952 | tf_op jit(solution)/shard_map/ppermute | solution.py:35
  124.1 8.1 %collective-permute-start.35 = (bf16[16,72,256]{2,1,0:T(8,128)(2,1)S(1)}, bf16[16,72,256]{2,1,0:T(8,128)(2,1)}, u32[]{:S(2)}, u32[]{:S(2)}) collective-permute-start(bf16[16,72,256]{2,1,0:T(8,128)(2,1)S(1)} %collective-permute-done.30.refs_11_.refs_7_), channel_id=1, source_target_pairs={{0,32},{32,0},{64,96},{96,64},{128,160},{160,128},{192,224},{224,1... | collective-permute-start | bytes 1769480 | tf_op jit(solution)/shard_map/ppermute | solution.py:35
  127.7 11.0 %collective-permute-start.36 = (bf16[16,72,256]{2,1,0:T(8,128)(2,1)S(1)}, bf16[16,72,256]{2,1,0:T(8,128)(2,1)}, u32[]{:S(2)}, u32[]{:S(2)}) collective-permute-start(bf16[16,72,256]{2,1,0:T(8,128)(2,1)S(1)} %collective-permute-done.32.refs_12_.refs_8_), channel_id=1, source_target_pairs={{0,32},{32,0},{64,96},{96,64},{128,160},{160,128},{192,224},{224,1... | collective-permute-start | bytes 1769480 | tf_op jit(solution)/shard_map/ppermute | solution.py:35
  132.3 27.5 %collective-permute-start.24 = (bf16[512,256]{1,0:T(8,128)(2,1)}, bf16[512,256]{1,0:T(8,128)(2,1)S(1)}, u32[]{:S(2)}, u32[]{:S(2)}) collective-permute-start(bf16[512,256]{1,0:T(8,128)(2,1)} %slice.71), channel_id=1, source_target_pairs={{0,4},{1,5},{2,6},{3,7},{4,8},{5,9},{6,10},{7,11},{8,12},{9,13},{1... | collective-permute-start | bytes 786440 | tf_op jit(solution)/shard_map/ppermute | solution.py:27
  132.3 27.6 %collective-permute-start.28 = (bf16[512,256]{1,0:T(8,128)(2,1)}, bf16[512,256]{1,0:T(8,128)(2,1)S(1)}, u32[]{:S(2)}, u32[]{:S(2)}) collective-permute-start(bf16[512,256]{1,0:T(8,128)(2,1)} %slice.72), channel_id=1, source_target_pairs={{0,28},{1,29},{2,30},{3,31},{4,0},{5,1},{6,2},{7,3},{8,4},{9,5},{1... | collective-permute-start | bytes 786440 | tf_op jit(solution)/shard_map/ppermute | solution.py:27
  160.6 21.2 %copy-start.11 = (bf16[256,512]{1,0:T(8,128)(2,1)S(1)}, bf16[256,512]{1,0:T(8,128)(2,1)}, u32[]{:S(2)}) copy-start(bf16[256,512]{1,0:T(8,128)(2,1)} %shard_map.76) | copy-start | bytes 786436
  (13 other events, 110.6 us)

commit v4 on v3

--- a/solution.py
+++ b/solution.py
@@ -8,8 +8,9 @@
 from jax.sharding import PartitionSpec as P
 
 NX, NY, NZ = 4, 4, 8
-ROWS_A = 256
+ROWS_A = 208
 LABEL_ROWS = 8
+GROUP = 4
 
 
 def ring_steps(axis, shift):
@@ -111,12 +112,36 @@
     )(pair_id, live, mirror.reshape(1, -1), *pieces)
 
 
-def ladder_kernel(tags_ref, place_ref, live_ref, pair_ref, *refs, n_amps):
-    pieces, pieces_w = refs[:n_amps], refs[n_amps:-5]
-    o_ref, amps, weights, total, sems = refs[-5:]
-    senders, width = weights.shape[1], weights.shape[3]
+def label_kernel(tile_ref, got_ref, o_ref):
+    senders, lanes = o_ref.shape
+    start = got_ref.shape[1] - LABEL_ROWS
+    labels = got_ref[:, start:, :lanes].astype(jnp.float32)
+    lane = lax.broadcasted_iota(jnp.int32, (senders, lanes), 1)
+    first = lane % 2 == 0
+    tag = jnp.where(first, labels[:, 0], labels[:, 2]).astype(jnp.int32)
+    col = jnp.where(first, labels[:, 1], labels[:, 3]).astype(jnp.int32)
+    me = tile_ref[0]
+    behind_z = (me // NY - col // NY + NZ) % NZ
+    behind_y = (me % NY - col % NY + NY) % NY
+    o_ref[...] = jnp.where(lane < 2, tag, jnp.where(lane < 4, behind_z, behind_y))
+
+
+def read_labels(tile_id, got):
+    return pl.pallas_call(
+        label_kernel,
+        in_specs=[pl.BlockSpec(memory_space=pltpu.SMEM), pl.BlockSpec(memory_space=pltpu.VMEM)],
+        out_specs=pl.BlockSpec(memory_space=pltpu.VMEM),
+        out_shape=jax.ShapeDtypeStruct((got.shape[0], 128), jnp.int32),
+        compiler_params=pltpu.CompilerParams(vmem_limit_bytes=8 << 20),
+    )(tile_id, got)
+
+
+def ladder_kernel(label_ref, live_ref, pair_ref, *refs, n_a, n_b):
+    pieces_a, pieces_b, pieces_w = refs[:n_a], refs[n_a : n_a + n_b], refs[n_a + n_b : -8]
+    o_ref, amps, weights, total, slots, z_list, y_list, sems = refs[-8:]
+    senders, width = weights.shape[1] - 1, weights.shape[3]
     share = width // weights.shape[0]
-    rows = amps.shape[0] // (NY * NZ)
+    rows_a = pieces_a[0].shape[1]
     me = pair_ref[0]
     made = []
 
@@ -124,36 +149,70 @@
         made.append(pltpu.make_async_copy(source, target, sems.at[len(made)]))
         made[-1].start()
 
-    at = 0
-    for piece in pieces:
-        copy(piece, amps.at[pl.ds(at, piece.shape[0]), :])
-        at += piece.shape[0]
     at = 0
     for piece in pieces_w:
         behind, core = at // senders % NX, at // senders // NX
         source = 2 * lax.rem(me // 2 + NX - behind, NX) + lax.rem(me + core, 2)
         copy(piece, weights.at[source, pl.ds(at % senders, piece.shape[0])])
         at += piece.shape[0]
+    at = 0
+    for piece in pieces_a:
+        copy(piece, amps.at[at // NY, pl.ds(at % NY, piece.shape[0]), pl.ds(0, rows_a), :])
+        at += piece.shape[0]
+    at = 0
+    for piece in pieces_b:
+        height = piece.shape[1]
+        copy(piece, amps.at[pl.ds(at % NZ, piece.shape[0]), at // NZ, pl.ds(rows_a, height), :])
+        at += piece.shape[0]
+
     total[...] = jnp.zeros_like(total)
+    weights[:, senders] = jnp.zeros(weights.shape[:1] + weights.shape[2:], weights.dtype)
+    room = slots.shape[0] // 2
+
+    def sort(slot, counts):
+        tag = label_ref[slot // 2, slot % 2]
+        at = jnp.where(tag == 2, room + counts[1], counts[0])
+
+        @pl.when(tag > 0)
+        def _():
+            slots[at] = slot
+            z_list[at] = label_ref[slot // 2, 2 + slot % 2]
+            y_list[at] = label_ref[slot // 2, 4 + slot % 2]
+
+        return (
+            counts[0] + (tag == 1).astype(jnp.int32),
+            counts[1] + (tag == 2).astype(jnp.int32),
+        )
+
+    counts = lax.fori_loop(0, 2 * senders, sort, (jnp.int32(0), jnp.int32(0)))
+    for r in range(2):
+        for i in range(GROUP):
+            at = r * room + counts[r] + i
+            slots[at] = 2 * senders
+            z_list[at] = 0
+            y_list[at] = 0
+
     for one in made:
         one.wait()
 
-    @pl.loop(0, senders)
-    def _(sender):
-        for j in range(2):
-            slot = sender * 2 + j
-            tag = tags_ref[slot]
-
-            @pl.when(tag > 0)
-            def _(j=j, slot=slot, tag=tag):
-                weight = weights[:, sender, j * share : (j + 1) * share, :].reshape(-1, width)
-                at = pl.multiple_of(place_ref[slot] * rows, 16)
-                total[tag - 1] += lax.dot_general(
-                    amps[pl.ds(at, rows), :],
+    for r in range(2):
+
+        @pl.loop(0, (counts[r] + GROUP - 1) // GROUP)
+        def _(g, r=r):
+            added = None
+            for i in range(GROUP):
+                at = r * room + g * GROUP + i
+                slot = slots[at]
+                low = pl.multiple_of(slot % 2 * share, share)
+                weight = weights[:, slot // 2, pl.ds(low, share), :].reshape(-1, width)
+                term = lax.dot_general(
+                    amps[z_list[at], y_list[at]],
                     weight,
                     (((1,), (1,)), ((), ())),
                     preferred_element_type=jnp.float32,
                 )
+                added = term if added is None else added + term
+            total[r] += added
 
     position = lax.broadcasted_iota(jnp.int32, (1, width), 1)
     for r in range(2):
@@ -161,25 +220,28 @@
         o_ref[:, r * width : (r + 1) * width] = kept.astype(jnp.bfloat16)
 
 
-def ladder(tags, place, live, pair_id, pieces, pieces_w):
+def ladder(labels, live, pair_id, pieces_a, pieces_b, pieces_w):
     senders, height, width = pieces_w[0].shape
-    n_amps, n_w = len(pieces), len(pieces_w)
-    all_rows = sum(p.shape[0] for p in pieces)
-    rows = all_rows // (NY * NZ)
+    count = pieces_a[0].shape[1] + pieces_b[0].shape[1]
+    n_a, n_b, n_w = len(pieces_a), len(pieces_b), len(pieces_w)
+    room = 2 * senders + GROUP
     return pl.pallas_call(
-        functools.partial(ladder_kernel, n_amps=n_amps),
-        in_specs=[pl.BlockSpec(memory_space=pltpu.SMEM)] * 4
-        + [pl.BlockSpec(memory_space=pl.ANY)] * (n_amps + n_w),
+        functools.partial(ladder_kernel, n_a=n_a, n_b=n_b),
+        in_specs=[pl.BlockSpec(memory_space=pltpu.SMEM)] * 3
+        + [pl.BlockSpec(memory_space=pl.ANY)] * (n_a + n_b + n_w),
         out_specs=pl.BlockSpec(memory_space=pltpu.VMEM),
         scratch_shapes=[
-            pltpu.VMEM((all_rows, width), jnp.bfloat16),
-            pltpu.VMEM((2 * NX, senders, height, width), jnp.bfloat16),
-            pltpu.VMEM((2, rows, width), jnp.float32),
-            pltpu.SemaphoreType.DMA((n_amps + n_w,)),
+            pltpu.VMEM((NZ, NY, count, width), jnp.bfloat16),
+            pltpu.VMEM((2 * NX, senders + 1, height, width), jnp.bfloat16),
+            pltpu.VMEM((2, count, width), jnp.float32),
+            pltpu.SMEM((2 * room,), jnp.int32),
+            pltpu.SMEM((2 * room,), jnp.int32),
+            pltpu.SMEM((2 * room,), jnp.int32),
+            pltpu.SemaphoreType.DMA((n_a + n_b + n_w,)),
         ],
-        out_shape=jax.ShapeDtypeStruct((rows, 2 * width), jnp.bfloat16),
+        out_shape=jax.ShapeDtypeStruct((count, 2 * width), jnp.bfloat16),
         compiler_params=pltpu.CompilerParams(vmem_limit_bytes=60 << 20),
-    )(tags, place, live, pair_id, *pieces, *pieces_w)
+    )(labels, live, pair_id, *pieces_a, *pieces_b, *pieces_w)
 
 
 def local(amplitudes, size_cd, integrals, block_rows, block_cols, size_ab, mirror):
@@ -188,8 +250,6 @@
     shares = lax.axis_size("pair")
     pair_id = lax.axis_index("pair").astype(jnp.int32)
     tile_id = lax.axis_index("tile").astype(jnp.int32)
-    share = width // shares
-
     raw = amplitudes.reshape(count, width)
     half = count // 2
     pieces = [
@@ -201,7 +261,7 @@
     ]
 
     routed = route(block_rows, block_cols, pair_id.reshape(1), integrals, owners, shares)
-    got = lax.all_to_all(routed, "tile", split_axis=0, concat_axis=0, tiled=True)
+    got = lax.all_to_all(after(routed, *pieces[1:]), "tile", split_axis=0, concat_axis=0, tiled=True)
 
     pieces += [other_core(p) for p in pieces]
     a, b = mirror_sum(pair_id.reshape(1), size_cd, mirror, pieces)
@@ -214,13 +274,14 @@
     a0 = after(a0, b1, b7)
     a1, a7 = send("z", 1, a0), send("z", -1, a0)
     b3, b5 = send("z", 1, b2), send("z", -1, b6)
+    b3, b5 = after(b3, got), after(b5, got)
     half = b.shape[0] // 2
     b4 = [send("z", 1, b3[:half]), send("z", -1, b5[half:])]
     a1, a7 = after(a1, b3, b5), after(a7, b3, b5)
     a2, a6 = send("z", 1, a1), send("z", -1, a7)
     b0 = jnp.concatenate([b, b1, b2, b3, *b4, b5, b6, b7], axis=0)
     by1, by3 = send("y", 1, b0), send("y", -1, b0)
-    a2, a6 = after(a2, *b4), after(a6, *b4)
+    a2, a6 = after(a2, b0), after(a6, b0)
     a3, a5 = send("z", 1, a2), send("z", -1, a6)
     half = a0.shape[0] // 2
     a4 = [send("z", 1, a3[:half]), send("z", -1, a5[half:])]
@@ -231,17 +292,20 @@
 
     w1, w3 = send("x", 1, got), send("x", -1, got)
     half = got.shape[0] // 2
+    w1, w3 = after(w1, a2, a6), after(w3, a2, a6)
     w2 = [send("x", 1, w1[:half]), send("x", -1, w3[half:])]
     pieces_w = [got, w1, *w2, w3]
-    pieces_w += [other_core(p) for p in pieces_w]
-    labels = got[:, 2 * share : 2 * share + 4, 0].astype(jnp.int32)
-    tags = labels[:, 0::2].reshape(-1)
-    cols = labels[:, 1::2].reshape(-1)
-    behind_z = (tile_id // NY - cols // NY) % NZ
-    behind_y = (tile_id % NY - cols % NY) % NY
-    above = ladder(tags, behind_z * NY + behind_y, size_ab, pair_id.reshape(1), pieces_a, pieces_w)
-    below = ladder(tags, behind_y * NZ + behind_z, size_ab, pair_id.reshape(1), pieces_b, pieces_w)
-    return jnp.concatenate([above, below], axis=0).reshape(count, 2, width)
+    held = [after(p, a3, a5) for p in (got, w1)] + [after(p, *a4) for p in w2] + [after(w3, a3, a5)]
+    pieces_w += [other_core(p) for p in held]
+    result = ladder(
+        read_labels(tile_id.reshape(1), got),
+        size_ab,
+        pair_id.reshape(1),
+        [p.reshape(-1, *a.shape) for p in pieces_a],
+        [p.reshape(-1, *b.shape) for p in pieces_b],
+        pieces_w,
+    )
+    return result.reshape(count, 2, width)
 
 
 def solution(mesh):

time: 183 us -> 160 us (0.87)
  the two profiles are of different devices: /device:TPU:24 before, /device:TPU:1 now
where the time goes in v4:
time: 160 us; the launch traced here: 158 us
  starting transfers between devices  67.9 us (42%)
  waiting for transfers between devices  61.4 us (38%)
  Pallas kernels  17.6 us (11%)
  local copies, waits for them, and re-layouts  9.81 us (6%)
    ppermute x32, waiting for transfers between devices, send(): lax.ppermute(piece, 'pair' if axis == 'x' else 'tile', ring_steps(axis, s...  59.4 us
    ppermute x32, starting transfers between devices, send(): lax.ppermute(piece, 'pair' if axis == 'x' else 'tile', ring_steps(axis, s...  39.5 us
    ppermute x10, starting transfers between devices, other_core(): return lax.ppermute(piece, 'pair', [(p, p ^ 1) for p in range(2 * NX)])  17.2 us
    pallas_call x1, Pallas kernels, ladder(): pl.pallas_call(functools.partial(ladder_kernel, n_a=n_a, n_b=n_b), in_spe...  12.5 us
    all_to_all x1, starting transfers between devices, local(): lax.all_to_all(after(routed, *pieces[1:]), 'tile', split_axis=0, concat_a...  11.2 us
    unnamed x50, local copies, waits for them, and re-layouts  3.61 us
  transfers between devices with their start and end apart: 43, of which 18 were waited for; matrix products, arithmetic and copies ran while one was open for 4% of the time, Pallas kernels for 3%

profile of v4, /device:TPU:1, one launch (start us, length us, event | category | flops | bytes accessed | tf_op | source)
XLA Modules:
  0.0 157.7 jit_solution(12593125043728108318)
XLA Ops:
  0.0 2.0 %collective-permute-start = (bf16[512,256]{1,0:T(8,128)(2,1)}, bf16[512,256]{1,0:T(8,128)(2,1)S(1)}, u32[]{:S(2)}, u32[]{:S(2)}) collective-permute-start(bf16[512,256]{1,0:T(8,128)(2,1)} %bitcast.22), channel_id=1, source_target_pairs={{0,64},{32,96},{64,128},{96,160},{128,192},{160,224},{192,0},{224,... | collective-permute-start | bytes 786440 | tf_op jit(solution)/shard_map/ppermute | solution.py:28
  2.0 1.3 collective-permute-start.3
  4.3 1.8 %collective-permute-start.1 = (bf16[256,256]{1,0:T(8,128)(2,1)S(1)}, bf16[256,256]{1,0:T(8,128)(2,1)S(1)}, u32[]{:S(2)}, u32[]{:S(2)}) collective-permute-start(bf16[256,256]{1,0:T(8,128)(2,1)S(1)} %get-tuple-element.40), channel_id=1, source_target_pairs={{0,128},{32,160},{64,192},{96,224},{128,0},{160,32},{192,64},{224,... | collective-permute-start | bytes 393224 | tf_op jit(solution)/shard_map/ppermute | solution.py:28
  6.1 1.2 collective-permute-start.2
  7.4 3.2 %shard_map.73 = bf16[32,72,256]{2,1,0:T(8,128)(2,1)} custom-call(s32[32]{0:T(128)} %rows_ref.1, s32[32]{0:T(128)} %cols_ref.1, s32[1]{0:T(128)} %bitcast.1.share_ref.pair_ref, bf16[32,256,256]{2,1,0:T(8,128)(2,1)} %w_ref.1), custom_call_target="tpu_custom_call" | custom-call | tf_op jit(solution)/shard_map/pallas_call | solution.py:61
  10.5 2.7 %collective-permute-done.1.refs_2_ = bf16[256,256]{1,0:T(8,128)(2,1)S(1)} collective-permute-done((bf16[256,256]{1,0:T(8,128)(2,1)S(1)}, bf16[256,256]{1,0:T(8,128)(2,1)S(1)}, u32[]{:S(2)}, u32[]{:S(2)}) %collective-permute-start.1) | collective-permute-done | bytes 131104 | tf_op jit(solution)/shard_map/ppermute | solution.py:28
  13.2 2.8 %collective-permute-done.2.refs_3_ = bf16[256,256]{1,0:T(8,128)(2,1)S(1)} collective-permute-done((bf16[256,256]{1,0:T(8,128)(2,1)S(1)}, bf16[256,256]{1,0:T(8,128)(2,1)S(1)}, u32[]{:S(2)}, u32[]{:S(2)}) %collective-permute-start.2) | collective-permute-done | bytes 131104 | tf_op jit(solution)/shard_map/ppermute | solution.py:28
  16.0 11.2 %all-to-all-start = ((bf16[32,72,256]{2,1,0:T(8,128)(2,1)}), bf16[32,72,256]{2,1,0:T(8,128)(2,1)S(1)}, u32[]{:S(2)}, u32[]{:S(2)}) async-start(bf16[32,72,256]{2,1,0:T(8,128)(2,1)} %shard_map.73), calls=%async_computation | async-start | bytes 2359296 | tf_op jit(solution)/shard_map/all_to_all | solution.py:264
  27.3 1.9 %collective-permute-start.4 = (bf16[512,256]{1,0:T(8,128)(2,1)S(1)}, bf16[512,256]{1,0:T(8,128)(2,1)S(1)}, u32[]{:S(2)}, u32[]{:S(2)}) collective-permute-start(bf16[512,256]{1,0:T(8,128)(2,1)S(1)} %bitcast.24), channel_id=1, source_target_pairs={{0,32},{32,0},{64,96},{96,64},{128,160},{160,128},{192,224},{224,1... | collective-permute-start | bytes 786440 | tf_op jit(solution)/shard_map/ppermute | solution.py:36
  31.5 1.8 %shard_map.75 = (bf16[208,256]{1,0:T(8,128)(2,1)S(1)}, bf16[304,256]{1,0:T(8,128)(2,1)S(1)}) custom-call(s32[1]{0:T(128)} %bitcast.1.share_ref.pair_ref, s32[1]{0:T(128)S(6)} %copy.20.live_ref, s32[1,4096]{1,0:T(1,128)S(1)} %bitcast.26, bf16[512,256]{1,0:T(8,128)(2,1)S(1)} %bitcast.25, bf16[512,256]{1,0:T(8,128)(2,1)S(1)} %collective-permute-done.refs_1_, ...), custom_call_target="tpu_custom_call" | custom-call | tf_op jit(solution)/shard_map/pallas_call | solution.py:104
  33.3 1.6 %collective-permute-start.9 = (bf16[208,256]{1,0:T(8,128)(2,1)S(1)}, bf16[208,256]{1,0:T(8,128)(2,1)S(1)}, u32[]{:S(2)}, u32[]{:S(2)}) collective-permute-start(bf16[208,256]{1,0:T(8,128)(2,1)S(1)} %get-tuple-element.23), channel_id=1, source_target_pairs={{0,1},{1,2},{2,3},{3,0},{4,5},{5,6},{6,7},{7,4},{8,9},{9,10},{10,1... | collective-permute-start | bytes 319496 | tf_op jit(solution)/shard_map/ppermute | solution.py:28
  34.8 1.3 collective-permute-start.12
  36.2 1.4 collective-permute-start.13
  37.5 1.3 collective-permute-start.14
  38.8 1.8 %collective-permute-start.10 = (bf16[104,256]{1,0:T(8,128)(2,1)S(1)}, bf16[104,256]{1,0:T(8,128)(2,1)S(1)}, u32[]{:S(2)}, u32[]{:S(2)}) collective-permute-start(bf16[104,256]{1,0:T(8,128)(2,1)S(1)} %get-tuple-element.42), channel_id=1, source_target_pairs={{0,2},{1,3},{2,0},{3,1},{4,6},{5,7},{6,4},{7,5},{8,10},{9,11},{10,... | collective-permute-start | bytes 159752 | tf_op jit(solution)/shard_map/ppermute | solution.py:28
  41.3 1.2 collective-permute-start.11
  42.5 2.3 %collective-permute-done.10 = bf16[104,256]{1,0:T(8,128)(2,1)S(1)} collective-permute-done((bf16[104,256]{1,0:T(8,128)(2,1)S(1)}, bf16[104,256]{1,0:T(8,128)(2,1)S(1)}, u32[]{:S(2)}, u32[]{:S(2)}) %collective-permute-start.10) | collective-permute-done | bytes 53280 | tf_op jit(solution)/shard_map/ppermute | solution.py:28
  44.8 3.0 %collective-permute-done.11 = bf16[104,256]{1,0:T(8,128)(2,1)S(1)} collective-permute-done((bf16[104,256]{1,0:T(8,128)(2,1)S(1)}, bf16[104,256]{1,0:T(8,128)(2,1)S(1)}, u32[]{:S(2)}, u32[]{:S(2)}) %collective-permute-start.11) | collective-permute-done | bytes 53280 | tf_op jit(solution)/shard_map/ppermute | solution.py:28
  47.9 9.1 %collective-permute-done.13 = bf16[304,256]{1,0:T(8,128)(2,1)S(1)} collective-permute-done((bf16[304,256]{1,0:T(8,128)(2,1)S(1)}, bf16[304,256]{1,0:T(8,128)(2,1)S(1)}, u32[]{:S(2)}, u32[]{:S(2)}) %collective-permute-start.13) | collective-permute-done | bytes 155680 | tf_op jit(solution)/shard_map/ppermute | solution.py:28
  57.1 1.5 collective-permute-start.16
  58.6 1.2 collective-permute-start.18
  59.8 1.4 collective-permute-start.25
  61.2 8.6 %collective-permute-done.16 = bf16[304,256]{1,0:T(8,128)(2,1)S(1)} collective-permute-done((bf16[304,256]{1,0:T(8,128)(2,1)S(1)}, bf16[304,256]{1,0:T(8,128)(2,1)S(1)}, u32[]{:S(2)}, u32[]{:S(2)}) %collective-permute-start.16) | collective-permute-done | bytes 155680 | tf_op jit(solution)/shard_map/ppermute | solution.py:28
  69.8 2.7 %collective-permute-start.19 = (bf16[304,256]{1,0:T(8,128)(2,1)}, bf16[304,256]{1,0:T(8,128)(2,1)S(1)}, u32[]{:S(2)}, u32[]{:S(2)}) collective-permute-start(bf16[304,256]{1,0:T(8,128)(2,1)} %collective-permute-done.18), channel_id=1, source_target_pairs={{0,28},{1,29},{2,30},{3,31},{4,0},{5,1},{6,2},{7,3},{8,4},{9,5},{1... | collective-permute-start | bytes 466952 | tf_op jit(solution)/shard_map/ppermute | solution.py:28
  72.5 2.7 %collective-permute-done.17 = bf16[304,256]{1,0:T(8,128)(2,1)} collective-permute-done((bf16[304,256]{1,0:T(8,128)(2,1)S(1)}, bf16[304,256]{1,0:T(8,128)(2,1)}, u32[]{:S(2)}, u32[]{:S(2)}) %collective-permute-start.17) | collective-permute-done | bytes 155680 | tf_op jit(solution)/shard_map/ppermute | solution.py:28
  75.2 2.2 %collective-permute-done.19 = bf16[304,256]{1,0:T(8,128)(2,1)S(1)} collective-permute-done((bf16[304,256]{1,0:T(8,128)(2,1)}, bf16[304,256]{1,0:T(8,128)(2,1)S(1)}, u32[]{:S(2)}, u32[]{:S(2)}) %collective-permute-start.19) | collective-permute-done | bytes 155680 | tf_op jit(solution)/shard_map/ppermute | solution.py:28
  78.3 1.2 collective-permute-start.20
  79.5 1.2 collective-permute-start.21
  80.7 1.4 collective-permute-start.22
  83.6 5.8 %collective-permute-done.21 = bf16[152,256]{1,0:T(8,128)(2,1)S(1)} collective-permute-done((bf16[152,256]{1,0:T(8,128)(2,1)S(1)}, bf16[152,256]{1,0:T(8,128)(2,1)S(1)}, u32[]{:S(2)}, u32[]{:S(2)}) %collective-permute-start.21) | collective-permute-done | bytes 77856 | tf_op jit(solution)/shard_map/ppermute | solution.py:28
  91.3 1.1 collective-permute-start.26
  92.5 2.2 %collective-permute-start.31 = (bf16[2432,256]{1,0:T(8,128)(2,1)S(1)}, bf16[2432,256]{1,0:T(8,128)(2,1)S(1)}, u32[]{:S(2)}, u32[]{:S(2)}) collective-permute-start(bf16[2432,256]{1,0:T(8,128)(2,1)S(1)} %constant_dynamic-update-slice_fusion.5), channel_id=1, source_target_pairs={{0,3},{1,0},{2,1},{3,2},{4,7},{5,4},{6,5},{7,6},{8,11},{9,8},{10,9... | collective-permute-start | bytes 3735560 | tf_op jit(solution)/shard_map/ppermute | solution.py:28
  94.7 4.7 %collective-permute-done.26 = bf16[832,256]{1,0:T(8,128)(2,1)S(1)} collective-permute-done((bf16[832,256]{1,0:T(8,128)(2,1)}, bf16[832,256]{1,0:T(8,128)(2,1)S(1)}, u32[]{:S(2)}, u32[]{:S(2)}) %collective-permute-start.26) | collective-permute-done | bytes 426016 | tf_op jit(solution)/shard_map/ppermute | solution.py:28
  99.4 1.5 collective-permute-start.23
  100.8 6.3 %collective-permute-done.33.refs_15_ = bf16[32,72,256]{2,1,0:T(8,128)(2,1)} collective-permute-done((bf16[32,72,256]{2,1,0:T(8,128)(2,1)S(1)}, bf16[32,72,256]{2,1,0:T(8,128)(2,1)}, u32[]{:S(2)}, u32[]{:S(2)}) %collective-permute-start.33) | collective-permute-done | bytes 1179680 | tf_op jit(solution)/shard_map/ppermute | solution.py:28
  107.3 1.1 slice.54
  108.4 4.6 %collective-permute-done.35.refs_18_ = bf16[32,72,256]{2,1,0:T(8,128)(2,1)} collective-permute-done((bf16[32,72,256]{2,1,0:T(8,128)(2,1)S(1)}, bf16[32,72,256]{2,1,0:T(8,128)(2,1)}, u32[]{:S(2)}, u32[]{:S(2)}) %collective-permute-start.35) | collective-permute-done | bytes 1179680 | tf_op jit(solution)/shard_map/ppermute | solution.py:28
  113.4 1.1 slice.55
  114.6 2.4 %collective-permute-start.36 = (bf16[16,72,256]{2,1,0:T(8,128)(2,1)S(1)}, bf16[16,72,256]{2,1,0:T(8,128)(2,1)}, u32[]{:S(2)}, u32[]{:S(2)}) collective-permute-start(bf16[16,72,256]{2,1,0:T(8,128)(2,1)S(1)} %slice.55), channel_id=1, source_target_pairs={{0,192},{32,224},{64,0},{96,32},{128,64},{160,96},{192,128},{224,1... | collective-permute-start | bytes 1769480 | tf_op jit(solution)/shard_map/ppermute | solution.py:28
  117.9 1.9 %collective-permute-start.28 = (bf16[416,256]{1,0:T(8,128)(2,1)S(1)}, bf16[416,256]{1,0:T(8,128)(2,1)S(1)}, u32[]{:S(2)}, u32[]{:S(2)}) collective-permute-start(bf16[416,256]{1,0:T(8,128)(2,1)S(1)} %slice.57), channel_id=1, source_target_pairs={{0,28},{1,29},{2,30},{3,31},{4,0},{5,1},{6,2},{7,3},{8,4},{9,5},{1... | collective-permute-start | bytes 638984 | tf_op jit(solution)/shard_map/ppermute | solution.py:28
  120.1 3.3 %collective-permute-done.24 = bf16[416,256]{1,0:T(8,128)(2,1)S(1)} collective-permute-done((bf16[416,256]{1,0:T(8,128)(2,1)S(1)}, bf16[416,256]{1,0:T(8,128)(2,1)S(1)}, u32[]{:S(2)}, u32[]{:S(2)}) %collective-permute-start.24) | collective-permute-done | bytes 213024 | tf_op jit(solution)/shard_map/ppermute | solution.py:28
  123.4 2.5 %collective-permute-start.32 = (bf16[1216,256]{1,0:T(8,128)(2,1)S(1)}, bf16[1216,256]{1,0:T(8,128)(2,1)}, u32[]{:S(2)}, u32[]{:S(2)}) collective-permute-start(bf16[1216,256]{1,0:T(8,128)(2,1)S(1)} %slice.59), channel_id=1, source_target_pairs={{0,3},{1,0},{2,1},{3,2},{4,7},{5,4},{6,5},{7,6},{8,11},{9,8},{10,9... | collective-permute-start | bytes 1867784 | tf_op jit(solution)/shard_map/ppermute | solution.py:28
  125.9 6.2 %collective-permute-start.37 = (bf16[32,72,256]{2,1,0:T(8,128)(2,1)S(1)}, bf16[32,72,256]{2,1,0:T(8,128)(2,1)S(1)}, u32[]{:S(2)}, u32[]{:S(2)}) collective-permute-start(bf16[32,72,256]{2,1,0:T(8,128)(2,1)S(1)} %all-to-all-done.got_ref.refs_14_), channel_id=1, source_target_pairs={{0,32},{32,0},{64,96},{96,64},{128,160},{160,128},{192,224},{224,1... | collective-permute-start | bytes 3538952 | tf_op jit(solution)/shard_map/ppermute | solution.py:36
  132.7 5.1 %collective-permute-start.39 = (bf16[16,72,256]{2,1,0:T(8,128)(2,1)}, bf16[16,72,256]{2,1,0:T(8,128)(2,1)}, u32[]{:S(2)}, u32[]{:S(2)}) collective-permute-start(bf16[16,72,256]{2,1,0:T(8,128)(2,1)} %collective-permute-done.34.refs_16_), channel_id=1, source_target_pairs={{0,32},{32,0},{64,96},{96,64},{128,160},{160,128},{192,224},{224,1... | collective-permute-start | bytes 1769480 | tf_op jit(solution)/shard_map/ppermute | solution.py:36
  137.8 2.4 %collective-permute-start.40 = (bf16[16,72,256]{2,1,0:T(8,128)(2,1)}, bf16[16,72,256]{2,1,0:T(8,128)(2,1)}, u32[]{:S(2)}, u32[]{:S(2)}) collective-permute-start(bf16[16,72,256]{2,1,0:T(8,128)(2,1)} %collective-permute-done.36.refs_17_), channel_id=1, source_target_pairs={{0,32},{32,0},{64,96},{96,64},{128,160},{160,128},{192,224},{224,1... | collective-permute-start | bytes 1769480 | tf_op jit(solution)/shard_map/ppermute | solution.py:36
  140.8 1.3 collective-permute-done.40.refs_22_
  143.1 12.5 %shard_map.76 = bf16[512,512]{1,0:T(8,128)(2,1)} custom-call(s32[32,128]{1,0:T(8,128)} %copy-done.2, s32[2]{0:T(128)} %live_ref.2, s32[1]{0:T(128)} %bitcast.1.share_ref.pair_ref, bf16[4,208,256]{2,1,0:T(8,128)(2,1)} %bitcast.32, bf16[4,208,256]{2,1,0:T(8,128)(2,1)} %bitcast.33, bf16[4,208,256]{2,1,0:T(8,128)(2,1)} %bitcast.34, ...), custom_call_target="tpu_custom_call" | custom-call | tf_op jit(solution)/shard_map/pallas_call | solution.py:228
  155.7 2.0 %reshape.79 = bf16[512,2,256]{2,1,0:T(2,128)(2,1)} reshape(bf16[512,512]{1,0:T(8,128)(2,1)} %shard_map.76) | data formatting | bytes 1048576 | tf_op jit(solution)/shard_map/reshape | solution.py:308
  (105 shorter events, 11.8 us)
Async XLA Ops:
  0.0 16.0 %collective-permute-start = (bf16[512,256]{1,0:T(8,128)(2,1)}, bf16[512,256]{1,0:T(8,128)(2,1)S(1)}, u32[]{:S(2)}, u32[]{:S(2)}) collective-permute-start(bf16[512,256]{1,0:T(8,128)(2,1)} %bitcast.22), channel_id=1, source_target_pairs={{0,64},{32,96},{64,128},{96,160},{128,192},{160,224},{192,0},{224,... | collective-permute-start | bytes 786440 | tf_op jit(solution)/shard_map/ppermute | solution.py:28
  2.0 14.0 %collective-permute-start.3 = (bf16[512,256]{1,0:T(8,128)(2,1)}, bf16[512,256]{1,0:T(8,128)(2,1)S(1)}, u32[]{:S(2)}, u32[]{:S(2)}) collective-permute-start(bf16[512,256]{1,0:T(8,128)(2,1)} %bitcast.23), channel_id=1, source_target_pairs={{0,192},{32,224},{64,0},{96,32},{128,64},{160,96},{192,128},{224,1... | collective-permute-start | bytes 786440 | tf_op jit(solution)/shard_map/ppermute | solution.py:28
  4.3 8.9 %collective-permute-start.1 = (bf16[256,256]{1,0:T(8,128)(2,1)S(1)}, bf16[256,256]{1,0:T(8,128)(2,1)S(1)}, u32[]{:S(2)}, u32[]{:S(2)}) collective-permute-start(bf16[256,256]{1,0:T(8,128)(2,1)S(1)} %get-tuple-element.40), channel_id=1, source_target_pairs={{0,128},{32,160},{64,192},{96,224},{128,0},{160,32},{192,64},{224,... | collective-permute-start | bytes 393224 | tf_op jit(solution)/shard_map/ppermute | solution.py:28
  6.1 9.9 %collective-permute-start.2 = (bf16[256,256]{1,0:T(8,128)(2,1)S(1)}, bf16[256,256]{1,0:T(8,128)(2,1)S(1)}, u32[]{:S(2)}, u32[]{:S(2)}) collective-permute-start(bf16[256,256]{1,0:T(8,128)(2,1)S(1)} %get-tuple-element.39), channel_id=1, source_target_pairs={{0,128},{32,160},{64,192},{96,224},{128,0},{160,32},{192,64},{224,... | collective-permute-start | bytes 393224 | tf_op jit(solution)/shard_map/ppermute | solution.py:28
  16.0 59.1 %all-to-all-start = ((bf16[32,72,256]{2,1,0:T(8,128)(2,1)}), bf16[32,72,256]{2,1,0:T(8,128)(2,1)S(1)}, u32[]{:S(2)}, u32[]{:S(2)}) async-start(bf16[32,72,256]{2,1,0:T(8,128)(2,1)} %shard_map.73), calls=%async_computation | async-start | bytes 2359296 | tf_op jit(solution)/shard_map/all_to_all | solution.py:264
  27.3 3.6 %collective-permute-start.4 = (bf16[512,256]{1,0:T(8,128)(2,1)S(1)}, bf16[512,256]{1,0:T(8,128)(2,1)S(1)}, u32[]{:S(2)}, u32[]{:S(2)}) collective-permute-start(bf16[512,256]{1,0:T(8,128)(2,1)S(1)} %bitcast.24), channel_id=1, source_target_pairs={{0,32},{32,0},{64,96},{96,64},{128,160},{160,128},{192,224},{224,1... | collective-permute-start | bytes 786440 | tf_op jit(solution)/shard_map/ppermute | solution.py:36
  29.2 2.3 %collective-permute-start.5 = (bf16[512,256]{1,0:T(8,128)(2,1)S(1)}, bf16[512,256]{1,0:T(8,128)(2,1)S(1)}, u32[]{:S(2)}, u32[]{:S(2)}) collective-permute-start(bf16[512,256]{1,0:T(8,128)(2,1)S(1)} %collective-permute-done.refs_1_), channel_id=1, source_target_pairs={{0,32},{32,0},{64,96},{96,64},{128,160},{160,128},{192,224},{224,1... | collective-permute-start | bytes 786440 | tf_op jit(solution)/shard_map/ppermute | solution.py:36
  29.3 2.2 %collective-permute-start.8 = (bf16[512,256]{1,0:T(8,128)(2,1)S(1)}, bf16[512,256]{1,0:T(8,128)(2,1)S(1)}, u32[]{:S(2)}, u32[]{:S(2)}) collective-permute-start(bf16[512,256]{1,0:T(8,128)(2,1)S(1)} %collective-permute-done.3.refs_4_), channel_id=1, source_target_pairs={{0,32},{32,0},{64,96},{96,64},{128,160},{160,128},{192,224},{224,1... | collective-permute-start | bytes 786440 | tf_op jit(solution)/shard_map/ppermute | solution.py:36
  29.7 1.6 %collective-permute-start.6 = (bf16[256,256]{1,0:T(8,128)(2,1)S(1)}, bf16[256,256]{1,0:T(8,128)(2,1)S(1)}, u32[]{:S(2)}, u32[]{:S(2)}) collective-permute-start(bf16[256,256]{1,0:T(8,128)(2,1)S(1)} %collective-permute-done.1.refs_2_), channel_id=1, source_target_pairs={{0,32},{32,0},{64,96},{96,64},{128,160},{160,128},{192,224},{224,1... | collective-permute-start | bytes 393224 | tf_op jit(solution)/shard_map/ppermute | solution.py:36
  29.8 1.7 %collective-permute-start.7 = (bf16[256,256]{1,0:T(8,128)(2,1)S(1)}, bf16[256,256]{1,0:T(8,128)(2,1)S(1)}, u32[]{:S(2)}, u32[]{:S(2)}) collective-permute-start(bf16[256,256]{1,0:T(8,128)(2,1)S(1)} %collective-permute-done.2.refs_3_), channel_id=1, source_target_pairs={{0,32},{32,0},{64,96},{96,64},{128,160},{160,128},{192,224},{224,1... | collective-permute-start | bytes 393224 | tf_op jit(solution)/shard_map/ppermute | solution.py:36
  33.3 8.1 %collective-permute-start.9 = (bf16[208,256]{1,0:T(8,128)(2,1)S(1)}, bf16[208,256]{1,0:T(8,128)(2,1)S(1)}, u32[]{:S(2)}, u32[]{:S(2)}) collective-permute-start(bf16[208,256]{1,0:T(8,128)(2,1)S(1)} %get-tuple-element.23), channel_id=1, source_target_pairs={{0,1},{1,2},{2,3},{3,0},{4,5},{5,6},{6,7},{7,4},{8,9},{9,10},{10,1... | collective-permute-start | bytes 319496 | tf_op jit(solution)/shard_map/ppermute | solution.py:28
  34.8 13.0 %collective-permute-start.12 = (bf16[208,256]{1,0:T(8,128)(2,1)S(1)}, bf16[208,256]{1,0:T(8,128)(2,1)S(1)}, u32[]{:S(2)}, u32[]{:S(2)}) collective-permute-start(bf16[208,256]{1,0:T(8,128)(2,1)S(1)} %get-tuple-element.23), channel_id=1, source_target_pairs={{0,3},{1,0},{2,1},{3,2},{4,7},{5,4},{6,5},{7,6},{8,11},{9,8},{10,9... | collective-permute-start | bytes 319496 | tf_op jit(solution)/shard_map/ppermute | solution.py:28
  36.2 20.8 %collective-permute-start.13 = (bf16[304,256]{1,0:T(8,128)(2,1)S(1)}, bf16[304,256]{1,0:T(8,128)(2,1)S(1)}, u32[]{:S(2)}, u32[]{:S(2)}) collective-permute-start(bf16[304,256]{1,0:T(8,128)(2,1)S(1)} %get-tuple-element.24), channel_id=1, source_target_pairs={{0,4},{1,5},{2,6},{3,7},{4,8},{5,9},{6,10},{7,11},{8,12},{9,13},{1... | collective-permute-start | bytes 466952 | tf_op jit(solution)/shard_map/ppermute | solution.py:28
  37.5 19.4 %collective-permute-start.14 = (bf16[304,256]{1,0:T(8,128)(2,1)S(1)}, bf16[304,256]{1,0:T(8,128)(2,1)S(1)}, u32[]{:S(2)}, u32[]{:S(2)}) collective-permute-start(bf16[304,256]{1,0:T(8,128)(2,1)S(1)} %get-tuple-element.24), channel_id=1, source_target_pairs={{0,28},{1,29},{2,30},{3,31},{4,0},{5,1},{6,2},{7,3},{8,4},{9,5},{1... | collective-permute-start | bytes 466952 | tf_op jit(solution)/shard_map/ppermute | solution.py:28
  38.8 6.0 %collective-permute-start.10 = (bf16[104,256]{1,0:T(8,128)(2,1)S(1)}, bf16[104,256]{1,0:T(8,128)(2,1)S(1)}, u32[]{:S(2)}, u32[]{:S(2)}) collective-permute-start(bf16[104,256]{1,0:T(8,128)(2,1)S(1)} %get-tuple-element.42), channel_id=1, source_target_pairs={{0,2},{1,3},{2,0},{3,1},{4,6},{5,7},{6,4},{7,5},{8,10},{9,11},{10,... | collective-permute-start | bytes 159752 | tf_op jit(solution)/shard_map/ppermute | solution.py:28
  41.3 6.5 %collective-permute-start.11 = (bf16[104,256]{1,0:T(8,128)(2,1)S(1)}, bf16[104,256]{1,0:T(8,128)(2,1)S(1)}, u32[]{:S(2)}, u32[]{:S(2)}) collective-permute-start(bf16[104,256]{1,0:T(8,128)(2,1)S(1)} %get-tuple-element.41), channel_id=1, source_target_pairs={{0,2},{1,3},{2,0},{3,1},{4,6},{5,7},{6,4},{7,5},{8,10},{9,11},{10,... | collective-permute-start | bytes 159752 | tf_op jit(solution)/shard_map/ppermute | solution.py:28
  47.8 43.2 %copy-start.11 = (bf16[832,256]{1,0:T(8,128)(2,1)}, bf16[832,256]{1,0:T(8,128)(2,1)S(1)}, u32[]{:S(2)}) copy-start(bf16[832,256]{1,0:T(8,128)(2,1)S(1)} %constant_dynamic-update-slice_fusion) | copy-start | bytes 1277956
  56.9 21.3 %collective-permute-start.15 = (bf16[832,256]{1,0:T(8,128)(2,1)S(1)}, bf16[832,256]{1,0:T(8,128)(2,1)S(1)}, u32[]{:S(2)}, u32[]{:S(2)}) collective-permute-start(bf16[832,256]{1,0:T(8,128)(2,1)S(1)} %constant_dynamic-update-slice_fusion), channel_id=1, source_target_pairs={{0,4},{1,5},{2,6},{3,7},{4,8},{5,9},{6,10},{7,11},{8,12},{9,13},{1... | collective-permute-start | bytes 1277960 | tf_op jit(solution)/shard_map/ppermute | solution.py:28
  57.1 12.6 %collective-permute-start.16 = (bf16[304,256]{1,0:T(8,128)(2,1)S(1)}, bf16[304,256]{1,0:T(8,128)(2,1)S(1)}, u32[]{:S(2)}, u32[]{:S(2)}) collective-permute-start(bf16[304,256]{1,0:T(8,128)(2,1)S(1)} %collective-permute-done.13), channel_id=1, source_target_pairs={{0,4},{1,5},{2,6},{3,7},{4,8},{5,9},{6,10},{7,11},{8,12},{9,13},{1... | collective-permute-start | bytes 466952 | tf_op jit(solution)/shard_map/ppermute | solution.py:28
  58.6 11.2 %collective-permute-start.18 = (bf16[304,256]{1,0:T(8,128)(2,1)S(1)}, bf16[304,256]{1,0:T(8,128)(2,1)}, u32[]{:S(2)}, u32[]{:S(2)}) collective-permute-start(bf16[304,256]{1,0:T(8,128)(2,1)S(1)} %collective-permute-done.14), channel_id=1, source_target_pairs={{0,28},{1,29},{2,30},{3,31},{4,0},{5,1},{6,2},{7,3},{8,4},{9,5},{1... | collective-permute-start | bytes 466952 | tf_op jit(solution)/shard_map/ppermute | solution.py:28
  59.8 31.5 %collective-permute-start.25 = (bf16[832,256]{1,0:T(8,128)(2,1)S(1)}, bf16[832,256]{1,0:T(8,128)(2,1)}, u32[]{:S(2)}, u32[]{:S(2)}) collective-permute-start(bf16[832,256]{1,0:T(8,128)(2,1)S(1)} %constant_dynamic-update-slice_fusion), channel_id=1, source_target_pairs={{0,28},{1,29},{2,30},{3,31},{4,0},{5,1},{6,2},{7,3},{8,4},{9,5},{1... | collective-permute-start | bytes 1277960 | tf_op jit(solution)/shard_map/ppermute | solution.py:28
  69.7 5.4 %collective-permute-start.17 = (bf16[304,256]{1,0:T(8,128)(2,1)S(1)}, bf16[304,256]{1,0:T(8,128)(2,1)}, u32[]{:S(2)}, u32[]{:S(2)}) collective-permute-start(bf16[304,256]{1,0:T(8,128)(2,1)S(1)} %collective-permute-done.16), channel_id=1, source_target_pairs={{0,4},{1,5},{2,6},{3,7},{4,8},{5,9},{6,10},{7,11},{8,12},{9,13},{1... | collective-permute-start | bytes 466952 | tf_op jit(solution)/shard_map/ppermute | solution.py:28
  69.8 7.6 %collective-permute-start.19 = (bf16[304,256]{1,0:T(8,128)(2,1)}, bf16[304,256]{1,0:T(8,128)(2,1)S(1)}, u32[]{:S(2)}, u32[]{:S(2)}) collective-permute-start(bf16[304,256]{1,0:T(8,128)(2,1)} %collective-permute-done.18), channel_id=1, source_target_pairs={{0,28},{1,29},{2,30},{3,31},{4,0},{5,1},{6,2},{7,3},{8,4},{9,5},{1... | collective-permute-start | bytes 466952 | tf_op jit(solution)/shard_map/ppermute | solution.py:28
  75.1 65.0 %copy-start = (bf16[32,72,256]{2,1,0:T(8,128)(2,1)}, bf16[32,72,256]{2,1,0:T(8,128)(2,1)S(1)}, u32[]{:S(2)}) copy-start(bf16[32,72,256]{2,1,0:T(8,128)(2,1)S(1)} %all-to-all-done.got_ref.refs_14_) | copy-start | bytes 3538948
  78.3 30.2 %copy-start.12 = (bf16[832,256]{1,0:T(8,128)(2,1)}, bf16[832,256]{1,0:T(8,128)(2,1)S(1)}, u32[]{:S(2)}) copy-start(bf16[832,256]{1,0:T(8,128)(2,1)S(1)} %collective-permute-done.15) | copy-start | bytes 1277956
  78.3 14.2 %collective-permute-start.20 = (bf16[832,256]{1,0:T(8,128)(2,1)S(1)}, bf16[832,256]{1,0:T(8,128)(2,1)S(1)}, u32[]{:S(2)}, u32[]{:S(2)}) collective-permute-start(bf16[832,256]{1,0:T(8,128)(2,1)S(1)} %collective-permute-done.15), channel_id=1, source_target_pairs={{0,4},{1,5},{2,6},{3,7},{4,8},{5,9},{6,10},{7,11},{8,12},{9,13},{1... | collective-permute-start | bytes 1277960 | tf_op jit(solution)/shard_map/ppermute | solution.py:28
  79.5 10.0 %collective-permute-start.21 = (bf16[152,256]{1,0:T(8,128)(2,1)S(1)}, bf16[152,256]{1,0:T(8,128)(2,1)S(1)}, u32[]{:S(2)}, u32[]{:S(2)}) collective-permute-start(bf16[152,256]{1,0:T(8,128)(2,1)S(1)} %slice.48), channel_id=1, source_target_pairs={{0,4},{1,5},{2,6},{3,7},{4,8},{5,9},{6,10},{7,11},{8,12},{9,13},{1... | collective-permute-start | bytes 233480 | tf_op jit(solution)/shard_map/ppermute | solution.py:28
  80.7 9.3 %collective-permute-start.22 = (bf16[152,256]{1,0:T(8,128)(2,1)S(1)}, bf16[152,256]{1,0:T(8,128)(2,1)S(1)}, u32[]{:S(2)}, u32[]{:S(2)}) collective-permute-start(bf16[152,256]{1,0:T(8,128)(2,1)S(1)} %slice.49), channel_id=1, source_target_pairs={{0,28},{1,29},{2,30},{3,31},{4,0},{5,1},{6,2},{7,3},{8,4},{9,5},{1... | collective-permute-start | bytes 233480 | tf_op jit(solution)/shard_map/ppermute | solution.py:28
  82.2 24.9 %collective-permute-start.33 = (bf16[32,72,256]{2,1,0:T(8,128)(2,1)S(1)}, bf16[32,72,256]{2,1,0:T(8,128)(2,1)}, u32[]{:S(2)}, u32[]{:S(2)}) collective-permute-start(bf16[32,72,256]{2,1,0:T(8,128)(2,1)S(1)} %all-to-all-done.got_ref.refs_14_), channel_id=1, source_target_pairs={{0,64},{32,96},{64,128},{96,160},{128,192},{160,224},{192,0},{224,... | collective-permute-start | bytes 3538952 | tf_op jit(solution)/shard_map/ppermute | solution.py:28
  89.5 23.6 %collective-permute-start.35 = (bf16[32,72,256]{2,1,0:T(8,128)(2,1)S(1)}, bf16[32,72,256]{2,1,0:T(8,128)(2,1)}, u32[]{:S(2)}, u32[]{:S(2)}) collective-permute-start(bf16[32,72,256]{2,1,0:T(8,128)(2,1)S(1)} %all-to-all-done.got_ref.refs_14_), channel_id=1, source_target_pairs={{0,192},{32,224},{64,0},{96,32},{128,64},{160,96},{192,128},{224,1... | collective-permute-start | bytes 3538952 | tf_op jit(solution)/shard_map/ppermute | solution.py:28
  91.0 25.9 %copy-start.6 = (bf16[2432,256]{1,0:T(8,128)(2,1)}, bf16[2432,256]{1,0:T(8,128)(2,1)S(1)}, u32[]{:S(2)}) copy-start(bf16[2432,256]{1,0:T(8,128)(2,1)S(1)} %constant_dynamic-update-slice_fusion.5) | copy-start | bytes 3735556
  91.0 26.9 %collective-permute-start.29 = (bf16[2432,256]{1,0:T(8,128)(2,1)S(1)}, bf16[2432,256]{1,0:T(8,128)(2,1)S(1)}, u32[]{:S(2)}, u32[]{:S(2)}) collective-permute-start(bf16[2432,256]{1,0:T(8,128)(2,1)S(1)} %constant_dynamic-update-slice_fusion.5), channel_id=1, source_target_pairs={{0,1},{1,2},{2,3},{3,0},{4,5},{5,6},{6,7},{7,4},{8,9},{9,10},{10,1... | collective-permute-start | bytes 3735560 | tf_op jit(solution)/shard_map/ppermute | solution.py:28
  91.3 8.0 %collective-permute-start.26 = (bf16[832,256]{1,0:T(8,128)(2,1)}, bf16[832,256]{1,0:T(8,128)(2,1)S(1)}, u32[]{:S(2)}, u32[]{:S(2)}) collective-permute-start(bf16[832,256]{1,0:T(8,128)(2,1)} %collective-permute-done.25), channel_id=1, source_target_pairs={{0,28},{1,29},{2,30},{3,31},{4,0},{5,1},{6,2},{7,3},{8,4},{9,5},{1... | collective-permute-start | bytes 1277960 | tf_op jit(solution)/shard_map/ppermute | solution.py:28
  92.5 24.5 %copy-start.13 = (bf16[832,256]{1,0:T(8,128)(2,1)}, bf16[832,256]{1,0:T(8,128)(2,1)S(1)}, u32[]{:S(2)}) copy-start(bf16[832,256]{1,0:T(8,128)(2,1)S(1)} %collective-permute-done.20) | copy-start | bytes 1277956
  92.5 27.4 %collective-permute-start.31 = (bf16[2432,256]{1,0:T(8,128)(2,1)S(1)}, bf16[2432,256]{1,0:T(8,128)(2,1)S(1)}, u32[]{:S(2)}, u32[]{:S(2)}) collective-permute-start(bf16[2432,256]{1,0:T(8,128)(2,1)S(1)} %constant_dynamic-update-slice_fusion.5), channel_id=1, source_target_pairs={{0,3},{1,0},{2,1},{3,2},{4,7},{5,4},{6,5},{7,6},{8,11},{9,8},{10,9... | collective-permute-start | bytes 3735560 | tf_op jit(solution)/shard_map/ppermute | solution.py:28
  99.4 15.2 %collective-permute-start.23 = (bf16[832,256]{1,0:T(8,128)(2,1)S(1)}, bf16[832,256]{1,0:T(8,128)(2,1)S(1)}, u32[]{:S(2)}, u32[]{:S(2)}) collective-permute-start(bf16[832,256]{1,0:T(8,128)(2,1)S(1)} %collective-permute-done.20), channel_id=1, source_target_pairs={{0,4},{1,5},{2,6},{3,7},{4,8},{5,9},{6,10},{7,11},{8,12},{9,13},{1... | collective-permute-start | bytes 1277960 | tf_op jit(solution)/shard_map/ppermute | solution.py:28
  107.1 9.9 %collective-permute-start.27 = (bf16[832,256]{1,0:T(8,128)(2,1)S(1)}, bf16[832,256]{1,0:T(8,128)(2,1)S(1)}, u32[]{:S(2)}, u32[]{:S(2)}) collective-permute-start(bf16[832,256]{1,0:T(8,128)(2,1)S(1)} %collective-permute-done.26), channel_id=1, source_target_pairs={{0,28},{1,29},{2,30},{3,31},{4,0},{5,1},{6,2},{7,3},{8,4},{9,5},{1... | collective-permute-start | bytes 1277960 | tf_op jit(solution)/shard_map/ppermute | solution.py:28
  113.0 19.1 %collective-permute-start.34 = (bf16[16,72,256]{2,1,0:T(8,128)(2,1)S(1)}, bf16[16,72,256]{2,1,0:T(8,128)(2,1)}, u32[]{:S(2)}, u32[]{:S(2)}) collective-permute-start(bf16[16,72,256]{2,1,0:T(8,128)(2,1)S(1)} %slice.54), channel_id=1, source_target_pairs={{0,64},{32,96},{64,128},{96,160},{128,192},{160,224},{192,0},{224,... | collective-permute-start | bytes 1769480 | tf_op jit(solution)/shard_map/ppermute | solution.py:28
  114.6 17.7 %collective-permute-start.36 = (bf16[16,72,256]{2,1,0:T(8,128)(2,1)S(1)}, bf16[16,72,256]{2,1,0:T(8,128)(2,1)}, u32[]{:S(2)}, u32[]{:S(2)}) collective-permute-start(bf16[16,72,256]{2,1,0:T(8,128)(2,1)S(1)} %slice.55), channel_id=1, source_target_pairs={{0,192},{32,224},{64,0},{96,32},{128,64},{160,96},{192,128},{224,1... | collective-permute-start | bytes 1769480 | tf_op jit(solution)/shard_map/ppermute | solution.py:28
  117.0 6.4 %collective-permute-start.24 = (bf16[416,256]{1,0:T(8,128)(2,1)S(1)}, bf16[416,256]{1,0:T(8,128)(2,1)S(1)}, u32[]{:S(2)}, u32[]{:S(2)}) collective-permute-start(bf16[416,256]{1,0:T(8,128)(2,1)S(1)} %slice.56), channel_id=1, source_target_pairs={{0,4},{1,5},{2,6},{3,7},{4,8},{5,9},{6,10},{7,11},{8,12},{9,13},{1... | collective-permute-start | bytes 638984 | tf_op jit(solution)/shard_map/ppermute | solution.py:28
  117.9 8.0 %collective-permute-start.28 = (bf16[416,256]{1,0:T(8,128)(2,1)S(1)}, bf16[416,256]{1,0:T(8,128)(2,1)S(1)}, u32[]{:S(2)}, u32[]{:S(2)}) collective-permute-start(bf16[416,256]{1,0:T(8,128)(2,1)S(1)} %slice.57), channel_id=1, source_target_pairs={{0,28},{1,29},{2,30},{3,31},{4,0},{5,1},{6,2},{7,3},{8,4},{9,5},{1... | collective-permute-start | bytes 638984 | tf_op jit(solution)/shard_map/ppermute | solution.py:28
  119.9 12.7 %collective-permute-start.30 = (bf16[1216,256]{1,0:T(8,128)(2,1)S(1)}, bf16[1216,256]{1,0:T(8,128)(2,1)}, u32[]{:S(2)}, u32[]{:S(2)}) collective-permute-start(bf16[1216,256]{1,0:T(8,128)(2,1)S(1)} %slice.58), channel_id=1, source_target_pairs={{0,1},{1,2},{2,3},{3,0},{4,5},{5,6},{6,7},{7,4},{8,9},{9,10},{10,1... | collective-permute-start | bytes 1867784 | tf_op jit(solution)/shard_map/ppermute | solution.py:28
  123.4 14.4 %collective-permute-start.32 = (bf16[1216,256]{1,0:T(8,128)(2,1)S(1)}, bf16[1216,256]{1,0:T(8,128)(2,1)}, u32[]{:S(2)}, u32[]{:S(2)}) collective-permute-start(bf16[1216,256]{1,0:T(8,128)(2,1)S(1)} %slice.59), channel_id=1, source_target_pairs={{0,3},{1,0},{2,1},{3,2},{4,7},{5,4},{6,5},{7,6},{8,11},{9,8},{10,9... | collective-permute-start | bytes 1867784 | tf_op jit(solution)/shard_map/ppermute | solution.py:28
  125.9 14.9 %collective-permute-start.37 = (bf16[32,72,256]{2,1,0:T(8,128)(2,1)S(1)}, bf16[32,72,256]{2,1,0:T(8,128)(2,1)S(1)}, u32[]{:S(2)}, u32[]{:S(2)}) collective-permute-start(bf16[32,72,256]{2,1,0:T(8,128)(2,1)S(1)} %all-to-all-done.got_ref.refs_14_), channel_id=1, source_target_pairs={{0,32},{32,0},{64,96},{96,64},{128,160},{160,128},{192,224},{224,1... | collective-permute-start | bytes 3538952 | tf_op jit(solution)/shard_map/ppermute | solution.py:36
  132.1 10.0 %collective-permute-start.38 = (bf16[32,72,256]{2,1,0:T(8,128)(2,1)}, bf16[32,72,256]{2,1,0:T(8,128)(2,1)S(1)}, u32[]{:S(2)}, u32[]{:S(2)}) collective-permute-start(bf16[32,72,256]{2,1,0:T(8,128)(2,1)} %collective-permute-done.33.refs_15_), channel_id=1, source_target_pairs={{0,32},{32,0},{64,96},{96,64},{128,160},{160,128},{192,224},{224,1... | collective-permute-start | bytes 3538952 | tf_op jit(solution)/shard_map/ppermute | solution.py:36
  132.3 9.9 %collective-permute-start.41 = (bf16[32,72,256]{2,1,0:T(8,128)(2,1)}, bf16[32,72,256]{2,1,0:T(8,128)(2,1)}, u32[]{:S(2)}, u32[]{:S(2)}) collective-permute-start(bf16[32,72,256]{2,1,0:T(8,128)(2,1)} %collective-permute-done.35.refs_18_), channel_id=1, source_target_pairs={{0,32},{32,0},{64,96},{96,64},{128,160},{160,128},{192,224},{224,1... | collective-permute-start | bytes 3538952 | tf_op jit(solution)/shard_map/ppermute | solution.py:36
  132.7 8.2 %collective-permute-start.39 = (bf16[16,72,256]{2,1,0:T(8,128)(2,1)}, bf16[16,72,256]{2,1,0:T(8,128)(2,1)}, u32[]{:S(2)}, u32[]{:S(2)}) collective-permute-start(bf16[16,72,256]{2,1,0:T(8,128)(2,1)} %collective-permute-done.34.refs_16_), channel_id=1, source_target_pairs={{0,32},{32,0},{64,96},{96,64},{128,160},{160,128},{192,224},{224,1... | collective-permute-start | bytes 1769480 | tf_op jit(solution)/shard_map/ppermute | solution.py:36
  137.8 4.3 %collective-permute-start.40 = (bf16[16,72,256]{2,1,0:T(8,128)(2,1)}, bf16[16,72,256]{2,1,0:T(8,128)(2,1)}, u32[]{:S(2)}, u32[]{:S(2)}) collective-permute-start(bf16[16,72,256]{2,1,0:T(8,128)(2,1)} %collective-permute-done.36.refs_17_), channel_id=1, source_target_pairs={{0,32},{32,0},{64,96},{96,64},{128,160},{160,128},{192,224},{224,1... | collective-permute-start | bytes 1769480 | tf_op jit(solution)/shard_map/ppermute | solution.py:36
  (14 other events, 132.6 us)

commit v5 on v4

--- a/solution.py
+++ b/solution.py
@@ -8,7 +8,7 @@
 from jax.sharding import PartitionSpec as P
 
 NX, NY, NZ = 4, 4, 8
-ROWS_A = 208
+ROWS_A = 224
 LABEL_ROWS = 8
 GROUP = 4
 
@@ -261,7 +261,7 @@
     ]
 
     routed = route(block_rows, block_cols, pair_id.reshape(1), integrals, owners, shares)
-    got = lax.all_to_all(after(routed, *pieces[1:]), "tile", split_axis=0, concat_axis=0, tiled=True)
+    got = lax.all_to_all(routed, "tile", split_axis=0, concat_axis=0, tiled=True)
 
     pieces += [other_core(p) for p in pieces]
     a, b = mirror_sum(pair_id.reshape(1), size_cd, mirror, pieces)
@@ -271,13 +271,13 @@
     ay = [a, send("y", 1, a), send("y", 2, a[:half]), send("y", -2, a[half:]), send("y", -1, a)]
     a0 = jnp.concatenate(ay, axis=0)
     b2, b6 = send("z", 1, b1), send("z", -1, b7)
-    a0 = after(a0, b1, b7)
+    a0 = after(a0, b2, b6)
     a1, a7 = send("z", 1, a0), send("z", -1, a0)
     b3, b5 = send("z", 1, b2), send("z", -1, b6)
     b3, b5 = after(b3, got), after(b5, got)
     half = b.shape[0] // 2
     b4 = [send("z", 1, b3[:half]), send("z", -1, b5[half:])]
-    a1, a7 = after(a1, b3, b5), after(a7, b3, b5)
+    a1, a7 = after(a1, *b4), after(a7, *b4)
     a2, a6 = send("z", 1, a1), send("z", -1, a7)
     b0 = jnp.concatenate([b, b1, b2, b3, *b4, b5, b6, b7], axis=0)
     by1, by3 = send("y", 1, b0), send("y", -1, b0)

time: 160 us -> 153 us (0.956); the launches traced: 158 us -> 153 us
  waiting for transfers between devices: 61.4 us -> 49.3 us
  local copies, waits for them, and re-layouts: 9.81 us -> 14.1 us
  starting transfers between devices: 67.9 us -> 69.8 us
    ppermute x32, waiting for transfers between devices: 59.4 us -> 47.3 us  [send(): lax.ppermute(piece, 'pair' if axis == 'x' else 'tile', ring_steps(axis, s...]
    ppermute x10, starting transfers between devices: 17.2 us -> 25.4 us  [other_core(): return lax.ppermute(piece, 'pair', [(p, p ^ 1) for p in range(2 * NX)])]
    ppermute x32, starting transfers between devices: 39.5 us -> 32.3 us  [send(): lax.ppermute(piece, 'pair' if axis == 'x' else 'tile', ring_steps(axis, s...]
    unnamed x50 -> x54, local copies, waits for them, and re-layouts: 3.61 us -> 10.6 us
    slice x2, local copies, waits for them, and re-layouts: 2.2 us -> 0.08 us  [local(): w2 = [send('x', 1, w1[:half]), send('x', -1, w3[half:])]]
  transfers between devices with their start and end apart: 43 -> 43, of which waited for: 18 -> 17; matrix products, arithmetic and copies ran while one was open for 4% -> 6% of each run, Pallas kernels for 3% -> 1%
where the time goes in v5:
time: 153 us
  starting transfers between devices  69.8 us (46%)
  waiting for transfers between devices  49.3 us (32%)
  Pallas kernels  18.5 us (12%)
  local copies, waits for them, and re-layouts  14.1 us (9%)
    ppermute x32, waiting for transfers between devices, send(): lax.ppermute(piece, 'pair' if axis == 'x' else 'tile', ring_steps(axis, s...  47.3 us
    ppermute x32, starting transfers between devices, send(): lax.ppermute(piece, 'pair' if axis == 'x' else 'tile', ring_steps(axis, s...  32.3 us
    ppermute x10, starting transfers between devices, other_core(): return lax.ppermute(piece, 'pair', [(p, p ^ 1) for p in range(2 * NX)])  25.4 us
    pallas_call x1, Pallas kernels, ladder(): pl.pallas_call(functools.partial(ladder_kernel, n_a=n_a, n_b=n_b), in_spe...  13.5 us
    all_to_all x1, starting transfers between devices, local(): lax.all_to_all(routed, 'tile', split_axis=0, concat_axis=0, tiled=True)  12.2 us
    unnamed x54, local copies, waits for them, and re-layouts  10.6 us
    pallas_call x1, Pallas kernels, route(): pl.pallas_call(route_kernel, grid_spec=pltpu.PrefetchScalarGridSpec(num_s...  3.15 us
  transfers between devices with their start and end apart: 43, of which 17 were waited for; matrix products, arithmetic and copies ran while one was open for 6% of the time, Pallas kernels for 1%

profile of v5, /device:TPU:1, one launch (start us, length us, event | category | flops | bytes accessed | tf_op | source)
XLA Modules:
  0.0 152.7 jit_solution(4855459961092444326)
XLA Ops:
  0.0 3.1 %shard_map.73 = bf16[32,72,256]{2,1,0:T(8,128)(2,1)} custom-call(s32[32]{0:T(128)} %rows_ref.1, s32[32]{0:T(128)} %cols_ref.1, s32[1]{0:T(128)} %bitcast.1.share_ref.pair_ref, bf16[32,256,256]{2,1,0:T(8,128)(2,1)} %w_ref.1), custom_call_target="tpu_custom_call" | custom-call | tf_op jit(solution)/shard_map/pallas_call | solution.py:61
  3.2 12.2 %all-to-all-start = ((bf16[32,72,256]{2,1,0:T(8,128)(2,1)}), bf16[32,72,256]{2,1,0:T(8,128)(2,1)S(1)}, u32[]{:S(2)}, u32[]{:S(2)}) async-start(bf16[32,72,256]{2,1,0:T(8,128)(2,1)} %shard_map.73), calls=%async_computation | async-start | bytes 2359296 | tf_op jit(solution)/shard_map/all_to_all | solution.py:264
  15.3 2.6 %collective-permute-start.3 = (bf16[512,256]{1,0:T(8,128)(2,1)S(1)}, bf16[512,256]{1,0:T(8,128)(2,1)S(1)}, u32[]{:S(2)}, u32[]{:S(2)}) collective-permute-start(bf16[512,256]{1,0:T(8,128)(2,1)S(1)} %bitcast.22), channel_id=1, source_target_pairs={{0,192},{32,224},{64,0},{96,32},{128,64},{160,96},{192,128},{224,1... | collective-permute-start | bytes 786440 | tf_op jit(solution)/shard_map/ppermute | solution.py:28
  17.9 1.2 collective-permute-start.4
  19.2 2.1 %collective-permute-start.2 = (bf16[256,256]{1,0:T(8,128)(2,1)S(1)}, bf16[256,256]{1,0:T(8,128)(2,1)S(1)}, u32[]{:S(2)}, u32[]{:S(2)}) collective-permute-start(bf16[256,256]{1,0:T(8,128)(2,1)S(1)} %get-tuple-element.37), channel_id=1, source_target_pairs={{0,128},{32,160},{64,192},{96,224},{128,0},{160,32},{192,64},{224,... | collective-permute-start | bytes 393224 | tf_op jit(solution)/shard_map/ppermute | solution.py:28
  21.3 1.0 collective-permute-start.1
  22.6 7.5 %collective-permute-start.8 = (bf16[512,256]{1,0:T(8,128)(2,1)S(1)}, bf16[512,256]{1,0:T(8,128)(2,1)S(1)}, u32[]{:S(2)}, u32[]{:S(2)}) collective-permute-start(bf16[512,256]{1,0:T(8,128)(2,1)S(1)} %collective-permute-done.3.refs_4_), channel_id=1, source_target_pairs={{0,32},{32,0},{64,96},{96,64},{128,160},{160,128},{192,224},{224,1... | collective-permute-start | bytes 786440 | tf_op jit(solution)/shard_map/ppermute | solution.py:36
  30.1 3.4 %collective-permute-start.5 = (bf16[512,256]{1,0:T(8,128)(2,1)S(1)}, bf16[512,256]{1,0:T(8,128)(2,1)S(1)}, u32[]{:S(2)}, u32[]{:S(2)}) collective-permute-start(bf16[512,256]{1,0:T(8,128)(2,1)S(1)} %collective-permute-done.refs_1_), channel_id=1, source_target_pairs={{0,32},{32,0},{64,96},{96,64},{128,160},{160,128},{192,224},{224,1... | collective-permute-start | bytes 786440 | tf_op jit(solution)/shard_map/ppermute | solution.py:36
  35.0 1.8 %shard_map.75 = (bf16[224,256]{1,0:T(8,128)(2,1)S(1)}, bf16[288,256]{1,0:T(8,128)(2,1)S(1)}) custom-call(s32[1]{0:T(128)} %bitcast.1.share_ref.pair_ref, s32[1]{0:T(128)S(6)} %copy.20.live_ref, s32[1,4096]{1,0:T(1,128)S(1)} %bitcast.26, bf16[512,256]{1,0:T(8,128)(2,1)S(1)} %bitcast.25, bf16[512,256]{1,0:T(8,128)(2,1)S(1)} %collective-permute-done.refs_1_, ...), custom_call_target="tpu_custom_call" | custom-call | tf_op jit(solution)/shard_map/pallas_call | solution.py:104
  36.8 2.5 %collective-permute-start.12 = (bf16[224,256]{1,0:T(8,128)(2,1)S(1)}, bf16[224,256]{1,0:T(8,128)(2,1)S(1)}, u32[]{:S(2)}, u32[]{:S(2)}) collective-permute-start(bf16[224,256]{1,0:T(8,128)(2,1)S(1)} %get-tuple-element.21), channel_id=1, source_target_pairs={{0,3},{1,0},{2,1},{3,2},{4,7},{5,4},{6,5},{7,6},{8,11},{9,8},{10,9... | collective-permute-start | bytes 344072 | tf_op jit(solution)/shard_map/ppermute | solution.py:28
  39.3 2.5 %collective-permute-start.15 = (bf16[288,256]{1,0:T(8,128)(2,1)S(1)}, bf16[288,256]{1,0:T(8,128)(2,1)S(1)}, u32[]{:S(2)}, u32[]{:S(2)}) collective-permute-start(bf16[288,256]{1,0:T(8,128)(2,1)S(1)} %get-tuple-element.22), channel_id=1, source_target_pairs={{0,28},{1,29},{2,30},{3,31},{4,0},{5,1},{6,2},{7,3},{8,4},{9,5},{1... | collective-permute-start | bytes 442376 | tf_op jit(solution)/shard_map/ppermute | solution.py:28
  41.8 1.8 %collective-permute-start.11 = (bf16[112,256]{1,0:T(8,128)(2,1)S(1)}, bf16[112,256]{1,0:T(8,128)(2,1)S(1)}, u32[]{:S(2)}, u32[]{:S(2)}) collective-permute-start(bf16[112,256]{1,0:T(8,128)(2,1)S(1)} %get-tuple-element.39), channel_id=1, source_target_pairs={{0,2},{1,3},{2,0},{3,1},{4,6},{5,7},{6,4},{7,5},{8,10},{9,11},{10,... | collective-permute-start | bytes 172040 | tf_op jit(solution)/shard_map/ppermute | solution.py:28
  44.3 3.0 %collective-permute-done.9 = bf16[224,256]{1,0:T(8,128)(2,1)S(1)} collective-permute-done((bf16[224,256]{1,0:T(8,128)(2,1)S(1)}, bf16[224,256]{1,0:T(8,128)(2,1)S(1)}, u32[]{:S(2)}, u32[]{:S(2)}) %collective-permute-start.9) | collective-permute-done | bytes 114720 | tf_op jit(solution)/shard_map/ppermute | solution.py:28
  47.3 0.7 constant_dynamic-update-slice_fusion.3
  47.9 3.9 %collective-permute-done.10 = bf16[112,256]{1,0:T(8,128)(2,1)S(1)} collective-permute-done((bf16[112,256]{1,0:T(8,128)(2,1)S(1)}, bf16[112,256]{1,0:T(8,128)(2,1)S(1)}, u32[]{:S(2)}, u32[]{:S(2)}) %collective-permute-start.10) | collective-permute-done | bytes 57376 | tf_op jit(solution)/shard_map/ppermute | solution.py:28
  53.0 1.0 collective-permute-start.14
  55.2 1.2 collective-permute-done.16
  56.4 1.7 %collective-permute-done.14 = bf16[288,256]{1,0:T(8,128)(2,1)S(1)} collective-permute-done((bf16[288,256]{1,0:T(8,128)(2,1)S(1)}, bf16[288,256]{1,0:T(8,128)(2,1)S(1)}, u32[]{:S(2)}, u32[]{:S(2)}) %collective-permute-start.14) | collective-permute-done | bytes 147488 | tf_op jit(solution)/shard_map/ppermute | solution.py:28
  58.2 1.5 collective-permute-start.17
  59.6 1.3 collective-permute-start.20
  61.2 8.7 %collective-permute-done.20 = bf16[288,256]{1,0:T(8,128)(2,1)S(1)} collective-permute-done((bf16[288,256]{1,0:T(8,128)(2,1)S(1)}, bf16[288,256]{1,0:T(8,128)(2,1)S(1)}, u32[]{:S(2)}, u32[]{:S(2)}) %collective-permute-start.20) | collective-permute-done | bytes 147488 | tf_op jit(solution)/shard_map/ppermute | solution.py:28
  69.9 1.0 collective-permute-done.18
  71.6 1.0 collective-permute-start.19
  72.6 4.5 %collective-permute-start.35 = (bf16[32,72,256]{2,1,0:T(8,128)(2,1)S(1)}, bf16[32,72,256]{2,1,0:T(8,128)(2,1)S(1)}, u32[]{:S(2)}, u32[]{:S(2)}) collective-permute-start(bf16[32,72,256]{2,1,0:T(8,128)(2,1)S(1)} %all-to-all-done.got_ref.refs_14_), channel_id=1, source_target_pairs={{0,192},{32,224},{64,0},{96,32},{128,64},{160,96},{192,128},{224,1... | collective-permute-start | bytes 3538952 | tf_op jit(solution)/shard_map/ppermute | solution.py:28
  77.1 0.9 constant_dynamic-update-slice_fusion.10
  78.0 1.0 copy-done.8
  79.2 2.6 %collective-permute-start.26 = (bf16[896,256]{1,0:T(8,128)(2,1)}, bf16[896,256]{1,0:T(8,128)(2,1)S(1)}, u32[]{:S(2)}, u32[]{:S(2)}) collective-permute-start(bf16[896,256]{1,0:T(8,128)(2,1)} %collective-permute-done.25), channel_id=1, source_target_pairs={{0,28},{1,29},{2,30},{3,31},{4,0},{5,1},{6,2},{7,3},{8,4},{9,5},{1... | collective-permute-start | bytes 1376264 | tf_op jit(solution)/shard_map/ppermute | solution.py:28
  83.1 1.6 %constant_dynamic-update-slice_fusion.7 = bf16[2304,256]{1,0:T(8,128)(2,1)} fusion(bf16[2304,256]{1,0:T(8,128)(2,1)} %constant_dynamic-update-slice_fusion.8, bf16[288,256]{1,0:T(8,128)(2,1)} %copy-done.14), kind=kLoop, calls=%fused_computation.9 | loop fusion | bytes 294912
  84.6 1.6 %constant_dynamic-update-slice_fusion.6 = bf16[2304,256]{1,0:T(8,128)(2,1)} fusion(bf16[2304,256]{1,0:T(8,128)(2,1)} %constant_dynamic-update-slice_fusion.7, bf16[288,256]{1,0:T(8,128)(2,1)} %copy-done.20), kind=kLoop, calls=%fused_computation.8 | loop fusion | bytes 294912
  86.2 0.7 constant_dynamic-update-slice_fusion.5
  86.9 1.0 collective-permute-done.22
  88.3 9.4 %collective-permute-done.35.refs_18_ = bf16[32,72,256]{2,1,0:T(8,128)(2,1)S(1)} collective-permute-done((bf16[32,72,256]{2,1,0:T(8,128)(2,1)S(1)}, bf16[32,72,256]{2,1,0:T(8,128)(2,1)S(1)}, u32[]{:S(2)}, u32[]{:S(2)}) %collective-permute-start.35) | collective-permute-done | bytes 1179680 | tf_op jit(solution)/shard_map/ppermute | solution.py:28
  97.8 2.0 %collective-permute-start.27 = (bf16[896,256]{1,0:T(8,128)(2,1)S(1)}, bf16[896,256]{1,0:T(8,128)(2,1)S(1)}, u32[]{:S(2)}, u32[]{:S(2)}) collective-permute-start(bf16[896,256]{1,0:T(8,128)(2,1)S(1)} %collective-permute-done.26), channel_id=1, source_target_pairs={{0,28},{1,29},{2,30},{3,31},{4,0},{5,1},{6,2},{7,3},{8,4},{9,5},{1... | collective-permute-start | bytes 1376264 | tf_op jit(solution)/shard_map/ppermute | solution.py:28
  99.8 3.1 %collective-permute-done.33.refs_15_ = bf16[32,72,256]{2,1,0:T(8,128)(2,1)S(1)} collective-permute-done((bf16[32,72,256]{2,1,0:T(8,128)(2,1)S(1)}, bf16[32,72,256]{2,1,0:T(8,128)(2,1)S(1)}, u32[]{:S(2)}, u32[]{:S(2)}) %collective-permute-start.33) | collective-permute-done | bytes 1179680 | tf_op jit(solution)/shard_map/ppermute | solution.py:28
  103.4 1.1 collective-permute-start.34
  104.5 0.9 collective-permute-done.27
  105.8 3.4 %collective-permute-done.31 = bf16[2304,256]{1,0:T(8,128)(2,1)S(1)} collective-permute-done((bf16[2304,256]{1,0:T(8,128)(2,1)}, bf16[2304,256]{1,0:T(8,128)(2,1)S(1)}, u32[]{:S(2)}, u32[]{:S(2)}) %collective-permute-start.31) | collective-permute-done | bytes 1179680 | tf_op jit(solution)/shard_map/ppermute | solution.py:28
  109.2 0.8 collective-permute-start.28
  110.1 7.6 %collective-permute-start.37 = (bf16[32,72,256]{2,1,0:T(8,128)(2,1)S(1)}, bf16[32,72,256]{2,1,0:T(8,128)(2,1)}, u32[]{:S(2)}, u32[]{:S(2)}) collective-permute-start(bf16[32,72,256]{2,1,0:T(8,128)(2,1)S(1)} %all-to-all-done.got_ref.refs_14_), channel_id=1, source_target_pairs={{0,32},{32,0},{64,96},{96,64},{128,160},{160,128},{192,224},{224,1... | collective-permute-start | bytes 3538952 | tf_op jit(solution)/shard_map/ppermute | solution.py:36
  117.9 1.4 collective-permute-start.30
  119.3 2.3 %collective-permute-start.41 = (bf16[32,72,256]{2,1,0:T(8,128)(2,1)S(1)}, bf16[32,72,256]{2,1,0:T(8,128)(2,1)}, u32[]{:S(2)}, u32[]{:S(2)}) collective-permute-start(bf16[32,72,256]{2,1,0:T(8,128)(2,1)S(1)} %collective-permute-done.35.refs_18_), channel_id=1, source_target_pairs={{0,32},{32,0},{64,96},{96,64},{128,160},{160,128},{192,224},{224,1... | collective-permute-start | bytes 3538952 | tf_op jit(solution)/shard_map/ppermute | solution.py:36
  121.8 9.7 %collective-permute-done.32 = bf16[1152,256]{1,0:T(8,128)(2,1)S(1)} collective-permute-done((bf16[1152,256]{1,0:T(8,128)(2,1)S(1)}, bf16[1152,256]{1,0:T(8,128)(2,1)S(1)}, u32[]{:S(2)}, u32[]{:S(2)}) %collective-permute-start.32) | collective-permute-done | bytes 589856 | tf_op jit(solution)/shard_map/ppermute | solution.py:28
  131.5 0.8 copy-done.11
  132.3 2.1 %collective-permute-start.40 = (bf16[16,72,256]{2,1,0:T(8,128)(2,1)}, bf16[16,72,256]{2,1,0:T(8,128)(2,1)}, u32[]{:S(2)}, u32[]{:S(2)}) collective-permute-start(bf16[16,72,256]{2,1,0:T(8,128)(2,1)} %collective-permute-done.36.refs_17_), channel_id=1, source_target_pairs={{0,32},{32,0},{64,96},{96,64},{128,160},{160,128},{192,224},{224,1... | collective-permute-start | bytes 1769480 | tf_op jit(solution)/shard_map/ppermute | solution.py:36
  135.7 0.7 collective-permute-done.40.refs_22_
  136.4 0.8 collective-permute-done.39.refs_21_
  137.2 13.5 %shard_map.76 = bf16[512,512]{1,0:T(8,128)(2,1)} custom-call(s32[32,128]{1,0:T(8,128)} %copy-done.2, s32[2]{0:T(128)} %live_ref.2, s32[1]{0:T(128)} %bitcast.1.share_ref.pair_ref, bf16[4,224,256]{2,1,0:T(8,128)(2,1)} %bitcast.6.refs_0_, bf16[4,224,256]{2,1,0:T(8,128)(2,1)} %bitcast.7.refs_1_, bf16[4,224,256]{2,1,0:T(8,128)(2,1)} %bitcast.33, ...), custom_call_target="tpu_custom_call" | custom-call | tf_op jit(solution)/shard_map/pallas_call | solution.py:228
  150.8 2.0 %reshape.79 = bf16[512,2,256]{2,1,0:T(2,128)(2,1)} reshape(bf16[512,512]{1,0:T(8,128)(2,1)} %shard_map.76) | data formatting | bytes 1048576 | tf_op jit(solution)/shard_map/reshape | solution.py:308
  (109 shorter events, 9.7 us)
Async XLA Ops:
  3.2 31.8 %copy-start.3 = (s32[4096]{0:T(1024)S(1)}, s32[4096]{0:T(1024)}, u32[]{:S(2)}) copy-start(s32[4096]{0:T(1024)} %param.13) | copy-start | bytes 49156
  3.2 66.7 %all-to-all-start = ((bf16[32,72,256]{2,1,0:T(8,128)(2,1)}), bf16[32,72,256]{2,1,0:T(8,128)(2,1)S(1)}, u32[]{:S(2)}, u32[]{:S(2)}) async-start(bf16[32,72,256]{2,1,0:T(8,128)(2,1)} %shard_map.73), calls=%async_computation | async-start | bytes 2359296 | tf_op jit(solution)/shard_map/all_to_all | solution.py:264
  15.3 7.2 %collective-permute-start.3 = (bf16[512,256]{1,0:T(8,128)(2,1)S(1)}, bf16[512,256]{1,0:T(8,128)(2,1)S(1)}, u32[]{:S(2)}, u32[]{:S(2)}) collective-permute-start(bf16[512,256]{1,0:T(8,128)(2,1)S(1)} %bitcast.22), channel_id=1, source_target_pairs={{0,192},{32,224},{64,0},{96,32},{128,64},{160,96},{192,128},{224,1... | collective-permute-start | bytes 786440 | tf_op jit(solution)/shard_map/ppermute | solution.py:28
  17.9 12.2 %collective-permute-start = (bf16[512,256]{1,0:T(8,128)(2,1)S(1)}, bf16[512,256]{1,0:T(8,128)(2,1)S(1)}, u32[]{:S(2)}, u32[]{:S(2)}) collective-permute-start(bf16[512,256]{1,0:T(8,128)(2,1)S(1)} %bitcast.23), channel_id=1, source_target_pairs={{0,64},{32,96},{64,128},{96,160},{128,192},{160,224},{192,0},{224,... | collective-permute-start | bytes 786440 | tf_op jit(solution)/shard_map/ppermute | solution.py:28
  17.9 17.1 %collective-permute-start.4 = (bf16[512,256]{1,0:T(8,128)(2,1)S(1)}, bf16[512,256]{1,0:T(8,128)(2,1)S(1)}, u32[]{:S(2)}, u32[]{:S(2)}) collective-permute-start(bf16[512,256]{1,0:T(8,128)(2,1)S(1)} %bitcast.24), channel_id=1, source_target_pairs={{0,32},{32,0},{64,96},{96,64},{128,160},{160,128},{192,224},{224,1... | collective-permute-start | bytes 786440 | tf_op jit(solution)/shard_map/ppermute | solution.py:36
  19.2 14.3 %collective-permute-start.2 = (bf16[256,256]{1,0:T(8,128)(2,1)S(1)}, bf16[256,256]{1,0:T(8,128)(2,1)S(1)}, u32[]{:S(2)}, u32[]{:S(2)}) collective-permute-start(bf16[256,256]{1,0:T(8,128)(2,1)S(1)} %get-tuple-element.37), channel_id=1, source_target_pairs={{0,128},{32,160},{64,192},{96,224},{128,0},{160,32},{192,64},{224,... | collective-permute-start | bytes 393224 | tf_op jit(solution)/shard_map/ppermute | solution.py:28
  21.3 12.2 %collective-permute-start.1 = (bf16[256,256]{1,0:T(8,128)(2,1)S(1)}, bf16[256,256]{1,0:T(8,128)(2,1)S(1)}, u32[]{:S(2)}, u32[]{:S(2)}) collective-permute-start(bf16[256,256]{1,0:T(8,128)(2,1)S(1)} %get-tuple-element.38), channel_id=1, source_target_pairs={{0,128},{32,160},{64,192},{96,224},{128,0},{160,32},{192,64},{224,... | collective-permute-start | bytes 393224 | tf_op jit(solution)/shard_map/ppermute | solution.py:28
  22.6 12.4 %collective-permute-start.8 = (bf16[512,256]{1,0:T(8,128)(2,1)S(1)}, bf16[512,256]{1,0:T(8,128)(2,1)S(1)}, u32[]{:S(2)}, u32[]{:S(2)}) collective-permute-start(bf16[512,256]{1,0:T(8,128)(2,1)S(1)} %collective-permute-done.3.refs_4_), channel_id=1, source_target_pairs={{0,32},{32,0},{64,96},{96,64},{128,160},{160,128},{192,224},{224,1... | collective-permute-start | bytes 786440 | tf_op jit(solution)/shard_map/ppermute | solution.py:36
  30.1 4.9 %collective-permute-start.5 = (bf16[512,256]{1,0:T(8,128)(2,1)S(1)}, bf16[512,256]{1,0:T(8,128)(2,1)S(1)}, u32[]{:S(2)}, u32[]{:S(2)}) collective-permute-start(bf16[512,256]{1,0:T(8,128)(2,1)S(1)} %collective-permute-done.refs_1_), channel_id=1, source_target_pairs={{0,32},{32,0},{64,96},{96,64},{128,160},{160,128},{192,224},{224,1... | collective-permute-start | bytes 786440 | tf_op jit(solution)/shard_map/ppermute | solution.py:36
  33.5 1.3 collective-permute-start.7
  33.5 1.5 %collective-permute-start.6 = (bf16[256,256]{1,0:T(8,128)(2,1)S(1)}, bf16[256,256]{1,0:T(8,128)(2,1)S(1)}, u32[]{:S(2)}, u32[]{:S(2)}) collective-permute-start(bf16[256,256]{1,0:T(8,128)(2,1)S(1)} %collective-permute-done.1.refs_2_), channel_id=1, source_target_pairs={{0,32},{32,0},{64,96},{96,64},{128,160},{160,128},{192,224},{224,1... | collective-permute-start | bytes 393224 | tf_op jit(solution)/shard_map/ppermute | solution.py:36
  36.8 17.7 %collective-permute-start.12 = (bf16[224,256]{1,0:T(8,128)(2,1)S(1)}, bf16[224,256]{1,0:T(8,128)(2,1)S(1)}, u32[]{:S(2)}, u32[]{:S(2)}) collective-permute-start(bf16[224,256]{1,0:T(8,128)(2,1)S(1)} %get-tuple-element.21), channel_id=1, source_target_pairs={{0,3},{1,0},{2,1},{3,2},{4,7},{5,4},{6,5},{7,6},{8,11},{9,8},{10,9... | collective-permute-start | bytes 344072 | tf_op jit(solution)/shard_map/ppermute | solution.py:28
  39.3 8.0 %collective-permute-start.9 = (bf16[224,256]{1,0:T(8,128)(2,1)S(1)}, bf16[224,256]{1,0:T(8,128)(2,1)S(1)}, u32[]{:S(2)}, u32[]{:S(2)}) collective-permute-start(bf16[224,256]{1,0:T(8,128)(2,1)S(1)} %get-tuple-element.21), channel_id=1, source_target_pairs={{0,1},{1,2},{2,3},{3,0},{4,5},{5,6},{6,7},{7,4},{8,9},{9,10},{10,1... | collective-permute-start | bytes 344072 | tf_op jit(solution)/shard_map/ppermute | solution.py:28
  39.3 13.1 %collective-permute-start.15 = (bf16[288,256]{1,0:T(8,128)(2,1)S(1)}, bf16[288,256]{1,0:T(8,128)(2,1)S(1)}, u32[]{:S(2)}, u32[]{:S(2)}) collective-permute-start(bf16[288,256]{1,0:T(8,128)(2,1)S(1)} %get-tuple-element.22), channel_id=1, source_target_pairs={{0,28},{1,29},{2,30},{3,31},{4,0},{5,1},{6,2},{7,3},{8,4},{9,5},{1... | collective-permute-start | bytes 442376 | tf_op jit(solution)/shard_map/ppermute | solution.py:28
  41.8 11.1 %collective-permute-start.13 = (bf16[288,256]{1,0:T(8,128)(2,1)S(1)}, bf16[288,256]{1,0:T(8,128)(2,1)S(1)}, u32[]{:S(2)}, u32[]{:S(2)}) collective-permute-start(bf16[288,256]{1,0:T(8,128)(2,1)S(1)} %get-tuple-element.22), channel_id=1, source_target_pairs={{0,4},{1,5},{2,6},{3,7},{4,8},{5,9},{6,10},{7,11},{8,12},{9,13},{1... | collective-permute-start | bytes 442376 | tf_op jit(solution)/shard_map/ppermute | solution.py:28
  41.8 12.1 %collective-permute-start.11 = (bf16[112,256]{1,0:T(8,128)(2,1)S(1)}, bf16[112,256]{1,0:T(8,128)(2,1)S(1)}, u32[]{:S(2)}, u32[]{:S(2)}) collective-permute-start(bf16[112,256]{1,0:T(8,128)(2,1)S(1)} %get-tuple-element.39), channel_id=1, source_target_pairs={{0,2},{1,3},{2,0},{3,1},{4,6},{5,7},{6,4},{7,5},{8,10},{9,11},{10,... | collective-permute-start | bytes 172040 | tf_op jit(solution)/shard_map/ppermute | solution.py:28
  47.3 4.5 %collective-permute-start.10 = (bf16[112,256]{1,0:T(8,128)(2,1)S(1)}, bf16[112,256]{1,0:T(8,128)(2,1)S(1)}, u32[]{:S(2)}, u32[]{:S(2)}) collective-permute-start(bf16[112,256]{1,0:T(8,128)(2,1)S(1)} %get-tuple-element.40), channel_id=1, source_target_pairs={{0,2},{1,3},{2,0},{3,1},{4,6},{5,7},{6,4},{7,5},{8,10},{9,11},{10,... | collective-permute-start | bytes 172040 | tf_op jit(solution)/shard_map/ppermute | solution.py:28
  52.4 4.0 %collective-permute-start.16 = (bf16[288,256]{1,0:T(8,128)(2,1)S(1)}, bf16[288,256]{1,0:T(8,128)(2,1)S(1)}, u32[]{:S(2)}, u32[]{:S(2)}) collective-permute-start(bf16[288,256]{1,0:T(8,128)(2,1)S(1)} %collective-permute-done.15), channel_id=1, source_target_pairs={{0,28},{1,29},{2,30},{3,31},{4,0},{5,1},{6,2},{7,3},{8,4},{9,5},{1... | collective-permute-start | bytes 442376 | tf_op jit(solution)/shard_map/ppermute | solution.py:28
  53.0 5.2 %collective-permute-start.14 = (bf16[288,256]{1,0:T(8,128)(2,1)S(1)}, bf16[288,256]{1,0:T(8,128)(2,1)S(1)}, u32[]{:S(2)}, u32[]{:S(2)}) collective-permute-start(bf16[288,256]{1,0:T(8,128)(2,1)S(1)} %collective-permute-done.13), channel_id=1, source_target_pairs={{0,4},{1,5},{2,6},{3,7},{4,8},{5,9},{6,10},{7,11},{8,12},{9,13},{1... | collective-permute-start | bytes 442376 | tf_op jit(solution)/shard_map/ppermute | solution.py:28
  58.2 20.8 %collective-permute-start.25 = (bf16[896,256]{1,0:T(8,128)(2,1)}, bf16[896,256]{1,0:T(8,128)(2,1)}, u32[]{:S(2)}, u32[]{:S(2)}) collective-permute-start(bf16[896,256]{1,0:T(8,128)(2,1)} %constant_dynamic-update-slice_fusion), channel_id=1, source_target_pairs={{0,28},{1,29},{2,30},{3,31},{4,0},{5,1},{6,2},{7,3},{8,4},{9,5},{1... | collective-permute-start | bytes 1376264 | tf_op jit(solution)/shard_map/ppermute | solution.py:28
  58.2 20.9 %collective-permute-start.17 = (bf16[896,256]{1,0:T(8,128)(2,1)}, bf16[896,256]{1,0:T(8,128)(2,1)}, u32[]{:S(2)}, u32[]{:S(2)}) collective-permute-start(bf16[896,256]{1,0:T(8,128)(2,1)} %constant_dynamic-update-slice_fusion), channel_id=1, source_target_pairs={{0,4},{1,5},{2,6},{3,7},{4,8},{5,9},{6,10},{7,11},{8,12},{9,13},{1... | collective-permute-start | bytes 1376264 | tf_op jit(solution)/shard_map/ppermute | solution.py:28
  59.6 10.2 %collective-permute-start.20 = (bf16[288,256]{1,0:T(8,128)(2,1)S(1)}, bf16[288,256]{1,0:T(8,128)(2,1)S(1)}, u32[]{:S(2)}, u32[]{:S(2)}) collective-permute-start(bf16[288,256]{1,0:T(8,128)(2,1)S(1)} %collective-permute-done.16), channel_id=1, source_target_pairs={{0,28},{1,29},{2,30},{3,31},{4,0},{5,1},{6,2},{7,3},{8,4},{9,5},{1... | collective-permute-start | bytes 442376 | tf_op jit(solution)/shard_map/ppermute | solution.py:28
  60.9 10.0 %collective-permute-start.18 = (bf16[288,256]{1,0:T(8,128)(2,1)S(1)}, bf16[288,256]{1,0:T(8,128)(2,1)S(1)}, u32[]{:S(2)}, u32[]{:S(2)}) collective-permute-start(bf16[288,256]{1,0:T(8,128)(2,1)S(1)} %collective-permute-done.14), channel_id=1, source_target_pairs={{0,4},{1,5},{2,6},{3,7},{4,8},{5,9},{6,10},{7,11},{8,12},{9,13},{1... | collective-permute-start | bytes 442376 | tf_op jit(solution)/shard_map/ppermute | solution.py:28
  69.9 65.1 %copy-start = (bf16[32,72,256]{2,1,0:T(8,128)(2,1)}, bf16[32,72,256]{2,1,0:T(8,128)(2,1)S(1)}, u32[]{:S(2)}) copy-start(bf16[32,72,256]{2,1,0:T(8,128)(2,1)S(1)} %all-to-all-done.got_ref.refs_14_) | copy-start | bytes 3538948
  70.9 8.1 %collective-permute-start.21 = (bf16[144,256]{1,0:T(8,128)(2,1)S(1)}, bf16[144,256]{1,0:T(8,128)(2,1)S(1)}, u32[]{:S(2)}, u32[]{:S(2)}) collective-permute-start(bf16[144,256]{1,0:T(8,128)(2,1)S(1)} %slice.49), channel_id=1, source_target_pairs={{0,28},{1,29},{2,30},{3,31},{4,0},{5,1},{6,2},{7,3},{8,4},{9,5},{1... | collective-permute-start | bytes 221192 | tf_op jit(solution)/shard_map/ppermute | solution.py:28
  71.6 7.5 %collective-permute-start.19 = (bf16[144,256]{1,0:T(8,128)(2,1)S(1)}, bf16[144,256]{1,0:T(8,128)(2,1)S(1)}, u32[]{:S(2)}, u32[]{:S(2)}) collective-permute-start(bf16[144,256]{1,0:T(8,128)(2,1)S(1)} %slice.48), channel_id=1, source_target_pairs={{0,4},{1,5},{2,6},{3,7},{4,8},{5,9},{6,10},{7,11},{8,12},{9,13},{1... | collective-permute-start | bytes 221192 | tf_op jit(solution)/shard_map/ppermute | solution.py:28
  72.6 25.2 %collective-permute-start.35 = (bf16[32,72,256]{2,1,0:T(8,128)(2,1)S(1)}, bf16[32,72,256]{2,1,0:T(8,128)(2,1)S(1)}, u32[]{:S(2)}, u32[]{:S(2)}) collective-permute-start(bf16[32,72,256]{2,1,0:T(8,128)(2,1)S(1)} %all-to-all-done.got_ref.refs_14_), channel_id=1, source_target_pairs={{0,192},{32,224},{64,0},{96,32},{128,64},{160,96},{192,128},{224,1... | collective-permute-start | bytes 3538952 | tf_op jit(solution)/shard_map/ppermute | solution.py:28
  79.0 23.9 %collective-permute-start.33 = (bf16[32,72,256]{2,1,0:T(8,128)(2,1)S(1)}, bf16[32,72,256]{2,1,0:T(8,128)(2,1)S(1)}, u32[]{:S(2)}, u32[]{:S(2)}) collective-permute-start(bf16[32,72,256]{2,1,0:T(8,128)(2,1)S(1)} %all-to-all-done.got_ref.refs_14_), channel_id=1, source_target_pairs={{0,64},{32,96},{64,128},{96,160},{128,192},{160,224},{192,0},{224,... | collective-permute-start | bytes 3538952 | tf_op jit(solution)/shard_map/ppermute | solution.py:28
  79.0 8.8 %collective-permute-start.22 = (bf16[896,256]{1,0:T(8,128)(2,1)}, bf16[896,256]{1,0:T(8,128)(2,1)S(1)}, u32[]{:S(2)}, u32[]{:S(2)}) collective-permute-start(bf16[896,256]{1,0:T(8,128)(2,1)} %collective-permute-done.17), channel_id=1, source_target_pairs={{0,4},{1,5},{2,6},{3,7},{4,8},{5,9},{6,10},{7,11},{8,12},{9,13},{1... | collective-permute-start | bytes 1376264 | tf_op jit(solution)/shard_map/ppermute | solution.py:28
  79.2 9.1 %collective-permute-start.26 = (bf16[896,256]{1,0:T(8,128)(2,1)}, bf16[896,256]{1,0:T(8,128)(2,1)S(1)}, u32[]{:S(2)}, u32[]{:S(2)}) collective-permute-start(bf16[896,256]{1,0:T(8,128)(2,1)} %collective-permute-done.25), channel_id=1, source_target_pairs={{0,28},{1,29},{2,30},{3,31},{4,0},{5,1},{6,2},{7,3},{8,4},{9,5},{1... | collective-permute-start | bytes 1376264 | tf_op jit(solution)/shard_map/ppermute | solution.py:28
  86.9 22.3 %collective-permute-start.31 = (bf16[2304,256]{1,0:T(8,128)(2,1)}, bf16[2304,256]{1,0:T(8,128)(2,1)S(1)}, u32[]{:S(2)}, u32[]{:S(2)}) collective-permute-start(bf16[2304,256]{1,0:T(8,128)(2,1)} %constant_dynamic-update-slice_fusion.5), channel_id=1, source_target_pairs={{0,3},{1,0},{2,1},{3,2},{4,7},{5,4},{6,5},{7,6},{8,11},{9,8},{10,9... | collective-permute-start | bytes 3538952 | tf_op jit(solution)/shard_map/ppermute | solution.py:28
  87.9 21.3 %copy-start.12 = (bf16[896,256]{1,0:T(8,128)(2,1)}, bf16[896,256]{1,0:T(8,128)(2,1)S(1)}, u32[]{:S(2)}) copy-start(bf16[896,256]{1,0:T(8,128)(2,1)S(1)} %collective-permute-done.22) | copy-start | bytes 1376260
  87.9 22.2 %collective-permute-start.29 = (bf16[2304,256]{1,0:T(8,128)(2,1)}, bf16[2304,256]{1,0:T(8,128)(2,1)S(1)}, u32[]{:S(2)}, u32[]{:S(2)}) collective-permute-start(bf16[2304,256]{1,0:T(8,128)(2,1)} %constant_dynamic-update-slice_fusion.5), channel_id=1, source_target_pairs={{0,1},{1,2},{2,3},{3,0},{4,5},{5,6},{6,7},{7,4},{8,9},{9,10},{10,1... | collective-permute-start | bytes 3538952 | tf_op jit(solution)/shard_map/ppermute | solution.py:28
  88.3 20.8 %copy-start.13 = (bf16[896,256]{1,0:T(8,128)(2,1)}, bf16[896,256]{1,0:T(8,128)(2,1)S(1)}, u32[]{:S(2)}) copy-start(bf16[896,256]{1,0:T(8,128)(2,1)S(1)} %collective-permute-done.26) | copy-start | bytes 1376260
  88.3 15.0 %collective-permute-start.23 = (bf16[896,256]{1,0:T(8,128)(2,1)S(1)}, bf16[896,256]{1,0:T(8,128)(2,1)S(1)}, u32[]{:S(2)}, u32[]{:S(2)}) collective-permute-start(bf16[896,256]{1,0:T(8,128)(2,1)S(1)} %collective-permute-done.22), channel_id=1, source_target_pairs={{0,4},{1,5},{2,6},{3,7},{4,8},{5,9},{6,10},{7,11},{8,12},{9,13},{1... | collective-permute-start | bytes 1376264 | tf_op jit(solution)/shard_map/ppermute | solution.py:28
  97.8 21.5 %copy-start.4 = (bf16[32,72,256]{2,1,0:T(8,128)(2,1)}, bf16[32,72,256]{2,1,0:T(8,128)(2,1)S(1)}, u32[]{:S(2)}) copy-start(bf16[32,72,256]{2,1,0:T(8,128)(2,1)S(1)} %collective-permute-done.35.refs_18_) | copy-start | bytes 3538948
  97.8 7.6 %collective-permute-start.27 = (bf16[896,256]{1,0:T(8,128)(2,1)S(1)}, bf16[896,256]{1,0:T(8,128)(2,1)S(1)}, u32[]{:S(2)}, u32[]{:S(2)}) collective-permute-start(bf16[896,256]{1,0:T(8,128)(2,1)S(1)} %collective-permute-done.26), channel_id=1, source_target_pairs={{0,28},{1,29},{2,30},{3,31},{4,0},{5,1},{6,2},{7,3},{8,4},{9,5},{1... | collective-permute-start | bytes 1376264 | tf_op jit(solution)/shard_map/ppermute | solution.py:28
  102.9 16.4 %collective-permute-start.36 = (bf16[16,72,256]{2,1,0:T(8,128)(2,1)S(1)}, bf16[16,72,256]{2,1,0:T(8,128)(2,1)}, u32[]{:S(2)}, u32[]{:S(2)}) collective-permute-start(bf16[16,72,256]{2,1,0:T(8,128)(2,1)S(1)} %slice.55), channel_id=1, source_target_pairs={{0,192},{32,224},{64,0},{96,32},{128,64},{160,96},{192,128},{224,1... | collective-permute-start | bytes 1769480 | tf_op jit(solution)/shard_map/ppermute | solution.py:28
  103.4 18.3 %collective-permute-start.34 = (bf16[16,72,256]{2,1,0:T(8,128)(2,1)S(1)}, bf16[16,72,256]{2,1,0:T(8,128)(2,1)}, u32[]{:S(2)}, u32[]{:S(2)}) collective-permute-start(bf16[16,72,256]{2,1,0:T(8,128)(2,1)S(1)} %slice.54), channel_id=1, source_target_pairs={{0,64},{32,96},{64,128},{96,160},{128,192},{160,224},{192,0},{224,... | collective-permute-start | bytes 1769480 | tf_op jit(solution)/shard_map/ppermute | solution.py:28
  105.4 12.3 %collective-permute-start.24 = (bf16[448,256]{1,0:T(8,128)(2,1)S(1)}, bf16[448,256]{1,0:T(8,128)(2,1)S(1)}, u32[]{:S(2)}, u32[]{:S(2)}) collective-permute-start(bf16[448,256]{1,0:T(8,128)(2,1)S(1)} %slice.56), channel_id=1, source_target_pairs={{0,4},{1,5},{2,6},{3,7},{4,8},{5,9},{6,10},{7,11},{8,12},{9,13},{1... | collective-permute-start | bytes 688136 | tf_op jit(solution)/shard_map/ppermute | solution.py:28
  109.2 8.7 %collective-permute-start.28 = (bf16[448,256]{1,0:T(8,128)(2,1)S(1)}, bf16[448,256]{1,0:T(8,128)(2,1)S(1)}, u32[]{:S(2)}, u32[]{:S(2)}) collective-permute-start(bf16[448,256]{1,0:T(8,128)(2,1)S(1)} %slice.57), channel_id=1, source_target_pairs={{0,28},{1,29},{2,30},{3,31},{4,0},{5,1},{6,2},{7,3},{8,4},{9,5},{1... | collective-permute-start | bytes 688136 | tf_op jit(solution)/shard_map/ppermute | solution.py:28
  110.1 25.6 %collective-permute-start.37 = (bf16[32,72,256]{2,1,0:T(8,128)(2,1)S(1)}, bf16[32,72,256]{2,1,0:T(8,128)(2,1)}, u32[]{:S(2)}, u32[]{:S(2)}) collective-permute-start(bf16[32,72,256]{2,1,0:T(8,128)(2,1)S(1)} %all-to-all-done.got_ref.refs_14_), channel_id=1, source_target_pairs={{0,32},{32,0},{64,96},{96,64},{128,160},{160,128},{192,224},{224,1... | collective-permute-start | bytes 3538952 | tf_op jit(solution)/shard_map/ppermute | solution.py:36
  117.8 13.7 %collective-permute-start.32 = (bf16[1152,256]{1,0:T(8,128)(2,1)S(1)}, bf16[1152,256]{1,0:T(8,128)(2,1)S(1)}, u32[]{:S(2)}, u32[]{:S(2)}) collective-permute-start(bf16[1152,256]{1,0:T(8,128)(2,1)S(1)} %slice.59), channel_id=1, source_target_pairs={{0,3},{1,0},{2,1},{3,2},{4,7},{5,4},{6,5},{7,6},{8,11},{9,8},{10,9... | collective-permute-start | bytes 1769480 | tf_op jit(solution)/shard_map/ppermute | solution.py:28
  117.9 16.5 %collective-permute-start.30 = (bf16[1152,256]{1,0:T(8,128)(2,1)S(1)}, bf16[1152,256]{1,0:T(8,128)(2,1)}, u32[]{:S(2)}, u32[]{:S(2)}) collective-permute-start(bf16[1152,256]{1,0:T(8,128)(2,1)S(1)} %slice.58), channel_id=1, source_target_pairs={{0,1},{1,2},{2,3},{3,0},{4,5},{5,6},{6,7},{7,4},{8,9},{9,10},{10,1... | collective-permute-start | bytes 1769480 | tf_op jit(solution)/shard_map/ppermute | solution.py:28
  119.3 17.9 %collective-permute-start.41 = (bf16[32,72,256]{2,1,0:T(8,128)(2,1)S(1)}, bf16[32,72,256]{2,1,0:T(8,128)(2,1)}, u32[]{:S(2)}, u32[]{:S(2)}) collective-permute-start(bf16[32,72,256]{2,1,0:T(8,128)(2,1)S(1)} %collective-permute-done.35.refs_18_), channel_id=1, source_target_pairs={{0,32},{32,0},{64,96},{96,64},{128,160},{160,128},{192,224},{224,1... | collective-permute-start | bytes 3538952 | tf_op jit(solution)/shard_map/ppermute | solution.py:36
  121.7 15.6 %collective-permute-start.38 = (bf16[32,72,256]{2,1,0:T(8,128)(2,1)S(1)}, bf16[32,72,256]{2,1,0:T(8,128)(2,1)}, u32[]{:S(2)}, u32[]{:S(2)}) collective-permute-start(bf16[32,72,256]{2,1,0:T(8,128)(2,1)S(1)} %collective-permute-done.33.refs_15_), channel_id=1, source_target_pairs={{0,32},{32,0},{64,96},{96,64},{128,160},{160,128},{192,224},{224,1... | collective-permute-start | bytes 3538952 | tf_op jit(solution)/shard_map/ppermute | solution.py:36
  132.3 4.1 %collective-permute-start.40 = (bf16[16,72,256]{2,1,0:T(8,128)(2,1)}, bf16[16,72,256]{2,1,0:T(8,128)(2,1)}, u32[]{:S(2)}, u32[]{:S(2)}) collective-permute-start(bf16[16,72,256]{2,1,0:T(8,128)(2,1)} %collective-permute-done.36.refs_17_), channel_id=1, source_target_pairs={{0,32},{32,0},{64,96},{96,64},{128,160},{160,128},{192,224},{224,1... | collective-permute-start | bytes 1769480 | tf_op jit(solution)/shard_map/ppermute | solution.py:36
  134.4 2.8 %collective-permute-start.39 = (bf16[16,72,256]{2,1,0:T(8,128)(2,1)}, bf16[16,72,256]{2,1,0:T(8,128)(2,1)}, u32[]{:S(2)}, u32[]{:S(2)}) collective-permute-start(bf16[16,72,256]{2,1,0:T(8,128)(2,1)} %collective-permute-done.34.refs_16_), channel_id=1, source_target_pairs={{0,32},{32,0},{64,96},{96,64},{128,160},{160,128},{192,224},{224,1... | collective-permute-start | bytes 1769480 | tf_op jit(solution)/shard_map/ppermute | solution.py:36
  (16 other events, 155.7 us)

commit v6 on v5

--- a/solution.py
+++ b/solution.py
@@ -8,9 +8,19 @@
 from jax.sharding import PartitionSpec as P
 
 NX, NY, NZ = 4, 4, 8
-ROWS_A = 224
+ROWS_A = 240
 LABEL_ROWS = 8
 GROUP = 4
+
+
+B_RUNS = (
+    *((p, skip, z, tall, y) for p, y in ((0, 0), (1, 1), (4, 3)) for skip, z, tall in ((0, 6, 2), (2, 0, 3), (5, 5, 1), (6, 3, 2))),
+    (2, 0, 6, 2, 2),
+    (2, 2, 0, 2, 2),
+    (3, 0, 2, 1, 2),
+    (3, 1, 5, 1, 2),
+    (3, 2, 3, 2, 2),
+)
 
 
 def ring_steps(axis, shift):
@@ -159,11 +169,12 @@
     for piece in pieces_a:
         copy(piece, amps.at[at // NY, pl.ds(at % NY, piece.shape[0]), pl.ds(0, rows_a), :])
         at += piece.shape[0]
-    at = 0
-    for piece in pieces_b:
-        height = piece.shape[1]
-        copy(piece, amps.at[pl.ds(at % NZ, piece.shape[0]), at // NZ, pl.ds(rows_a, height), :])
-        at += piece.shape[0]
+    for piece, skip, z, tall, y in B_RUNS:
+        height = pieces_b[piece].shape[1]
+        copy(
+            pieces_b[piece].at[pl.ds(skip, tall)],
+            amps.at[pl.ds(z, tall), y, pl.ds(rows_a, height), :],
+        )
 
     total[...] = jnp.zeros_like(total)
     weights[:, senders] = jnp.zeros(weights.shape[:1] + weights.shape[2:], weights.dtype)
@@ -237,7 +248,7 @@
             pltpu.SMEM((2 * room,), jnp.int32),
             pltpu.SMEM((2 * room,), jnp.int32),
             pltpu.SMEM((2 * room,), jnp.int32),
-            pltpu.SemaphoreType.DMA((n_a + n_b + n_w,)),
+            pltpu.SemaphoreType.DMA((n_a + len(B_RUNS) + n_w,)),
         ],
         out_shape=jax.ShapeDtypeStruct((count, 2 * width), jnp.bfloat16),
         compiler_params=pltpu.CompilerParams(vmem_limit_bytes=60 << 20),
@@ -279,7 +290,7 @@
     b4 = [send("z", 1, b3[:half]), send("z", -1, b5[half:])]
     a1, a7 = after(a1, *b4), after(a7, *b4)
     a2, a6 = send("z", 1, a1), send("z", -1, a7)
-    b0 = jnp.concatenate([b, b1, b2, b3, *b4, b5, b6, b7], axis=0)
+    b0 = jnp.concatenate([b6, b7, b, b1, b2, b5, b3, *b4], axis=0)
     by1, by3 = send("y", 1, b0), send("y", -1, b0)
     a2, a6 = after(a2, b0), after(a6, b0)
     a3, a5 = send("z", 1, a2), send("z", -1, a6)
@@ -295,7 +306,7 @@
     w1, w3 = after(w1, a2, a6), after(w3, a2, a6)
     w2 = [send("x", 1, w1[:half]), send("x", -1, w3[half:])]
     pieces_w = [got, w1, *w2, w3]
-    held = [after(p, a3, a5) for p in (got, w1)] + [after(p, *a4) for p in w2] + [after(w3, a3, a5)]
+    held = [after(p, a3, a5) for p in (got, w1)] + [after(p, *a4, *by2) for p in w2] + [after(w3, a3, a5)]
     pieces_w += [other_core(p) for p in held]
     result = ladder(
         read_labels(tile_id.reshape(1), got),

time: 153 us -> 159 us (1.039)
  starting transfers between devices: 69.8 us -> 78.4 us
  local copies, waits for them, and re-layouts: 14.1 us -> 8.87 us
  waiting for transfers between devices: 49.3 us -> 52.6 us
    ppermute x10, starting transfers between devices: 25.4 us -> 31.7 us  [other_core(): return lax.ppermute(piece, 'pair', [(p, p ^ 1) for p in range(2 * NX)])]
    unnamed x54 -> x48, local copies, waits for them, and re-layouts: 10.6 us -> 6.04 us
    ppermute x32, waiting for transfers between devices: 47.3 us -> 50.9 us  [send(): lax.ppermute(piece, 'pair' if axis == 'x' else 'tile', ring_steps(axis, s...]
    ppermute x32, starting transfers between devices: 32.3 us -> 34.6 us  [send(): lax.ppermute(piece, 'pair' if axis == 'x' else 'tile', ring_steps(axis, s...]
  transfers between devices with their start and end apart: 43 -> 43, of which waited for: 17 -> 17; matrix products, arithmetic and copies ran while one was open for 6% -> 4% of each run, Pallas kernels for 1% -> 1%
where the time goes in v6:
time: 159 us; the launch traced here: 158 us
  starting transfers between devices  78.4 us (49%)
  waiting for transfers between devices  52.6 us (33%)
  Pallas kernels  17.6 us (11%)
  local copies, waits for them, and re-layouts  8.87 us (6%)
    ppermute x32, waiting for transfers between devices, send(): lax.ppermute(piece, 'pair' if axis == 'x' else 'tile', ring_steps(axis, s...  50.9 us
    ppermute x32, starting transfers between devices, send(): lax.ppermute(piece, 'pair' if axis == 'x' else 'tile', ring_steps(axis, s...  34.6 us
    ppermute x10, starting transfers between devices, other_core(): return lax.ppermute(piece, 'pair', [(p, p ^ 1) for p in range(2 * NX)])  31.7 us
    pallas_call x1, Pallas kernels, ladder(): pl.pallas_call(functools.partial(ladder_kernel, n_a=n_a, n_b=n_b), in_spe...  12.5 us
    all_to_all x1, starting transfers between devices, local(): lax.all_to_all(routed, 'tile', split_axis=0, concat_axis=0, tiled=True)  12.2 us
    unnamed x48, local copies, waits for them, and re-layouts  6.04 us
  transfers between devices with their start and end apart: 43, of which 17 were waited for; matrix products, arithmetic and copies ran while one was open for 4% of the time, Pallas kernels for 1%

profile of v6, /device:TPU:1, one launch (start us, length us, event | category | flops | bytes accessed | tf_op | source)
XLA Modules:
  0.0 158.5 jit_solution(17520728747136805969)
XLA Ops:
  0.0 3.2 %shard_map.73 = bf16[32,72,256]{2,1,0:T(8,128)(2,1)} custom-call(s32[32]{0:T(128)} %rows_ref.1, s32[32]{0:T(128)} %cols_ref.1, s32[1]{0:T(128)} %bitcast.1.share_ref.pair_ref, bf16[32,256,256]{2,1,0:T(8,128)(2,1)} %w_ref.1), custom_call_target="tpu_custom_call" | custom-call | tf_op jit(solution)/shard_map/pallas_call | solution.py:71
  3.2 12.2 %all-to-all-start = ((bf16[32,72,256]{2,1,0:T(8,128)(2,1)}), bf16[32,72,256]{2,1,0:T(8,128)(2,1)S(1)}, u32[]{:S(2)}, u32[]{:S(2)}) async-start(bf16[32,72,256]{2,1,0:T(8,128)(2,1)} %shard_map.73), calls=%async_computation | async-start | bytes 2359296 | tf_op jit(solution)/shard_map/all_to_all | solution.py:275
  15.4 2.6 %collective-permute-start.3 = (bf16[512,256]{1,0:T(8,128)(2,1)S(1)}, bf16[512,256]{1,0:T(8,128)(2,1)S(1)}, u32[]{:S(2)}, u32[]{:S(2)}) collective-permute-start(bf16[512,256]{1,0:T(8,128)(2,1)S(1)} %bitcast.22), channel_id=1, source_target_pairs={{0,192},{32,224},{64,0},{96,32},{128,64},{160,96},{192,128},{224,1... | collective-permute-start | bytes 786440 | tf_op jit(solution)/shard_map/ppermute | solution.py:38
  17.9 1.2 collective-permute-start.4
  19.2 2.1 %collective-permute-start.2 = (bf16[256,256]{1,0:T(8,128)(2,1)S(1)}, bf16[256,256]{1,0:T(8,128)(2,1)S(1)}, u32[]{:S(2)}, u32[]{:S(2)}) collective-permute-start(bf16[256,256]{1,0:T(8,128)(2,1)S(1)} %get-tuple-element.37), channel_id=1, source_target_pairs={{0,128},{32,160},{64,192},{96,224},{128,0},{160,32},{192,64},{224,... | collective-permute-start | bytes 393224 | tf_op jit(solution)/shard_map/ppermute | solution.py:38
  21.3 1.0 collective-permute-start.1
  22.6 7.5 %collective-permute-start.8 = (bf16[512,256]{1,0:T(8,128)(2,1)S(1)}, bf16[512,256]{1,0:T(8,128)(2,1)S(1)}, u32[]{:S(2)}, u32[]{:S(2)}) collective-permute-start(bf16[512,256]{1,0:T(8,128)(2,1)S(1)} %collective-permute-done.3.refs_4_), channel_id=1, source_target_pairs={{0,32},{32,0},{64,96},{96,64},{128,160},{160,128},{192,224},{224,1... | collective-permute-start | bytes 786440 | tf_op jit(solution)/shard_map/ppermute | solution.py:46
  30.1 3.4 %collective-permute-start.5 = (bf16[512,256]{1,0:T(8,128)(2,1)S(1)}, bf16[512,256]{1,0:T(8,128)(2,1)S(1)}, u32[]{:S(2)}, u32[]{:S(2)}) collective-permute-start(bf16[512,256]{1,0:T(8,128)(2,1)S(1)} %collective-permute-done.refs_1_), channel_id=1, source_target_pairs={{0,32},{32,0},{64,96},{96,64},{128,160},{160,128},{192,224},{224,1... | collective-permute-start | bytes 786440 | tf_op jit(solution)/shard_map/ppermute | solution.py:46
  35.0 1.8 %shard_map.75 = (bf16[240,256]{1,0:T(8,128)(2,1)S(1)}, bf16[272,256]{1,0:T(8,128)(2,1)S(1)}) custom-call(s32[1]{0:T(128)} %bitcast.1.share_ref.pair_ref, s32[1]{0:T(128)S(6)} %copy.20.live_ref, s32[1,4096]{1,0:T(1,128)S(1)} %bitcast.26, bf16[512,256]{1,0:T(8,128)(2,1)S(1)} %bitcast.25, bf16[512,256]{1,0:T(8,128)(2,1)S(1)} %collective-permute-done.refs_1_, ...), custom_call_target="tpu_custom_call" | custom-call | tf_op jit(solution)/shard_map/pallas_call | solution.py:114
  36.8 1.3 collective-permute-start.9
  38.1 1.5 collective-permute-start.12
  39.7 2.5 %collective-permute-start.15 = (bf16[272,256]{1,0:T(8,128)(2,1)S(1)}, bf16[272,256]{1,0:T(8,128)(2,1)S(1)}, u32[]{:S(2)}, u32[]{:S(2)}) collective-permute-start(bf16[272,256]{1,0:T(8,128)(2,1)S(1)} %get-tuple-element.22), channel_id=1, source_target_pairs={{0,28},{1,29},{2,30},{3,31},{4,0},{5,1},{6,2},{7,3},{8,4},{9,5},{1... | collective-permute-start | bytes 417800 | tf_op jit(solution)/shard_map/ppermute | solution.py:38
  42.2 1.5 collective-permute-start.11
  43.7 1.7 %collective-permute-done.9 = bf16[240,256]{1,0:T(8,128)(2,1)S(1)} collective-permute-done((bf16[240,256]{1,0:T(8,128)(2,1)S(1)}, bf16[240,256]{1,0:T(8,128)(2,1)S(1)}, u32[]{:S(2)}, u32[]{:S(2)}) %collective-permute-start.9) | collective-permute-done | bytes 122912 | tf_op jit(solution)/shard_map/ppermute | solution.py:38
  45.8 4.1 %collective-permute-done.10 = bf16[120,256]{1,0:T(8,128)(2,1)S(1)} collective-permute-done((bf16[120,256]{1,0:T(8,128)(2,1)S(1)}, bf16[120,256]{1,0:T(8,128)(2,1)S(1)}, u32[]{:S(2)}, u32[]{:S(2)}) %collective-permute-start.10) | collective-permute-done | bytes 61472 | tf_op jit(solution)/shard_map/ppermute | solution.py:38
  49.9 2.2 %collective-permute-start.16 = (bf16[272,256]{1,0:T(8,128)(2,1)S(1)}, bf16[272,256]{1,0:T(8,128)(2,1)S(1)}, u32[]{:S(2)}, u32[]{:S(2)}) collective-permute-start(bf16[272,256]{1,0:T(8,128)(2,1)S(1)} %collective-permute-done.15), channel_id=1, source_target_pairs={{0,28},{1,29},{2,30},{3,31},{4,0},{5,1},{6,2},{7,3},{8,4},{9,5},{1... | collective-permute-start | bytes 417800 | tf_op jit(solution)/shard_map/ppermute | solution.py:38
  52.2 2.3 %collective-permute-done.16 = bf16[272,256]{1,0:T(8,128)(2,1)S(1)} collective-permute-done((bf16[272,256]{1,0:T(8,128)(2,1)S(1)}, bf16[272,256]{1,0:T(8,128)(2,1)S(1)}, u32[]{:S(2)}, u32[]{:S(2)}) %collective-permute-start.16) | collective-permute-done | bytes 139296 | tf_op jit(solution)/shard_map/ppermute | solution.py:38
  54.5 2.8 %collective-permute-done.14 = bf16[272,256]{1,0:T(8,128)(2,1)S(1)} collective-permute-done((bf16[272,256]{1,0:T(8,128)(2,1)S(1)}, bf16[272,256]{1,0:T(8,128)(2,1)S(1)}, u32[]{:S(2)}, u32[]{:S(2)}) %collective-permute-start.14) | collective-permute-done | bytes 139296 | tf_op jit(solution)/shard_map/ppermute | solution.py:38
  57.6 1.2 collective-permute-start.17
  58.7 1.5 collective-permute-start.20
  60.9 0.7 constant_dynamic-update-slice_fusion.12
  61.6 0.7 constant_dynamic-update-slice_fusion.11
  62.3 0.7 constant_dynamic-update-slice_fusion.10
  62.9 0.7 constant_dynamic-update-slice_fusion.9
  63.6 6.0 %collective-permute-done.20 = bf16[272,256]{1,0:T(8,128)(2,1)S(1)} collective-permute-done((bf16[272,256]{1,0:T(8,128)(2,1)S(1)}, bf16[272,256]{1,0:T(8,128)(2,1)S(1)}, u32[]{:S(2)}, u32[]{:S(2)}) %collective-permute-start.20) | collective-permute-done | bytes 139296 | tf_op jit(solution)/shard_map/ppermute | solution.py:38
  69.6 0.7 constant_dynamic-update-slice_fusion.8
  70.3 0.8 collective-permute-done.18
  71.2 2.7 %collective-permute-start.21 = (bf16[136,256]{1,0:T(8,128)(2,1)S(1)}, bf16[136,256]{1,0:T(8,128)(2,1)S(1)}, u32[]{:S(2)}, u32[]{:S(2)}) collective-permute-start(bf16[136,256]{1,0:T(8,128)(2,1)S(1)} %slice.49), channel_id=1, source_target_pairs={{0,28},{1,29},{2,30},{3,31},{4,0},{5,1},{6,2},{7,3},{8,4},{9,5},{1... | collective-permute-start | bytes 208904 | tf_op jit(solution)/shard_map/ppermute | solution.py:38
  74.5 1.0 collective-permute-done.19
  77.3 1.1 collective-permute-start.29
  78.3 2.6 %collective-permute-start.26 = (bf16[960,256]{1,0:T(8,128)(2,1)}, bf16[960,256]{1,0:T(8,128)(2,1)S(1)}, u32[]{:S(2)}, u32[]{:S(2)}) collective-permute-start(bf16[960,256]{1,0:T(8,128)(2,1)} %collective-permute-done.25), channel_id=1, source_target_pairs={{0,28},{1,29},{2,30},{3,31},{4,0},{5,1},{6,2},{7,3},{8,4},{9,5},{1... | collective-permute-start | bytes 1474568 | tf_op jit(solution)/shard_map/ppermute | solution.py:38
  80.9 1.2 collective-permute-start.35
  82.2 4.0 %collective-permute-done.22 = bf16[960,256]{1,0:T(8,128)(2,1)S(1)} collective-permute-done((bf16[960,256]{1,0:T(8,128)(2,1)S(1)}, bf16[960,256]{1,0:T(8,128)(2,1)S(1)}, u32[]{:S(2)}, u32[]{:S(2)}) %collective-permute-start.22) | collective-permute-done | bytes 491552 | tf_op jit(solution)/shard_map/ppermute | solution.py:38
  86.2 0.9 collective-permute-done.26
  87.7 10.0 %collective-permute-done.31 = bf16[2176,256]{1,0:T(8,128)(2,1)S(1)} collective-permute-done((bf16[2176,256]{1,0:T(8,128)(2,1)}, bf16[2176,256]{1,0:T(8,128)(2,1)S(1)}, u32[]{:S(2)}, u32[]{:S(2)}) %collective-permute-start.31) | collective-permute-done | bytes 1114144 | tf_op jit(solution)/shard_map/ppermute | solution.py:38
  97.6 1.8 %collective-permute-start.27 = (bf16[960,256]{1,0:T(8,128)(2,1)S(1)}, bf16[960,256]{1,0:T(8,128)(2,1)S(1)}, u32[]{:S(2)}, u32[]{:S(2)}) collective-permute-start(bf16[960,256]{1,0:T(8,128)(2,1)S(1)} %collective-permute-done.26), channel_id=1, source_target_pairs={{0,28},{1,29},{2,30},{3,31},{4,0},{5,1},{6,2},{7,3},{8,4},{9,5},{1... | collective-permute-start | bytes 1474568 | tf_op jit(solution)/shard_map/ppermute | solution.py:38
  99.5 1.1 collective-permute-start.32
  101.2 4.4 %collective-permute-done.27 = bf16[960,256]{1,0:T(8,128)(2,1)S(1)} collective-permute-done((bf16[960,256]{1,0:T(8,128)(2,1)S(1)}, bf16[960,256]{1,0:T(8,128)(2,1)S(1)}, u32[]{:S(2)}, u32[]{:S(2)}) %collective-permute-start.27) | collective-permute-done | bytes 491552 | tf_op jit(solution)/shard_map/ppermute | solution.py:38
  105.9 2.8 %collective-permute-start.28 = (bf16[480,256]{1,0:T(8,128)(2,1)S(1)}, bf16[480,256]{1,0:T(8,128)(2,1)S(1)}, u32[]{:S(2)}, u32[]{:S(2)}) collective-permute-start(bf16[480,256]{1,0:T(8,128)(2,1)S(1)} %slice.57), channel_id=1, source_target_pairs={{0,28},{1,29},{2,30},{3,31},{4,0},{5,1},{6,2},{7,3},{8,4},{9,5},{1... | collective-permute-start | bytes 737288 | tf_op jit(solution)/shard_map/ppermute | solution.py:38
  108.8 1.1 collective-permute-start.36
  110.0 2.5 %collective-permute-done.24 = bf16[480,256]{1,0:T(8,128)(2,1)S(1)} collective-permute-done((bf16[480,256]{1,0:T(8,128)(2,1)S(1)}, bf16[480,256]{1,0:T(8,128)(2,1)S(1)}, u32[]{:S(2)}, u32[]{:S(2)}) %collective-permute-start.24) | collective-permute-done | bytes 245792 | tf_op jit(solution)/shard_map/ppermute | solution.py:38
  112.5 12.3 %collective-permute-start.37 = (bf16[32,72,256]{2,1,0:T(8,128)(2,1)S(1)}, bf16[32,72,256]{2,1,0:T(8,128)(2,1)}, u32[]{:S(2)}, u32[]{:S(2)}) collective-permute-start(bf16[32,72,256]{2,1,0:T(8,128)(2,1)S(1)} %all-to-all-done.got_ref.refs_14_), channel_id=1, source_target_pairs={{0,32},{32,0},{64,96},{96,64},{128,160},{160,128},{192,224},{224,1... | collective-permute-start | bytes 3538952 | tf_op jit(solution)/shard_map/ppermute | solution.py:46
  125.6 5.2 %collective-permute-start.40 = (bf16[16,72,256]{2,1,0:T(8,128)(2,1)}, bf16[16,72,256]{2,1,0:T(8,128)(2,1)}, u32[]{:S(2)}, u32[]{:S(2)}) collective-permute-start(bf16[16,72,256]{2,1,0:T(8,128)(2,1)} %collective-permute-done.36.refs_17_), channel_id=1, source_target_pairs={{0,32},{32,0},{64,96},{96,64},{128,160},{160,128},{192,224},{224,1... | collective-permute-start | bytes 1769480 | tf_op jit(solution)/shard_map/ppermute | solution.py:46
  130.8 10.1 %collective-permute-done.34.refs_16_ = bf16[16,72,256]{2,1,0:T(8,128)(2,1)} collective-permute-done((bf16[16,72,256]{2,1,0:T(8,128)(2,1)S(1)}, bf16[16,72,256]{2,1,0:T(8,128)(2,1)}, u32[]{:S(2)}, u32[]{:S(2)}) %collective-permute-start.34) | collective-permute-done | bytes 589856 | tf_op jit(solution)/shard_map/ppermute | solution.py:38
  141.0 1.0 collective-permute-start.39
  142.7 1.3 collective-permute-done.39.refs_21_
  143.9 12.5 %shard_map.76 = bf16[512,512]{1,0:T(8,128)(2,1)} custom-call(s32[32,128]{1,0:T(8,128)} %copy-done.2, s32[2]{0:T(128)} %live_ref.2, s32[1]{0:T(128)} %bitcast.1.share_ref.pair_ref, bf16[4,240,256]{2,1,0:T(8,128)(2,1)} %bitcast.31, bf16[4,240,256]{2,1,0:T(8,128)(2,1)} %bitcast.34, bf16[4,240,256]{2,1,0:T(8,128)(2,1)} %bitcast.35, ...), custom_call_target="tpu_custom_call" | custom-call | tf_op jit(solution)/shard_map/pallas_call | solution.py:239
  156.5 2.0 %reshape.79 = bf16[512,2,256]{2,1,0:T(2,128)(2,1)} reshape(bf16[512,512]{1,0:T(8,128)(2,1)} %shard_map.76) | data formatting | bytes 1048576 | tf_op jit(solution)/shard_map/reshape | solution.py:319
  (103 shorter events, 8.3 us)
Async XLA Ops:
  3.2 31.8 %copy-start.3 = (s32[4096]{0:T(1024)S(1)}, s32[4096]{0:T(1024)}, u32[]{:S(2)}) copy-start(s32[4096]{0:T(1024)} %param.13) | copy-start | bytes 49156
  3.2 66.4 %all-to-all-start = ((bf16[32,72,256]{2,1,0:T(8,128)(2,1)}), bf16[32,72,256]{2,1,0:T(8,128)(2,1)S(1)}, u32[]{:S(2)}, u32[]{:S(2)}) async-start(bf16[32,72,256]{2,1,0:T(8,128)(2,1)} %shard_map.73), calls=%async_computation | async-start | bytes 2359296 | tf_op jit(solution)/shard_map/all_to_all | solution.py:275
  15.4 7.2 %collective-permute-start.3 = (bf16[512,256]{1,0:T(8,128)(2,1)S(1)}, bf16[512,256]{1,0:T(8,128)(2,1)S(1)}, u32[]{:S(2)}, u32[]{:S(2)}) collective-permute-start(bf16[512,256]{1,0:T(8,128)(2,1)S(1)} %bitcast.22), channel_id=1, source_target_pairs={{0,192},{32,224},{64,0},{96,32},{128,64},{160,96},{192,128},{224,1... | collective-permute-start | bytes 786440 | tf_op jit(solution)/shard_map/ppermute | solution.py:38
  17.9 12.2 %collective-permute-start = (bf16[512,256]{1,0:T(8,128)(2,1)S(1)}, bf16[512,256]{1,0:T(8,128)(2,1)S(1)}, u32[]{:S(2)}, u32[]{:S(2)}) collective-permute-start(bf16[512,256]{1,0:T(8,128)(2,1)S(1)} %bitcast.23), channel_id=1, source_target_pairs={{0,64},{32,96},{64,128},{96,160},{128,192},{160,224},{192,0},{224,... | collective-permute-start | bytes 786440 | tf_op jit(solution)/shard_map/ppermute | solution.py:38
  17.9 17.1 %collective-permute-start.4 = (bf16[512,256]{1,0:T(8,128)(2,1)S(1)}, bf16[512,256]{1,0:T(8,128)(2,1)S(1)}, u32[]{:S(2)}, u32[]{:S(2)}) collective-permute-start(bf16[512,256]{1,0:T(8,128)(2,1)S(1)} %bitcast.24), channel_id=1, source_target_pairs={{0,32},{32,0},{64,96},{96,64},{128,160},{160,128},{192,224},{224,1... | collective-permute-start | bytes 786440 | tf_op jit(solution)/shard_map/ppermute | solution.py:46
  19.2 14.3 %collective-permute-start.2 = (bf16[256,256]{1,0:T(8,128)(2,1)S(1)}, bf16[256,256]{1,0:T(8,128)(2,1)S(1)}, u32[]{:S(2)}, u32[]{:S(2)}) collective-permute-start(bf16[256,256]{1,0:T(8,128)(2,1)S(1)} %get-tuple-element.37), channel_id=1, source_target_pairs={{0,128},{32,160},{64,192},{96,224},{128,0},{160,32},{192,64},{224,... | collective-permute-start | bytes 393224 | tf_op jit(solution)/shard_map/ppermute | solution.py:38
  21.3 12.2 %collective-permute-start.1 = (bf16[256,256]{1,0:T(8,128)(2,1)S(1)}, bf16[256,256]{1,0:T(8,128)(2,1)S(1)}, u32[]{:S(2)}, u32[]{:S(2)}) collective-permute-start(bf16[256,256]{1,0:T(8,128)(2,1)S(1)} %get-tuple-element.38), channel_id=1, source_target_pairs={{0,128},{32,160},{64,192},{96,224},{128,0},{160,32},{192,64},{224,... | collective-permute-start | bytes 393224 | tf_op jit(solution)/shard_map/ppermute | solution.py:38
  22.6 12.4 %collective-permute-start.8 = (bf16[512,256]{1,0:T(8,128)(2,1)S(1)}, bf16[512,256]{1,0:T(8,128)(2,1)S(1)}, u32[]{:S(2)}, u32[]{:S(2)}) collective-permute-start(bf16[512,256]{1,0:T(8,128)(2,1)S(1)} %collective-permute-done.3.refs_4_), channel_id=1, source_target_pairs={{0,32},{32,0},{64,96},{96,64},{128,160},{160,128},{192,224},{224,1... | collective-permute-start | bytes 786440 | tf_op jit(solution)/shard_map/ppermute | solution.py:46
  30.1 4.9 %collective-permute-start.5 = (bf16[512,256]{1,0:T(8,128)(2,1)S(1)}, bf16[512,256]{1,0:T(8,128)(2,1)S(1)}, u32[]{:S(2)}, u32[]{:S(2)}) collective-permute-start(bf16[512,256]{1,0:T(8,128)(2,1)S(1)} %collective-permute-done.refs_1_), channel_id=1, source_target_pairs={{0,32},{32,0},{64,96},{96,64},{128,160},{160,128},{192,224},{224,1... | collective-permute-start | bytes 786440 | tf_op jit(solution)/shard_map/ppermute | solution.py:46
  33.5 1.3 collective-permute-start.7
  33.5 1.5 collective-permute-start.6
  36.8 8.5 %collective-permute-start.9 = (bf16[240,256]{1,0:T(8,128)(2,1)S(1)}, bf16[240,256]{1,0:T(8,128)(2,1)S(1)}, u32[]{:S(2)}, u32[]{:S(2)}) collective-permute-start(bf16[240,256]{1,0:T(8,128)(2,1)S(1)} %get-tuple-element.21), channel_id=1, source_target_pairs={{0,1},{1,2},{2,3},{3,0},{4,5},{5,6},{6,7},{7,4},{8,9},{9,10},{10,1... | collective-permute-start | bytes 368648 | tf_op jit(solution)/shard_map/ppermute | solution.py:38
  38.1 14.0 %collective-permute-start.12 = (bf16[240,256]{1,0:T(8,128)(2,1)S(1)}, bf16[240,256]{1,0:T(8,128)(2,1)S(1)}, u32[]{:S(2)}, u32[]{:S(2)}) collective-permute-start(bf16[240,256]{1,0:T(8,128)(2,1)S(1)} %get-tuple-element.21), channel_id=1, source_target_pairs={{0,3},{1,0},{2,1},{3,2},{4,7},{5,4},{6,5},{7,6},{8,11},{9,8},{10,9... | collective-permute-start | bytes 368648 | tf_op jit(solution)/shard_map/ppermute | solution.py:38
  39.7 10.3 %collective-permute-start.15 = (bf16[272,256]{1,0:T(8,128)(2,1)S(1)}, bf16[272,256]{1,0:T(8,128)(2,1)S(1)}, u32[]{:S(2)}, u32[]{:S(2)}) collective-permute-start(bf16[272,256]{1,0:T(8,128)(2,1)S(1)} %get-tuple-element.22), channel_id=1, source_target_pairs={{0,28},{1,29},{2,30},{3,31},{4,0},{5,1},{6,2},{7,3},{8,4},{9,5},{1... | collective-permute-start | bytes 417800 | tf_op jit(solution)/shard_map/ppermute | solution.py:38
  42.2 10.0 %collective-permute-start.13 = (bf16[272,256]{1,0:T(8,128)(2,1)S(1)}, bf16[272,256]{1,0:T(8,128)(2,1)S(1)}, u32[]{:S(2)}, u32[]{:S(2)}) collective-permute-start(bf16[272,256]{1,0:T(8,128)(2,1)S(1)} %get-tuple-element.22), channel_id=1, source_target_pairs={{0,4},{1,5},{2,6},{3,7},{4,8},{5,9},{6,10},{7,11},{8,12},{9,13},{1... | collective-permute-start | bytes 417800 | tf_op jit(solution)/shard_map/ppermute | solution.py:38
  42.2 10.0 %collective-permute-start.11 = (bf16[120,256]{1,0:T(8,128)(2,1)S(1)}, bf16[120,256]{1,0:T(8,128)(2,1)S(1)}, u32[]{:S(2)}, u32[]{:S(2)}) collective-permute-start(bf16[120,256]{1,0:T(8,128)(2,1)S(1)} %get-tuple-element.39), channel_id=1, source_target_pairs={{0,2},{1,3},{2,0},{3,1},{4,6},{5,7},{6,4},{7,5},{8,10},{9,11},{10,... | collective-permute-start | bytes 184328 | tf_op jit(solution)/shard_map/ppermute | solution.py:38
  45.3 4.6 %collective-permute-start.10 = (bf16[120,256]{1,0:T(8,128)(2,1)S(1)}, bf16[120,256]{1,0:T(8,128)(2,1)S(1)}, u32[]{:S(2)}, u32[]{:S(2)}) collective-permute-start(bf16[120,256]{1,0:T(8,128)(2,1)S(1)} %get-tuple-element.40), channel_id=1, source_target_pairs={{0,2},{1,3},{2,0},{3,1},{4,6},{5,7},{6,4},{7,5},{8,10},{9,11},{10,... | collective-permute-start | bytes 184328 | tf_op jit(solution)/shard_map/ppermute | solution.py:38
  49.9 4.5 %collective-permute-start.16 = (bf16[272,256]{1,0:T(8,128)(2,1)S(1)}, bf16[272,256]{1,0:T(8,128)(2,1)S(1)}, u32[]{:S(2)}, u32[]{:S(2)}) collective-permute-start(bf16[272,256]{1,0:T(8,128)(2,1)S(1)} %collective-permute-done.15), channel_id=1, source_target_pairs={{0,28},{1,29},{2,30},{3,31},{4,0},{5,1},{6,2},{7,3},{8,4},{9,5},{1... | collective-permute-start | bytes 417800 | tf_op jit(solution)/shard_map/ppermute | solution.py:38
  52.1 5.1 %collective-permute-start.14 = (bf16[272,256]{1,0:T(8,128)(2,1)S(1)}, bf16[272,256]{1,0:T(8,128)(2,1)S(1)}, u32[]{:S(2)}, u32[]{:S(2)}) collective-permute-start(bf16[272,256]{1,0:T(8,128)(2,1)S(1)} %collective-permute-done.13), channel_id=1, source_target_pairs={{0,4},{1,5},{2,6},{3,7},{4,8},{5,9},{6,10},{7,11},{8,12},{9,13},{1... | collective-permute-start | bytes 417800 | tf_op jit(solution)/shard_map/ppermute | solution.py:38
  57.3 21.1 %collective-permute-start.25 = (bf16[960,256]{1,0:T(8,128)(2,1)S(1)}, bf16[960,256]{1,0:T(8,128)(2,1)}, u32[]{:S(2)}, u32[]{:S(2)}) collective-permute-start(bf16[960,256]{1,0:T(8,128)(2,1)S(1)} %constant_dynamic-update-slice_fusion), channel_id=1, source_target_pairs={{0,28},{1,29},{2,30},{3,31},{4,0},{5,1},{6,2},{7,3},{8,4},{9,5},{1... | collective-permute-start | bytes 1474568 | tf_op jit(solution)/shard_map/ppermute | solution.py:38
  57.6 19.7 %collective-permute-start.17 = (bf16[960,256]{1,0:T(8,128)(2,1)S(1)}, bf16[960,256]{1,0:T(8,128)(2,1)S(1)}, u32[]{:S(2)}, u32[]{:S(2)}) collective-permute-start(bf16[960,256]{1,0:T(8,128)(2,1)S(1)} %constant_dynamic-update-slice_fusion), channel_id=1, source_target_pairs={{0,4},{1,5},{2,6},{3,7},{4,8},{5,9},{6,10},{7,11},{8,12},{9,13},{1... | collective-permute-start | bytes 1474568 | tf_op jit(solution)/shard_map/ppermute | solution.py:38
  58.7 10.8 %collective-permute-start.20 = (bf16[272,256]{1,0:T(8,128)(2,1)S(1)}, bf16[272,256]{1,0:T(8,128)(2,1)S(1)}, u32[]{:S(2)}, u32[]{:S(2)}) collective-permute-start(bf16[272,256]{1,0:T(8,128)(2,1)S(1)} %collective-permute-done.16), channel_id=1, source_target_pairs={{0,28},{1,29},{2,30},{3,31},{4,0},{5,1},{6,2},{7,3},{8,4},{9,5},{1... | collective-permute-start | bytes 417800 | tf_op jit(solution)/shard_map/ppermute | solution.py:38
  60.2 10.9 %collective-permute-start.18 = (bf16[272,256]{1,0:T(8,128)(2,1)S(1)}, bf16[272,256]{1,0:T(8,128)(2,1)S(1)}, u32[]{:S(2)}, u32[]{:S(2)}) collective-permute-start(bf16[272,256]{1,0:T(8,128)(2,1)S(1)} %collective-permute-done.14), channel_id=1, source_target_pairs={{0,4},{1,5},{2,6},{3,7},{4,8},{5,9},{6,10},{7,11},{8,12},{9,13},{1... | collective-permute-start | bytes 417800 | tf_op jit(solution)/shard_map/ppermute | solution.py:38
  69.6 72.4 %copy-start = (bf16[32,72,256]{2,1,0:T(8,128)(2,1)}, bf16[32,72,256]{2,1,0:T(8,128)(2,1)S(1)}, u32[]{:S(2)}) copy-start(bf16[32,72,256]{2,1,0:T(8,128)(2,1)S(1)} %all-to-all-done.got_ref.refs_14_) | copy-start | bytes 3538948
  71.1 4.4 %collective-permute-start.19 = (bf16[136,256]{1,0:T(8,128)(2,1)S(1)}, bf16[136,256]{1,0:T(8,128)(2,1)S(1)}, u32[]{:S(2)}, u32[]{:S(2)}) collective-permute-start(bf16[136,256]{1,0:T(8,128)(2,1)S(1)} %slice.48), channel_id=1, source_target_pairs={{0,4},{1,5},{2,6},{3,7},{4,8},{5,9},{6,10},{7,11},{8,12},{9,13},{1... | collective-permute-start | bytes 208904 | tf_op jit(solution)/shard_map/ppermute | solution.py:38
  71.2 5.0 %collective-permute-start.21 = (bf16[136,256]{1,0:T(8,128)(2,1)S(1)}, bf16[136,256]{1,0:T(8,128)(2,1)S(1)}, u32[]{:S(2)}, u32[]{:S(2)}) collective-permute-start(bf16[136,256]{1,0:T(8,128)(2,1)S(1)} %slice.49), channel_id=1, source_target_pairs={{0,28},{1,29},{2,30},{3,31},{4,0},{5,1},{6,2},{7,3},{8,4},{9,5},{1... | collective-permute-start | bytes 208904 | tf_op jit(solution)/shard_map/ppermute | solution.py:38
  76.8 20.9 %collective-permute-start.31 = (bf16[2176,256]{1,0:T(8,128)(2,1)}, bf16[2176,256]{1,0:T(8,128)(2,1)S(1)}, u32[]{:S(2)}, u32[]{:S(2)}) collective-permute-start(bf16[2176,256]{1,0:T(8,128)(2,1)} %constant_dynamic-update-slice_fusion.5), channel_id=1, source_target_pairs={{0,3},{1,0},{2,1},{3,2},{4,7},{5,4},{6,5},{7,6},{8,11},{9,8},{10,9... | collective-permute-start | bytes 3342344 | tf_op jit(solution)/shard_map/ppermute | solution.py:38
  77.3 8.9 %collective-permute-start.22 = (bf16[960,256]{1,0:T(8,128)(2,1)S(1)}, bf16[960,256]{1,0:T(8,128)(2,1)S(1)}, u32[]{:S(2)}, u32[]{:S(2)}) collective-permute-start(bf16[960,256]{1,0:T(8,128)(2,1)S(1)} %collective-permute-done.17), channel_id=1, source_target_pairs={{0,4},{1,5},{2,6},{3,7},{4,8},{5,9},{6,10},{7,11},{8,12},{9,13},{1... | collective-permute-start | bytes 1474568 | tf_op jit(solution)/shard_map/ppermute | solution.py:38
  77.3 22.2 %collective-permute-start.29 = (bf16[2176,256]{1,0:T(8,128)(2,1)}, bf16[2176,256]{1,0:T(8,128)(2,1)S(1)}, u32[]{:S(2)}, u32[]{:S(2)}) collective-permute-start(bf16[2176,256]{1,0:T(8,128)(2,1)} %constant_dynamic-update-slice_fusion.5), channel_id=1, source_target_pairs={{0,1},{1,2},{2,3},{3,0},{4,5},{5,6},{6,7},{7,4},{8,9},{9,10},{10,1... | collective-permute-start | bytes 3342344 | tf_op jit(solution)/shard_map/ppermute | solution.py:38
  78.3 8.7 %collective-permute-start.26 = (bf16[960,256]{1,0:T(8,128)(2,1)}, bf16[960,256]{1,0:T(8,128)(2,1)S(1)}, u32[]{:S(2)}, u32[]{:S(2)}) collective-permute-start(bf16[960,256]{1,0:T(8,128)(2,1)} %collective-permute-done.25), channel_id=1, source_target_pairs={{0,28},{1,29},{2,30},{3,31},{4,0},{5,1},{6,2},{7,3},{8,4},{9,5},{1... | collective-permute-start | bytes 1474568 | tf_op jit(solution)/shard_map/ppermute | solution.py:38
  80.9 24.9 %collective-permute-start.35 = (bf16[32,72,256]{2,1,0:T(8,128)(2,1)S(1)}, bf16[32,72,256]{2,1,0:T(8,128)(2,1)S(1)}, u32[]{:S(2)}, u32[]{:S(2)}) collective-permute-start(bf16[32,72,256]{2,1,0:T(8,128)(2,1)S(1)} %all-to-all-done.got_ref.refs_14_), channel_id=1, source_target_pairs={{0,192},{32,224},{64,0},{96,32},{128,64},{160,96},{192,128},{224,1... | collective-permute-start | bytes 3538952 | tf_op jit(solution)/shard_map/ppermute | solution.py:38
  86.2 22.6 %collective-permute-start.33 = (bf16[32,72,256]{2,1,0:T(8,128)(2,1)S(1)}, bf16[32,72,256]{2,1,0:T(8,128)(2,1)S(1)}, u32[]{:S(2)}, u32[]{:S(2)}) collective-permute-start(bf16[32,72,256]{2,1,0:T(8,128)(2,1)S(1)} %all-to-all-done.got_ref.refs_14_), channel_id=1, source_target_pairs={{0,64},{32,96},{64,128},{96,160},{128,192},{160,224},{192,0},{224,... | collective-permute-start | bytes 3538952 | tf_op jit(solution)/shard_map/ppermute | solution.py:38
  87.0 53.9 %copy-start.15 = (bf16[960,256]{1,0:T(8,128)(2,1)}, bf16[960,256]{1,0:T(8,128)(2,1)S(1)}, u32[]{:S(2)}) copy-start(bf16[960,256]{1,0:T(8,128)(2,1)S(1)} %collective-permute-done.26) | copy-start | bytes 1474564
  87.0 13.6 %collective-permute-start.23 = (bf16[960,256]{1,0:T(8,128)(2,1)S(1)}, bf16[960,256]{1,0:T(8,128)(2,1)S(1)}, u32[]{:S(2)}, u32[]{:S(2)}) collective-permute-start(bf16[960,256]{1,0:T(8,128)(2,1)S(1)} %collective-permute-done.22), channel_id=1, source_target_pairs={{0,4},{1,5},{2,6},{3,7},{4,8},{5,9},{6,10},{7,11},{8,12},{9,13},{1... | collective-permute-start | bytes 1474568 | tf_op jit(solution)/shard_map/ppermute | solution.py:38
  97.6 8.0 %collective-permute-start.27 = (bf16[960,256]{1,0:T(8,128)(2,1)S(1)}, bf16[960,256]{1,0:T(8,128)(2,1)S(1)}, u32[]{:S(2)}, u32[]{:S(2)}) collective-permute-start(bf16[960,256]{1,0:T(8,128)(2,1)S(1)} %collective-permute-done.26), channel_id=1, source_target_pairs={{0,28},{1,29},{2,30},{3,31},{4,0},{5,1},{6,2},{7,3},{8,4},{9,5},{1... | collective-permute-start | bytes 1474568 | tf_op jit(solution)/shard_map/ppermute | solution.py:38
  99.5 25.5 %collective-permute-start.32 = (bf16[1088,256]{1,0:T(8,128)(2,1)S(1)}, bf16[1088,256]{1,0:T(8,128)(2,1)S(1)}, u32[]{:S(2)}, u32[]{:S(2)}) collective-permute-start(bf16[1088,256]{1,0:T(8,128)(2,1)S(1)} %slice.59), channel_id=1, source_target_pairs={{0,3},{1,0},{2,1},{3,2},{4,7},{5,4},{6,5},{7,6},{8,11},{9,8},{10,9... | collective-permute-start | bytes 1671176 | tf_op jit(solution)/shard_map/ppermute | solution.py:38
  100.7 24.8 %collective-permute-start.30 = (bf16[1088,256]{1,0:T(8,128)(2,1)S(1)}, bf16[1088,256]{1,0:T(8,128)(2,1)S(1)}, u32[]{:S(2)}, u32[]{:S(2)}) collective-permute-start(bf16[1088,256]{1,0:T(8,128)(2,1)S(1)} %slice.58), channel_id=1, source_target_pairs={{0,1},{1,2},{2,3},{3,0},{4,5},{5,6},{6,7},{7,4},{8,9},{9,10},{10,1... | collective-permute-start | bytes 1671176 | tf_op jit(solution)/shard_map/ppermute | solution.py:38
  105.6 6.9 %collective-permute-start.24 = (bf16[480,256]{1,0:T(8,128)(2,1)S(1)}, bf16[480,256]{1,0:T(8,128)(2,1)S(1)}, u32[]{:S(2)}, u32[]{:S(2)}) collective-permute-start(bf16[480,256]{1,0:T(8,128)(2,1)S(1)} %slice.56), channel_id=1, source_target_pairs={{0,4},{1,5},{2,6},{3,7},{4,8},{5,9},{6,10},{7,11},{8,12},{9,13},{1... | collective-permute-start | bytes 737288 | tf_op jit(solution)/shard_map/ppermute | solution.py:38
  105.9 18.9 %collective-permute-start.28 = (bf16[480,256]{1,0:T(8,128)(2,1)S(1)}, bf16[480,256]{1,0:T(8,128)(2,1)S(1)}, u32[]{:S(2)}, u32[]{:S(2)}) collective-permute-start(bf16[480,256]{1,0:T(8,128)(2,1)S(1)} %slice.57), channel_id=1, source_target_pairs={{0,28},{1,29},{2,30},{3,31},{4,0},{5,1},{6,2},{7,3},{8,4},{9,5},{1... | collective-permute-start | bytes 737288 | tf_op jit(solution)/shard_map/ppermute | solution.py:38
  108.8 33.3 %copy-start.5 = (bf16[32,72,256]{2,1,0:T(8,128)(2,1)}, bf16[32,72,256]{2,1,0:T(8,128)(2,1)S(1)}, u32[]{:S(2)}) copy-start(bf16[32,72,256]{2,1,0:T(8,128)(2,1)S(1)} %collective-permute-done.33.refs_15_) | copy-start | bytes 3538948
  108.8 16.8 %collective-permute-start.36 = (bf16[16,72,256]{2,1,0:T(8,128)(2,1)S(1)}, bf16[16,72,256]{2,1,0:T(8,128)(2,1)}, u32[]{:S(2)}, u32[]{:S(2)}) collective-permute-start(bf16[16,72,256]{2,1,0:T(8,128)(2,1)S(1)} %slice.55), channel_id=1, source_target_pairs={{0,192},{32,224},{64,0},{96,32},{128,64},{160,96},{192,128},{224,1... | collective-permute-start | bytes 1769480 | tf_op jit(solution)/shard_map/ppermute | solution.py:38
  112.5 28.5 %copy-start.16 = (bf16[480,256]{1,0:T(8,128)(2,1)}, bf16[480,256]{1,0:T(8,128)(2,1)S(1)}, u32[]{:S(2)}) copy-start(bf16[480,256]{1,0:T(8,128)(2,1)S(1)} %collective-permute-done.24) | copy-start | bytes 737284
  112.5 30.2 %collective-permute-start.37 = (bf16[32,72,256]{2,1,0:T(8,128)(2,1)S(1)}, bf16[32,72,256]{2,1,0:T(8,128)(2,1)}, u32[]{:S(2)}, u32[]{:S(2)}) collective-permute-start(bf16[32,72,256]{2,1,0:T(8,128)(2,1)S(1)} %all-to-all-done.got_ref.refs_14_), channel_id=1, source_target_pairs={{0,32},{32,0},{64,96},{96,64},{128,160},{160,128},{192,224},{224,1... | collective-permute-start | bytes 3538952 | tf_op jit(solution)/shard_map/ppermute | solution.py:46
  124.8 16.2 %collective-permute-start.34 = (bf16[16,72,256]{2,1,0:T(8,128)(2,1)S(1)}, bf16[16,72,256]{2,1,0:T(8,128)(2,1)}, u32[]{:S(2)}, u32[]{:S(2)}) collective-permute-start(bf16[16,72,256]{2,1,0:T(8,128)(2,1)S(1)} %slice.54), channel_id=1, source_target_pairs={{0,64},{32,96},{64,128},{96,160},{128,192},{160,224},{192,0},{224,... | collective-permute-start | bytes 1769480 | tf_op jit(solution)/shard_map/ppermute | solution.py:38
  125.0 18.9 %collective-permute-start.41 = (bf16[32,72,256]{2,1,0:T(8,128)(2,1)S(1)}, bf16[32,72,256]{2,1,0:T(8,128)(2,1)}, u32[]{:S(2)}, u32[]{:S(2)}) collective-permute-start(bf16[32,72,256]{2,1,0:T(8,128)(2,1)S(1)} %collective-permute-done.35.refs_18_), channel_id=1, source_target_pairs={{0,32},{32,0},{64,96},{96,64},{128,160},{160,128},{192,224},{224,1... | collective-permute-start | bytes 3538952 | tf_op jit(solution)/shard_map/ppermute | solution.py:46
  125.4 18.5 %collective-permute-start.38 = (bf16[32,72,256]{2,1,0:T(8,128)(2,1)S(1)}, bf16[32,72,256]{2,1,0:T(8,128)(2,1)}, u32[]{:S(2)}, u32[]{:S(2)}) collective-permute-start(bf16[32,72,256]{2,1,0:T(8,128)(2,1)S(1)} %collective-permute-done.33.refs_15_), channel_id=1, source_target_pairs={{0,32},{32,0},{64,96},{96,64},{128,160},{160,128},{192,224},{224,1... | collective-permute-start | bytes 3538952 | tf_op jit(solution)/shard_map/ppermute | solution.py:46
  125.6 17.1 %collective-permute-start.40 = (bf16[16,72,256]{2,1,0:T(8,128)(2,1)}, bf16[16,72,256]{2,1,0:T(8,128)(2,1)}, u32[]{:S(2)}, u32[]{:S(2)}) collective-permute-start(bf16[16,72,256]{2,1,0:T(8,128)(2,1)} %collective-permute-done.36.refs_17_), channel_id=1, source_target_pairs={{0,32},{32,0},{64,96},{96,64},{128,160},{160,128},{192,224},{224,1... | collective-permute-start | bytes 1769480 | tf_op jit(solution)/shard_map/ppermute | solution.py:46
  141.0 2.9 %collective-permute-start.39 = (bf16[16,72,256]{2,1,0:T(8,128)(2,1)}, bf16[16,72,256]{2,1,0:T(8,128)(2,1)}, u32[]{:S(2)}, u32[]{:S(2)}) collective-permute-start(bf16[16,72,256]{2,1,0:T(8,128)(2,1)} %collective-permute-done.34.refs_16_), channel_id=1, source_target_pairs={{0,32},{32,0},{64,96},{96,64},{128,160},{160,128},{192,224},{224,1... | collective-permute-start | bytes 1769480 | tf_op jit(solution)/shard_map/ppermute | solution.py:46
  (13 other events, 148.9 us)
